TPU v7x, 512 devices: a whole 4x4x16 slice. The times are simulated.
512 devices in a mesh: batch: 32 (over z, core), tensor: 16 (over y, x).
Axes of the slice: x: 4, y: 4, z: 16, core: 2. Of those that a mesh axis runs over, the one named last changes fastest.
Arguments:
- tokens: bfloat16 [640, 8192], P('tensor', 'batch'), may hold values from -32 to 32
- norm_gain: float32 [8192], P('batch'), may hold values from 0.1 to 1.9
- in_x_weight: bfloat16 [8192, 8192], P('batch', 'tensor'), may hold values from -0.0625 to 0.0625
- in_z_weight: bfloat16 [8192, 8192], P('batch', 'tensor'), may hold values from -0.0625 to 0.0625
- conv_state: bfloat16 [3, 640, 8192], P(None, 'batch', 'tensor'), may hold values from -6 to 6
- conv_weight: float32 [4, 8192], P(None, 'tensor'), may hold values from -3 to 3
- conv_bias: float32 [8192], P('tensor'), may hold values from -1 to 1
- proj_weight: bfloat16 [8192, 544], P('tensor'), may hold values from -0.0625 to 0.0625
- delta_weight: bfloat16 [512, 8192], P(None, 'tensor'), may hold values from -0.25 to 0.25
- delta_bias: float32 [8192], P('tensor'), may hold values from -4 to 0
- decay_log: float32 [16, 8192], P(None, 'tensor'), may hold values from 0 to 2.77
- ssm_state: float32 [640, 16, 8192], P('batch', None, 'tensor'), may hold values from -6 to 6
- skip_gain: float32 [8192], P('tensor'), may hold values from 0.5 to 1.5
- out_weight: bfloat16 [8192, 8192], P('tensor', 'batch'), may hold values from -0.0625 to 0.0625
- post_gain: float32 [8192], P('batch'), may hold values from 0.1 to 1.9
- gate_weight: bfloat16 [8192, 12288], P('batch', 'tensor'), may hold values from -0.0625 to 0.0625
- up_weight: bfloat16 [8192, 12288], P('batch', 'tensor'), may hold values from -0.0625 to 0.0625
- down_weight: bfloat16 [12288, 8192], P('tensor', 'batch'), may hold values from -0.0546875 to 0.0546875
Outputs:
- mixed: bfloat16 [640, 8192], P('tensor', 'batch')
- new_conv_state: bfloat16 [3, 640, 8192], P(None, 'batch', 'tensor')
- new_state: float32 [640, 16, 8192], P('batch', None, 'tensor')
All inputs are finite; a program needn't handle non-finite values.
Results may differ from a plain program's by a relative error of at most 0.03.
Values may be sent and summed in bfloat16 or wider, within the bound.
No kernel may reach another device: no remote copies, remote signals or barrier semaphores. Data moves between devices by JAX's collectives and lax.ppermute only.
A program may use at most 64 MiB of HBM per device.

v0:
```python
import jax
import jax.numpy as jnp
from jax import lax
from jax.sharding import PartitionSpec as P

WIDTH = 8192
RANK = 512
STATE = 16


epsilon = 1e-06


def on_device(
    tokens,
    norm_gain,
    in_x_weight,
    in_z_weight,
    conv_state,
    conv_weight,
    conv_bias,
    proj_weight,
    delta_weight,
    delta_bias,
    decay_log,
    ssm_state,
    skip_gain,
    out_weight,
    post_gain,
    gate_weight,
    up_weight,
    down_weight,
):
    inner_dev = in_x_weight.shape[1]
    gate_cols = gate_weight.shape[1]
    wide = tokens.astype(jnp.float32)
    first = lax.psum(jnp.sum(wide * wide, axis=1), "batch") / WIDTH
    normed = (wide * lax.rsqrt(first + epsilon)[:, None] * norm_gain[None, :]).astype(jnp.bfloat16)
    gathered = lax.all_gather(normed, "tensor", axis=0, tiled=True)
    block = gathered
    left_part = jnp.dot(block, in_x_weight, preferred_element_type=jnp.float32)
    right_part = jnp.dot(block, in_z_weight, preferred_element_type=jnp.float32)
    mixed_in = lax.psum_scatter(
        jnp.concatenate([left_part, right_part], axis=1).astype(jnp.bfloat16),
        "batch",
        scatter_dimension=0,
        tiled=True,
    ).astype(jnp.float32)
    inner_x = mixed_in[:, :inner_dev].astype(jnp.bfloat16)
    gate_z = mixed_in[:, inner_dev:].astype(jnp.bfloat16)
    window = jnp.concatenate([conv_state, inner_x[None]], axis=0)
    conv_pre = (
        jnp.sum(window.astype(jnp.float32) * conv_weight[:, None, :], axis=0) + conv_bias[None, :]
    )
    signal = jax.nn.silu(conv_pre).astype(jnp.bfloat16)
    projected = lax.psum(
        jnp.dot(signal, proj_weight, preferred_element_type=jnp.float32).astype(jnp.bfloat16),
        "tensor",
    ).astype(jnp.float32)
    delta_low = projected[:, :RANK]
    input_map = projected[:, RANK : RANK + STATE]
    output_map = projected[:, RANK + STATE :]
    delta_scale = lax.rsqrt(jnp.mean(delta_low * delta_low, axis=1, keepdims=True) + epsilon)
    delta_norm = (delta_low * delta_scale).astype(jnp.bfloat16)
    delta = jax.nn.softplus(
        jnp.dot(delta_norm, delta_weight, preferred_element_type=jnp.float32) + delta_bias[None, :]
    )
    signal_wide = signal.astype(jnp.float32)
    decay = jnp.exp(delta[:, None, :] * (-jnp.exp(decay_log))[None, :, :])
    new_state = decay * ssm_state + (delta * signal_wide)[:, None, :] * input_map[:, :, None]
    readout = jnp.sum(new_state * output_map[:, :, None], axis=1) + skip_gain[None, :] * signal_wide
    gated = (readout * jax.nn.silu(gate_z.astype(jnp.float32))).astype(jnp.bfloat16)
    out_terms = jnp.dot(
        lax.all_gather(gated, "batch", axis=0, tiled=True),
        out_weight,
        preferred_element_type=jnp.float32,
    )
    out_own = lax.psum_scatter(
        out_terms.astype(jnp.bfloat16), "tensor", scatter_dimension=0, tiled=True
    ).astype(jnp.float32)
    residual = (wide + out_own).astype(jnp.bfloat16)
    residual_wide = residual.astype(jnp.float32)
    second = lax.psum(jnp.sum(residual_wide * residual_wide, axis=1), "batch") / WIDTH
    post = (residual_wide * lax.rsqrt(second + epsilon)[:, None] * post_gain[None, :]).astype(
        jnp.bfloat16
    )
    hidden_in = lax.all_gather(post, "tensor", axis=0, tiled=True)
    block = hidden_in
    gate_part = jnp.dot(block, gate_weight, preferred_element_type=jnp.float32)
    up_part = jnp.dot(block, up_weight, preferred_element_type=jnp.float32)
    both = lax.psum_scatter(
        jnp.concatenate([gate_part, up_part], axis=1).astype(jnp.bfloat16),
        "batch",
        scatter_dimension=0,
        tiled=True,
    ).astype(jnp.float32)
    active = (jax.nn.silu(both[:, :gate_cols]) * both[:, gate_cols:]).astype(jnp.bfloat16)
    down_terms = jnp.dot(
        lax.all_gather(active, "batch", axis=0, tiled=True),
        down_weight,
        preferred_element_type=jnp.float32,
    )
    down_own = lax.psum_scatter(
        down_terms.astype(jnp.bfloat16), "tensor", scatter_dimension=0, tiled=True
    ).astype(jnp.float32)
    mixed = (residual.astype(jnp.float32) + down_own).astype(jnp.bfloat16)
    return (mixed, window[1:], new_state)


def solution(mesh):
    return jax.shard_map(
        on_device,
        mesh=mesh,
        in_specs=(
            P("tensor", "batch"),
            P("batch"),
            P("batch", "tensor"),
            P("batch", "tensor"),
            P(None, "batch", "tensor"),
            P(None, "tensor"),
            P("tensor"),
            P("tensor", None),
            P(None, "tensor"),
            P("tensor"),
            P(None, "tensor"),
            P("batch", None, "tensor"),
            P("tensor"),
            P("tensor", "batch"),
            P("batch"),
            P("batch", "tensor"),
            P("batch", "tensor"),
            P("tensor", "batch"),
        ),
        out_specs=(P("tensor", "batch"), P(None, "batch", "tensor"), P("batch", None, "tensor")),
        check_vma=False,
    )
```

profile of v0, /device:TPU:1, one launch (start us, length us, event | category | flops | bytes accessed | tf_op | source)
XLA Modules:
  0.0 765.5 jit_solution(8166824424402177066)
XLA Ops:
  8.1 53.3 %psum.21 = f32[40]{0:T(128)S(1)} all-reduce(f32[40]{0:T(128)S(1)} %fusion.9), channel_id=1, replica_groups=mesh['batch'=32,'tensor'=16] {'batch'}, use_global_device_ids=true, to_apply=%region_1.0 | all-reduce | flops 40 | bytes 320 | tf_op jit(solution)/shard_map/psum | solution.py:37
  62.2 18.9 %all_gather.12 = bf16[640,256]{1,0:T(8,128)(2,1)S(1)} all-gather(bf16[40,256]{1,0:T(8,128)(2,1)S(1)} %fusion.11), channel_id=1, replica_groups=mesh['batch'=32,'tensor'=16] {'tensor'}, dimensions={0}, use_global_device_ids=true | all-gather | bytes 348160 | tf_op jit(solution)/shard_map/all_gather | solution.py:39
  81.2 1.4 convolution_convert_fusion.2
  82.6 1.4 convolution_convert_fusion.3
  84.0 1.2 pad_maximum_fusion.1
  86.6 211.3 %all-reduce.7.cloned.1.call-done = bf16[640,1024]{0,1:T(8,128)(2,1)} async-done(((bf16[640,1024]{0,1:T(8,128)(2,1)}), bf16[640,1024]{0,1:T(8,128)(2,1)}) %all-reduce.7.cloned.1.call-update) | async-done | bytes 1310736
  297.9 1.2 dynamic-slice_bitcast_fusion
  299.5 60.5 %psum.22 = bf16[20,544]{1,0:T(8,128)(2,1)S(1)} all-reduce(bf16[20,544]{1,0:T(8,128)(2,1)S(1)} %convolution_convert_fusion.6), channel_id=1, replica_groups=mesh['batch'=32,'tensor'=16] {'tensor'}, use_global_device_ids=true, to_apply=%region_4.5 | all-reduce | flops 10880 | bytes 43520 | tf_op jit(solution)/shard_map/psum | solution.py:56
  360.7 1.1 multiply_reduce_fusion
  361.9 44.1 %all-gather = bf16[32,20,512]{2,1,0:T(8,128)(2,1)S(1)} all-gather(bf16[1,20,512]{2,1,0:T(8,128)(2,1)S(1)} %fusion.19), channel_id=1, replica_groups=mesh['batch'=32,'tensor'=16] {'batch'}, dimensions={0}, use_global_device_ids=true | all-gather | bytes 675840 | tf_op jit(solution)/shard_map/all_gather | solution.py:74
  407.2 78.6 %reduce-scatter.10.cloned.1.call-done = bf16[40,256]{1,0:T(8,128)(2,1)} async-done(((bf16[640,256]{1,0:T(8,128)(2,1)}), bf16[40,256]{1,0:T(8,128)(2,1)}) %reduce-scatter.10.cloned.1.call-update) | async-done | bytes 20496
  486.7 49.0 %psum.23 = f32[40]{0:T(128)S(1)} all-reduce(f32[40]{0:T(128)S(1)} %fusion.13), channel_id=1, replica_groups=mesh['batch'=32,'tensor'=16] {'batch'}, use_global_device_ids=true, to_apply=%region_9.10 | all-reduce | flops 40 | bytes 320 | tf_op jit(solution)/shard_map/psum | solution.py:83
  536.5 18.0 %all_gather.14 = bf16[640,256]{1,0:T(8,128)(2,1)S(1)} all-gather(bf16[40,256]{1,0:T(8,128)(2,1)S(1)} %fusion.15), channel_id=1, replica_groups=mesh['batch'=32,'tensor'=16] {'tensor'}, dimensions={0}, use_global_device_ids=true | all-gather | bytes 348160 | tf_op jit(solution)/shard_map/all_gather | solution.py:87
  555.5 61.8 %fusion = bf16[24,1536]{1,0:T(8,128)(2,1)S(1)} fusion(bf16[640,1536]{1,0:T(8,128)(2,1)S(1)} %pad_maximum_fusion), kind=kCustom, calls=%all-reduce-scatter | all-reduce-scatter fusion | flops 1179649 | bytes 2041856
  617.3 3.8 collective-permute-start.5
  621.2 5.8 collective-permute-start
  627.0 1.3 collective-permute-start.1
  628.3 1.6 collective-permute-start.2
  629.9 8.8 %collective-permute-start.3 = (bf16[24,1536]{1,0:T(8,128)(2,1)S(1)}, bf16[24,1536]{1,0:T(8,128)(2,1)S(1)}, u32[]{:S(2)}, u32[]{:S(2)}) collective-permute-start(bf16[24,1536]{1,0:T(8,128)(2,1)S(1)} %fusion), channel_id=1, source_target_pairs={{0,64},{16,80},{32,96},{48,112},{64,128},{80,144},{96,160},{112,17... | collective-permute-start | bytes 221192
  638.7 2.2 collective-permute-start.4
  643.9 33.8 %all-gather.1 = bf16[32,20,768]{2,1,0:T(8,128)(2,1)S(1)} all-gather(bf16[1,20,768]{2,1,0:T(8,128)(2,1)S(1)} %fusion.17), channel_id=1, replica_groups=mesh['batch'=32,'tensor'=16] {'batch'}, dimensions={0}, use_global_device_ids=true | all-gather | bytes 1013760 | tf_op jit(solution)/shard_map/all_gather | solution.py:99
  678.0 1.1 convolution_convert_fusion.4
  679.8 77.8 %reduce-scatter.12.cloned.1.call-done = bf16[40,256]{1,0:T(8,128)(2,1)} async-done(((bf16[640,256]{1,0:T(8,128)(2,1)}), bf16[40,256]{1,0:T(8,128)(2,1)}) %reduce-scatter.12.cloned.1.call-update) | async-done | bytes 20496
  757.6 1.3 fusion.16
  (75 shorter events, 10.6 us)
Async XLA Ops:
  7.2 292.0 %copy-start = (bf16[512,544]{0,1:T(8,128)(2,1)S(1)}, bf16[512,544]{0,1:T(8,128)(2,1)}, u32[]{:S(2)}) copy-start(bf16[512,544]{0,1:T(8,128)(2,1)} %param.25) | copy-start | bytes 1671172
  7.2 290.7 %all-reduce.7.cloned.1.call-start = ((), (), s32[]{:S(2)}) async-start(), calls=%async_computation.2 | async-start | bytes 2621440
  84.0 215.2 %copy-start.6 = (bf16[3,20,512]{2,1,0:T(8,128)(2,1)S(1)}, bf16[3,20,512]{2,1,0:T(8,128)(2,1)}, u32[]{:S(2)}) copy-start(bf16[3,20,512]{2,1,0:T(8,128)(2,1)} %param.22) | copy-start | bytes 184324
  84.0 215.2 %copy-start.11 = (f32[4,512]{1,0:T(4,128)S(1)}, f32[4,512]{1,0:T(4,128)}, u32[]{:S(2)}) copy-start(f32[4,512]{1,0:T(4,128)} %param.23) | copy-start | bytes 24580
  84.0 215.2 %copy-start.10 = (f32[512]{0:T(512)S(1)}, f32[512]{0:T(512)}, u32[]{:S(2)}) copy-start(f32[512]{0:T(512)} %param.24) | copy-start | bytes 6148
  85.2 275.2 %copy-start.2 = (bf16[512,512]{1,0:T(8,128)(2,1)S(1)}, bf16[512,512]{1,0:T(8,128)(2,1)}, u32[]{:S(2)}) copy-start(bf16[512,512]{1,0:T(8,128)(2,1)} %param.26) | copy-start | bytes 1572868
  85.2 275.2 %copy-start.12 = (f32[512]{0:T(512)S(1)}, f32[512]{0:T(512)}, u32[]{:S(2)}) copy-start(f32[512]{0:T(512)} %param.27) | copy-start | bytes 6148
  85.2 275.5 %copy-start.1 = (f32[20,16,512]{2,1,0:T(8,128)S(1)}, f32[20,16,512]{2,1,0:T(8,128)}, u32[]{:S(2)}) copy-start(f32[20,16,512]{2,1,0:T(8,128)} %param.29) | copy-start | bytes 1966084
  85.2 400.6 %reduce-scatter.10.cloned.1.call-start = ((), (), s32[]{:S(2)}) async-start(), calls=%async_computation.3 | async-start | bytes 348160
  86.6 275.3 %copy-start.13 = (f32[512]{0:T(512)S(1)}, f32[512]{0:T(512)}, u32[]{:S(2)}) copy-start(f32[512]{0:T(512)} %param.30) | copy-start | bytes 6148
  360.7 45.4 %copy-start.7 = (bf16[512,256]{1,0:T(8,128)(2,1)S(1)}, bf16[512,256]{1,0:T(8,128)(2,1)}, u32[]{:S(2)}) copy-start(bf16[512,256]{1,0:T(8,128)(2,1)} %param.31) | copy-start | bytes 786436
  361.8 124.0 %copy-start.3 = (bf16[40,256]{1,0:T(8,128)(2,1)S(1)}, bf16[40,256]{1,0:T(8,128)(2,1)}, u32[]{:S(2)}) copy-start(bf16[40,256]{1,0:T(8,128)(2,1)} %param.18) | copy-start | bytes 61444
  361.9 173.8 %copy-start.14 = (f32[256]{0:T(256)S(1)}, f32[256]{0:T(256)}, u32[]{:S(2)}) copy-start(f32[256]{0:T(256)} %param.32) | copy-start | bytes 3076
  361.9 192.6 %copy-start.4 = (bf16[256,768]{1,0:T(8,128)(2,1)S(1)}, bf16[256,768]{1,0:T(8,128)(2,1)}, u32[]{:S(2)}) copy-start(bf16[256,768]{1,0:T(8,128)(2,1)} %param.34) | copy-start | bytes 1179652
  406.1 148.8 %copy-start.5 = (bf16[256,768]{1,0:T(8,128)(2,1)S(1)}, bf16[256,768]{1,0:T(8,128)(2,1)}, u32[]{:S(2)}) copy-start(bf16[256,768]{1,0:T(8,128)(2,1)} %param.33) | copy-start | bytes 1179652
  407.2 350.4 %reduce-scatter.12.cloned.1.call-start = ((), (), s32[]{:S(2)}) async-start(), calls=%async_computation.4 | async-start | bytes 348160
  617.3 21.4 %collective-permute-start.5 = (bf16[4,1536]{1,0:T(4,128)(2,1)S(1)}, bf16[4,1536]{1,0:T(4,128)(2,1)S(1)}, u32[]{:S(2)}, u32[]{:S(2)}) collective-permute-start(bf16[4,1536]{1,0:T(4,128)(2,1)S(1)} %slice.41), channel_id=1, source_target_pairs={{0,96},{16,112},{32,128},{48,144},{64,160},{80,176},{96,192},{112,... | collective-permute-start | bytes 36872
  621.2 20.4 %collective-permute-start = (bf16[24,1536]{1,0:T(8,128)(2,1)S(1)}, bf16[24,1536]{1,0:T(8,128)(2,1)S(1)}, u32[]{:S(2)}, u32[]{:S(2)}) collective-permute-start(bf16[24,1536]{1,0:T(8,128)(2,1)S(1)} %fusion), channel_id=1, source_target_pairs={{0,16},{16,32},{32,48},{48,64},{64,80},{80,96},{96,112},{112,128},... | collective-permute-start | bytes 221192
  627.0 14.6 %collective-permute-start.1 = (bf16[24,1536]{1,0:T(8,128)(2,1)S(1)}, bf16[24,1536]{1,0:T(8,128)(2,1)S(1)}, u32[]{:S(2)}, u32[]{:S(2)}) collective-permute-start(bf16[24,1536]{1,0:T(8,128)(2,1)S(1)} %fusion), channel_id=1, source_target_pairs={{0,32},{16,48},{32,64},{48,80},{64,96},{80,112},{96,128},{112,144}... | collective-permute-start | bytes 221192
  628.3 13.3 %collective-permute-start.2 = (bf16[24,1536]{1,0:T(8,128)(2,1)S(1)}, bf16[24,1536]{1,0:T(8,128)(2,1)S(1)}, u32[]{:S(2)}, u32[]{:S(2)}) collective-permute-start(bf16[24,1536]{1,0:T(8,128)(2,1)S(1)} %fusion), channel_id=1, source_target_pairs={{0,48},{16,64},{32,80},{48,96},{64,112},{80,128},{96,144},{112,160... | collective-permute-start | bytes 221192
  629.9 11.7 %collective-permute-start.3 = (bf16[24,1536]{1,0:T(8,128)(2,1)S(1)}, bf16[24,1536]{1,0:T(8,128)(2,1)S(1)}, u32[]{:S(2)}, u32[]{:S(2)}) collective-permute-start(bf16[24,1536]{1,0:T(8,128)(2,1)S(1)} %fusion), channel_id=1, source_target_pairs={{0,64},{16,80},{32,96},{48,112},{64,128},{80,144},{96,160},{112,17... | collective-permute-start | bytes 221192
  638.7 4.0 collective-permute-start.4
  643.8 34.2 %copy-start.16 = (bf16[768,256]{1,0:T(8,128)(2,1)S(1)}, bf16[768,256]{1,0:T(8,128)(2,1)}, u32[]{:S(2)}) copy-start(bf16[768,256]{1,0:T(8,128)(2,1)} %param.35) | copy-start | bytes 1179652
  677.8 79.9 %copy-start.8 = (bf16[40,256]{1,0:T(8,128)(2,1)S(1)}, bf16[40,256]{1,0:T(8,128)(2,1)}, u32[]{:S(2)}) copy-start(bf16[40,256]{1,0:T(8,128)(2,1)} %reduce-scatter.10.cloned.1.call-done) | copy-start | bytes 61444
  (2 other events, 4.0 us)
Sparse Core Ops, SparseCore 0:
  85.3 212.4 all-reduce.6
  407.3 78.4 reduce-scatter.9
  679.3 78.2 reduce-scatter.11
where the time goes:
time: 767 us; the launch traced here: 765 us
  waiting for transfers between devices  369 us (48%)
  blocking collectives  339 us (44%)
  starting transfers between devices  23.6 us (3%)
  between operations  15.4 us (2%)
  other arithmetic  8.12 us (1%)
    unnamed x12, waiting for transfers between devices  369 us
    unnamed x1, blocking collectives  61.8 us
    psum x1, blocking collectives, on_device(): lax.psum(jnp.dot(signal, proj_weight, preferred_element_type=jnp.float32)...  60.5 us
    psum x1, blocking collectives, on_device(): first = lax.psum(jnp.sum(wide * wide, axis=1), 'batch') / WIDTH  53.3 us
    psum x1, blocking collectives, on_device(): lax.psum(jnp.sum(residual_wide * residual_wide, axis=1), 'batch') / WIDTH  49 us
    all_gather x1, blocking collectives, on_device(): lax.all_gather(gated, 'batch', axis=0, tiled=True)  44.1 us
    all_gather x1, blocking collectives, on_device(): lax.all_gather(active, 'batch', axis=0, tiled=True)  33.8 us
    unnamed x9, starting transfers between devices  23.6 us
  transfers between devices with their start and end apart: 9, of which 4 were waited for; matrix products, arithmetic and copies ran while one was open for 0% of the time, Pallas kernels for 0%

commit v1 on v0

v1 whole, which is shorter than its diff:
```python
import jax
import jax.numpy as jnp
import numpy as np
from jax import lax
from jax.sharding import Mesh, PartitionSpec as P

WIDTH = 8192
RANK = 512
STATE = 16

epsilon = 1e-06

F32 = jnp.float32
BF16 = jnp.bfloat16
ROW_MAJOR = ("y", "x")
ROW_SWAPPED = ("x", "y")
RING = ("zh", "zl")


def spread(block, axes, count):
    return lax.all_to_all(jnp.broadcast_to(block[None], (count,) + block.shape), axes, 0, 0)


def swap_cores(block):
    return lax.ppermute(block, "c", [(0, 1), (1, 0)])


def dot(left, right):
    return jnp.dot(left, right, preferred_element_type=F32)


def half_columns(weight, which):
    half = weight.shape[1] // 2
    return lax.dynamic_slice_in_dim(weight, which * half, half, 1)


def reduce_rows(rows, gain, left_weight, right_weight, core):
    blocks, size, depth = rows.shape
    wide = rows.astype(F32)
    scaled = (wide * gain[None, None, :]).astype(BF16).reshape(blocks * size, depth)
    squares = jnp.sum(wide * wide, axis=2).reshape(4, 4, size)

    def partial(which):
        weight = jnp.concatenate(
            [half_columns(left_weight, which), half_columns(right_weight, which)], axis=1
        )
        return dot(scaled, weight).astype(BF16).reshape(4, 4 * size, -1)

    other = partial(1 - core)
    columns = other.shape[2]
    tail = jnp.pad(squares.astype(BF16), ((0, 0), (0, 4), (0, columns - size)))
    received = swap_cores(jnp.concatenate([other, tail], axis=1))
    own = jnp.concatenate([partial(core), tail], axis=1)
    total = (own.astype(F32) + received.astype(F32)).astype(BF16)
    near = jnp.sum(lax.all_to_all(total, "zl", 0, 0).astype(F32), axis=0).astype(BF16)
    near_rows = near[: 4 * size].reshape(4, size, columns)
    near_tail = jnp.pad(near[4 * size : 4 * size + 4][:, None, :], ((0, 0), (0, 7), (0, 0)))
    far = lax.all_to_all(jnp.concatenate([near_rows, near_tail], axis=1), "zh", 0, 0)
    far = jnp.sum(far.astype(F32), axis=0)
    return far[:size], far[size, :size]


def on_device(
    tokens,
    norm_gain,
    in_x_weight,
    in_z_weight,
    conv_state,
    conv_weight,
    conv_bias,
    proj_weight,
    delta_weight,
    delta_bias,
    decay_log,
    ssm_state,
    skip_gain,
    out_weight,
    post_gain,
    gate_weight,
    up_weight,
    down_weight,
):
    core = lax.axis_index("c")
    inner_dev = in_x_weight.shape[1]
    half = inner_dev // 2
    own_rows = conv_state.shape[1]
    token_rows, token_cols = tokens.shape

    gathered = spread(tokens, ROW_SWAPPED, 16)
    sums, first = reduce_rows(gathered, norm_gain, in_x_weight, in_z_weight, core)
    scale = lax.rsqrt(first / WIDTH + epsilon)[:, None]
    mixed_in = (sums * scale).astype(BF16)
    mine = lax.dynamic_slice_in_dim(mixed_in, core * own_rows, own_rows, 0)
    theirs = swap_cores(lax.dynamic_slice_in_dim(mixed_in, (1 - core) * own_rows, own_rows, 0))
    low = jnp.where(core == 0, mine, theirs)
    high = jnp.where(core == 0, theirs, mine)
    inner_x = jnp.concatenate([low[:, :half], high[:, :half]], axis=1)
    gate_z = jnp.concatenate([low[:, half:], high[:, half:]], axis=1)
    window = jnp.concatenate([conv_state, inner_x[None]], axis=0)
    conv_pre = jnp.sum(window.astype(F32) * conv_weight[:, None, :], axis=0) + conv_bias[None, :]
    signal = jax.nn.silu(conv_pre).astype(BF16)
    projected = jnp.sum(
        spread(dot(signal, proj_weight).astype(BF16), ROW_MAJOR, 16).astype(F32), axis=0
    )
    delta_low = projected[:, :RANK]
    input_map = projected[:, RANK : RANK + STATE]
    output_map = projected[:, RANK + STATE :]
    delta_scale = lax.rsqrt(jnp.mean(delta_low * delta_low, axis=1, keepdims=True) + epsilon)
    delta_norm = (delta_low * delta_scale).astype(BF16)
    delta = jax.nn.softplus(dot(delta_norm, delta_weight) + delta_bias[None, :])
    signal_wide = signal.astype(F32)
    decay = jnp.exp(delta[:, None, :] * (-jnp.exp(decay_log))[None, :, :])
    new_state = decay * ssm_state + (delta * signal_wide)[:, None, :] * input_map[:, :, None]
    readout = jnp.sum(new_state * output_map[:, :, None], axis=1) + skip_gain[None, :] * signal_wide
    gated = (readout * jax.nn.silu(gate_z.astype(F32))).astype(BF16)

    same = spread(gated, RING, 16)
    other = swap_cores(same)
    rows = jnp.concatenate(
        [jnp.where(core == 0, same, other), jnp.where(core == 0, other, same)], axis=1
    )
    out_terms = dot(rows.reshape(16 * token_rows, inner_dev), out_weight).astype(BF16)
    out_own = jnp.sum(
        lax.all_to_all(out_terms.reshape(16, token_rows, token_cols), ROW_MAJOR, 0, 0).astype(F32),
        axis=0,
    )
    residual = (tokens.astype(F32) + out_own).astype(BF16)

    gathered = spread(residual, ROW_SWAPPED, 16)
    sums, second = reduce_rows(gathered, post_gain, gate_weight, up_weight, core)
    scale = lax.rsqrt(second / WIDTH + epsilon)[:, None]
    hidden = gate_weight.shape[1] // 2
    both = sums * scale
    active = (jax.nn.silu(both[:, :hidden]) * both[:, hidden:]).astype(BF16)
    same = spread(active, RING, 16)
    other = swap_cores(same)
    same = same.reshape(16 * token_rows, hidden)
    other = other.reshape(16 * token_rows, hidden)
    down_terms = dot(same, lax.dynamic_slice_in_dim(down_weight, core * hidden, hidden, 0)) + dot(
        other, lax.dynamic_slice_in_dim(down_weight, (1 - core) * hidden, hidden, 0)
    )
    down_own = jnp.sum(
        lax.all_to_all(
            down_terms.astype(BF16).reshape(16, token_rows, token_cols), ROW_MAJOR, 0, 0
        ).astype(F32),
        axis=0,
    )
    mixed = (residual.astype(F32) + down_own).astype(BF16)
    return (mixed, window[1:], new_state)


def solution(mesh):
    fine = Mesh(np.asarray(mesh.devices).reshape(4, 4, 2, 4, 4), ("zh", "zl", "c", "y", "x"))
    batch, tensor = ("zh", "zl", "c"), ("y", "x")
    return jax.shard_map(
        on_device,
        mesh=fine,
        in_specs=(
            P(tensor, batch),
            P(batch),
            P(batch, tensor),
            P(batch, tensor),
            P(None, batch, tensor),
            P(None, tensor),
            P(tensor),
            P(tensor, None),
            P(None, tensor),
            P(tensor),
            P(None, tensor),
            P(batch, None, tensor),
            P(tensor),
            P(tensor, batch),
            P(batch),
            P(batch, tensor),
            P(batch, tensor),
            P(tensor, batch),
        ),
        out_specs=(P(tensor, batch), P(None, batch, tensor), P(batch, None, tensor)),
        check_vma=False,
    )
```

time: 767 us -> 268 us (0.35)
  waiting for transfers between devices: 369 us -> 53.2 us
  blocking collectives: 339 us -> 132 us
  starting transfers between devices: 23.6 us -> 66.5 us
  between operations: 15.4 us -> 1.22 us
    unnamed x12 -> x0, waiting for transfers between devices: 369 us -> none
    psum x3 -> x0, blocking collectives: 163 us -> none  [the longest x1 60.5 us: on_device(): lax.psum(jnp.dot(signal, proj_weight, preferred_element_type=jnp.float32)...]
    all_to_all x0 -> x6, blocking collectives: none -> 132 us  [the longest x2 50.5 us: reduce_rows(): lax.all_to_all(total, 'zl', 0, 0).astype(F32)]
    all_gather x4 -> x0, blocking collectives: 115 us -> none  [the longest x1 44.1 us: on_device(): lax.all_gather(gated, 'batch', axis=0, tiled=True)]
    unnamed x1 -> x0, blocking collectives: 61.8 us -> none
    all_to_all x0 -> x5, waiting for transfers between devices: none -> 46.7 us  [the longest x3 25.7 us: spread(): lax.all_to_all(jnp.broadcast_to(block[None], (count,) + block.shape), axe...]
    ppermute x0 -> x5, starting transfers between devices: none -> 35.9 us  [swap_cores(): return lax.ppermute(block, 'c', [(0, 1), (1, 0)])]
    all_to_all x0 -> x5, starting transfers between devices: none -> 30.6 us  [the longest x3 15 us: spread(): lax.all_to_all(jnp.broadcast_to(block[None], (count,) + block.shape), axe...]
  transfers between devices with their start and end apart: 9 -> 10, of which waited for: 4 -> 10; matrix products, arithmetic and copies ran while one was open for 0% -> 1% of each run, Pallas kernels for 0% -> 0%
where the time goes in v1:
time: 268 us; the launch traced here: 267 us
  blocking collectives  132 us (49%)
  starting transfers between devices  66.5 us (25%)
  waiting for transfers between devices  53.2 us (20%)
  other arithmetic  5.21 us (2%)
  local copies, waits for them, and re-layouts  4.39 us (2%)
  matrix products  3.73 us (1%)
    all_to_all x2, blocking collectives, reduce_rows(): lax.all_to_all(total, 'zl', 0, 0).astype(F32)  50.5 us
    all_to_all x2, blocking collectives, spread(): lax.all_to_all(jnp.broadcast_to(block[None], (count,) + block.shape), axe...  47.5 us
    ppermute x5, starting transfers between devices, swap_cores(): return lax.ppermute(block, 'c', [(0, 1), (1, 0)])  35.9 us
    all_to_all x3, waiting for transfers between devices, spread(): lax.all_to_all(jnp.broadcast_to(block[None], (count,) + block.shape), axe...  25.7 us
    all_to_all x1, blocking collectives, reduce_rows(): lax.all_to_all(jnp.concatenate([near_rows, near_tail], axis=1), 'zh', 0, 0)  22.4 us
    all_to_all x3, starting transfers between devices, spread(): lax.all_to_all(jnp.broadcast_to(block[None], (count,) + block.shape), axe...  15 us
    all_to_all x1, waiting for transfers between devices, reduce_rows(): lax.all_to_all(jnp.concatenate([near_rows, near_tail], axis=1), 'zh', 0, 0)  12.7 us
    all_to_all x1, starting transfers between devices, reduce_rows(): lax.all_to_all(jnp.concatenate([near_rows, near_tail], axis=1), 'zh', 0, 0)  12.1 us
  transfers between devices with their start and end apart: 10, of which 10 were waited for; matrix products, arithmetic and copies ran while one was open for 1% of the time, Pallas kernels for 0%

profile of v1, /device:TPU:1, one launch (start us, length us, event | category | flops | bytes accessed | tf_op | source)
XLA Modules:
  0.0 266.6 jit_solution(8483200200056026681)
XLA Ops:
  0.7 1.6 broadcast_in_dim.16
  2.2 7.6 %all-to-all-start = ((bf16[16,40,256]{2,1,0:T(8,128)(2,1)}), bf16[16,40,256]{2,1,0:T(8,128)(2,1)S(1)}, u32[]{:S(2)}, u32[]{:S(2)}) async-start(bf16[16,40,256]{2,1,0:T(8,128)(2,1)} %broadcast_in_dim.16), calls=%async_computation | async-start | bytes 655360 | tf_op jit(solution)/shard_map/all_to_all | solution.py:21
  9.9 7.6 %all-to-all-done = bf16[16,40,256]{2,1,0:T(8,128)(2,1)S(1)} async-done(((bf16[16,40,256]{2,1,0:T(8,128)(2,1)}), bf16[16,40,256]{2,1,0:T(8,128)(2,1)S(1)}, u32[]{:S(2)}, u32[]{:S(2)}) %all-to-all-start) | async-done | bytes 327712 | tf_op jit(solution)/shard_map/all_to_all | solution.py:21
  18.1 5.8 %collective-permute-start = (bf16[4,168,512]{2,1,0:T(8,128)(2,1)S(1)}, bf16[4,168,512]{2,1,0:T(8,128)(2,1)S(1)}, u32[]{:S(2)}, u32[]{:S(2)}) collective-permute-start(bf16[4,168,512]{2,1,0:T(8,128)(2,1)S(1)} %fusion.6), channel_id=1, source_target_pairs={{0,16},{16,0},{1,17},{17,1},{2,18},{18,2},{3,19},{19,3},{4,20},{20... | collective-permute-start | bytes 2064392 | tf_op jit(solution)/shard_map/ppermute | solution.py:25
  24.3 1.4 collective-permute-done
  25.9 21.5 %all_to_all.55 = bf16[4,168,512]{2,1,0:T(8,128)(2,1)S(1)} all-to-all(bf16[4,168,512]{2,1,0:T(8,128)(2,1)S(1)} %add_convert_fusion.1), channel_id=1, replica_groups=mesh['zh'=4,'zl'=4,'c'=2,'y'=4,'x'=4] {'zl'}, dimensions={0} | all-to-all | bytes 1376256 | tf_op jit(solution)/shard_map/all_to_all | solution.py:55
  48.2 12.1 %all-to-all-start.2 = ((bf16[4,48,512]{2,1,0:T(8,128)(2,1)}), bf16[4,48,512]{2,1,0:T(8,128)(2,1)S(1)}, u32[]{:S(2)}, u32[]{:S(2)}) async-start(bf16[4,48,512]{2,1,0:T(8,128)(2,1)} %fusion.26), calls=%async_computation.2 | async-start | bytes 393216 | tf_op jit(solution)/shard_map/all_to_all | solution.py:58
  60.3 12.7 %all-to-all-done.2 = bf16[4,48,512]{2,1,0:T(8,128)(2,1)S(1)} async-done(((bf16[4,48,512]{2,1,0:T(8,128)(2,1)}), bf16[4,48,512]{2,1,0:T(8,128)(2,1)S(1)}, u32[]{:S(2)}, u32[]{:S(2)}) %all-to-all-start.2) | async-done | bytes 196640 | tf_op jit(solution)/shard_map/all_to_all | solution.py:58
  73.2 7.0 %collective-permute-start.1 = (bf16[20,512]{1,0:T(8,128)(2,1)S(1)}, bf16[20,512]{1,0:T(8,128)(2,1)S(1)}, u32[]{:S(2)}, u32[]{:S(2)}) collective-permute-start(bf16[20,512]{1,0:T(8,128)(2,1)S(1)} %constant_dynamic-slice_fusion.4), channel_id=1, source_target_pairs={{0,16},{16,0},{1,17},{17,1},{2,18},{18,2},{3,19},{19,3},{4,20},{20... | collective-permute-start | bytes 61448 | tf_op jit(solution)/shard_map/ppermute | solution.py:25
  82.3 3.7 %all-to-all-start.3 = ((bf16[16,20,544]{2,1,0:T(8,128)(2,1)}), bf16[16,20,544]{2,1,0:T(8,128)(2,1)S(1)}, u32[]{:S(2)}, u32[]{:S(2)}) async-start(bf16[16,20,544]{2,1,0:T(8,128)(2,1)} %broadcast_in_dim.19), calls=%async_computation.3 | async-start | bytes 983040 | tf_op jit(solution)/shard_map/all_to_all | solution.py:21
  86.0 10.4 %all-to-all-done.3 = bf16[16,20,544]{2,1,0:T(8,128)(2,1)S(1)} async-done(((bf16[16,20,544]{2,1,0:T(8,128)(2,1)}), bf16[16,20,544]{2,1,0:T(8,128)(2,1)S(1)}, u32[]{:S(2)}, u32[]{:S(2)}) %all-to-all-start.3) | async-done | bytes 348192 | tf_op jit(solution)/shard_map/all_to_all | solution.py:21
  98.3 20.2 %all_to_all.56 = bf16[16,20,512]{2,1,0:T(8,128)(2,1)S(1)} all-to-all(bf16[16,20,512]{2,1,0:T(8,128)(2,1)S(1)} %broadcast_in_dim.20), channel_id=1, replica_groups=mesh['zh'=4,'zl'=4,'c'=2,'y'=4,'x'=4] {'zh','zl'}, dimensions={0} | all-to-all | bytes 655360 | tf_op jit(solution)/shard_map/all_to_all | solution.py:21
  118.5 9.9 %collective-permute-start.2 = (bf16[16,20,512]{2,1,0:T(8,128)(2,1)S(1)}, bf16[16,20,512]{2,1,0:T(8,128)(2,1)S(1)}, u32[]{:S(2)}, u32[]{:S(2)}) collective-permute-start(bf16[16,20,512]{2,1,0:T(8,128)(2,1)S(1)} %all_to_all.56), channel_id=1, source_target_pairs={{0,16},{16,0},{1,17},{17,1},{2,18},{18,2},{3,19},{19,3},{4,20},{20... | collective-permute-start | bytes 983048 | tf_op jit(solution)/shard_map/ppermute | solution.py:25
  131.2 12.0 %all_to_all.57 = bf16[16,40,256]{2,1,0:T(8,128)(2,1)S(1)} all-to-all(bf16[16,40,256]{2,1,0:T(8,128)(2,1)S(1)} %bitcast.45), channel_id=1, replica_groups=mesh['zh'=4,'zl'=4,'c'=2,'y'=4,'x'=4] {'y','x'}, dimensions={0} | all-to-all | bytes 655360 | tf_op jit(solution)/shard_map/all_to_all | solution.py:124
  143.9 3.7 %all-to-all-start.6 = ((bf16[16,40,256]{2,1,0:T(8,128)(2,1)}), bf16[16,40,256]{2,1,0:T(8,128)(2,1)S(1)}, u32[]{:S(2)}, u32[]{:S(2)}) async-start(bf16[16,40,256]{2,1,0:T(8,128)(2,1)} %broadcast_in_dim.21), calls=%async_computation.6 | async-start | bytes 655360 | tf_op jit(solution)/shard_map/all_to_all | solution.py:21
  147.7 7.6 %all-to-all-done.6 = bf16[16,40,256]{2,1,0:T(8,128)(2,1)S(1)} async-done(((bf16[16,40,256]{2,1,0:T(8,128)(2,1)}), bf16[16,40,256]{2,1,0:T(8,128)(2,1)S(1)}, u32[]{:S(2)}, u32[]{:S(2)}) %all-to-all-start.6) | async-done | bytes 327712 | tf_op jit(solution)/shard_map/all_to_all | solution.py:21
  156.1 4.4 %collective-permute-start.3 = (bf16[4,168,768]{2,1,0:T(8,128)(2,1)S(1)}, bf16[4,168,768]{2,1,0:T(8,128)(2,1)S(1)}, u32[]{:S(2)}, u32[]{:S(2)}) collective-permute-start(bf16[4,168,768]{2,1,0:T(8,128)(2,1)S(1)} %fusion.4), channel_id=1, source_target_pairs={{0,16},{16,0},{1,17},{17,1},{2,18},{18,2},{3,19},{19,3},{4,20},{20... | collective-permute-start | bytes 3096584 | tf_op jit(solution)/shard_map/ppermute | solution.py:25
  160.9 1.8 collective-permute-done.3
  163.0 29.0 %all_to_all.58 = bf16[4,168,768]{2,1,0:T(8,128)(2,1)S(1)} all-to-all(bf16[4,168,768]{2,1,0:T(8,128)(2,1)S(1)} %add_convert_fusion), channel_id=1, replica_groups=mesh['zh'=4,'zl'=4,'c'=2,'y'=4,'x'=4] {'zl'}, dimensions={0} | all-to-all | bytes 2064384 | tf_op jit(solution)/shard_map/all_to_all | solution.py:55
  192.3 22.4 %all_to_all.59 = bf16[4,48,768]{2,1,0:T(8,128)(2,1)S(1)} all-to-all(bf16[4,48,768]{2,1,0:T(8,128)(2,1)S(1)} %fusion.19), channel_id=1, replica_groups=mesh['zh'=4,'zl'=4,'c'=2,'y'=4,'x'=4] {'zh'}, dimensions={0} | all-to-all | bytes 589824 | tf_op jit(solution)/shard_map/all_to_all | solution.py:58
  214.9 27.3 %all_to_all.60 = bf16[16,40,384]{2,1,0:T(8,128)(2,1)S(1)} all-to-all(bf16[16,40,384]{2,1,0:T(8,128)(2,1)S(1)} %broadcast_in_dim.23), channel_id=1, replica_groups=mesh['zh'=4,'zl'=4,'c'=2,'y'=4,'x'=4] {'zh','zl'}, dimensions={0} | all-to-all | bytes 983040 | tf_op jit(solution)/shard_map/all_to_all | solution.py:21
  242.2 8.8 %collective-permute-start.4 = (bf16[16,40,384]{2,1,0:T(8,128)(2,1)S(1)}, bf16[16,40,384]{2,1,0:T(8,128)(2,1)S(1)}, u32[]{:S(2)}, u32[]{:S(2)}) collective-permute-start(bf16[16,40,384]{2,1,0:T(8,128)(2,1)S(1)} %all_to_all.60), channel_id=1, source_target_pairs={{0,16},{16,0},{1,17},{17,1},{2,18},{18,2},{3,19},{19,3},{4,20},{20... | collective-permute-start | bytes 1474568 | tf_op jit(solution)/shard_map/ppermute | solution.py:25
  253.5 3.5 %all-to-all-start.10 = ((bf16[16,40,256]{2,1,0:T(8,128)(2,1)}), bf16[16,40,256]{2,1,0:T(8,128)(2,1)S(1)}, u32[]{:S(2)}, u32[]{:S(2)}) async-start(bf16[16,40,256]{2,1,0:T(8,128)(2,1)} %bitcast.19), calls=%async_computation.10 | async-start | bytes 655360 | tf_op jit(solution)/shard_map/all_to_all | solution.py:143
  257.7 8.2 %all-to-all-done.10 = bf16[16,40,256]{2,1,0:T(8,128)(2,1)S(1)} async-done(((bf16[16,40,256]{2,1,0:T(8,128)(2,1)}), bf16[16,40,256]{2,1,0:T(8,128)(2,1)S(1)}, u32[]{:S(2)}, u32[]{:S(2)}) %all-to-all-start.10) | async-done | bytes 327712 | tf_op jit(solution)/shard_map/all_to_all | solution.py:143
  (97 shorter events, 15.0 us)
Async XLA Ops:
  0.6 80.5 %copy-start = (bf16[512,544]{0,1:T(8,128)(2,1)S(1)}, bf16[512,544]{0,1:T(8,128)(2,1)}, u32[]{:S(2)}) copy-start(bf16[512,544]{0,1:T(8,128)(2,1)} %param.25) | copy-start | bytes 1671172
  0.6 9.2 %copy-start.8 = (bf16[256,512]{1,0:T(8,128)(2,1)S(1)}, bf16[256,512]{1,0:T(8,128)(2,1)}, u32[]{:S(2)}) copy-start(bf16[256,512]{1,0:T(8,128)(2,1)} %param.20) | copy-start | bytes 786436
  0.7 16.9 %copy-start.16 = (f32[256]{0:T(256)S(1)}, f32[256]{0:T(256)}, u32[]{:S(2)}) copy-start(f32[256]{0:T(256)} %param.19) | copy-start | bytes 3076
  2.2 15.3 %all-to-all-start = ((bf16[16,40,256]{2,1,0:T(8,128)(2,1)}), bf16[16,40,256]{2,1,0:T(8,128)(2,1)S(1)}, u32[]{:S(2)}, u32[]{:S(2)}) async-start(bf16[16,40,256]{2,1,0:T(8,128)(2,1)} %broadcast_in_dim.16), calls=%async_computation | async-start | bytes 655360 | tf_op jit(solution)/shard_map/all_to_all | solution.py:21
  18.1 7.6 %collective-permute-start = (bf16[4,168,512]{2,1,0:T(8,128)(2,1)S(1)}, bf16[4,168,512]{2,1,0:T(8,128)(2,1)S(1)}, u32[]{:S(2)}, u32[]{:S(2)}) collective-permute-start(bf16[4,168,512]{2,1,0:T(8,128)(2,1)S(1)} %fusion.6), channel_id=1, source_target_pairs={{0,16},{16,0},{1,17},{17,1},{2,18},{18,2},{3,19},{19,3},{4,20},{20... | collective-permute-start | bytes 2064392 | tf_op jit(solution)/shard_map/ppermute | solution.py:25
  47.4 33.6 %copy-start.6 = (bf16[3,20,512]{2,1,0:T(8,128)(2,1)S(1)}, bf16[3,20,512]{2,1,0:T(8,128)(2,1)}, u32[]{:S(2)}) copy-start(bf16[3,20,512]{2,1,0:T(8,128)(2,1)} %param.22) | copy-start | bytes 184324
  47.5 33.6 %copy-start.13 = (f32[4,512]{1,0:T(4,128)S(1)}, f32[4,512]{1,0:T(4,128)}, u32[]{:S(2)}) copy-start(f32[4,512]{1,0:T(4,128)} %param.23) | copy-start | bytes 24580
  47.5 33.7 %copy-start.12 = (f32[512]{0:T(512)S(1)}, f32[512]{0:T(512)}, u32[]{:S(2)}) copy-start(f32[512]{0:T(512)} %param.24) | copy-start | bytes 6148
  48.2 24.8 %all-to-all-start.2 = ((bf16[4,48,512]{2,1,0:T(8,128)(2,1)}), bf16[4,48,512]{2,1,0:T(8,128)(2,1)S(1)}, u32[]{:S(2)}, u32[]{:S(2)}) async-start(bf16[4,48,512]{2,1,0:T(8,128)(2,1)} %fusion.26), calls=%async_computation.2 | async-start | bytes 393216 | tf_op jit(solution)/shard_map/all_to_all | solution.py:58
  73.2 7.8 %collective-permute-start.1 = (bf16[20,512]{1,0:T(8,128)(2,1)S(1)}, bf16[20,512]{1,0:T(8,128)(2,1)S(1)}, u32[]{:S(2)}, u32[]{:S(2)}) collective-permute-start(bf16[20,512]{1,0:T(8,128)(2,1)S(1)} %constant_dynamic-slice_fusion.4), channel_id=1, source_target_pairs={{0,16},{16,0},{1,17},{17,1},{2,18},{18,2},{3,19},{19,3},{4,20},{20... | collective-permute-start | bytes 61448 | tf_op jit(solution)/shard_map/ppermute | solution.py:25
  81.4 15.4 %copy-start.2 = (bf16[512,512]{1,0:T(8,128)(2,1)S(1)}, bf16[512,512]{1,0:T(8,128)(2,1)}, u32[]{:S(2)}) copy-start(bf16[512,512]{1,0:T(8,128)(2,1)} %param.26) | copy-start | bytes 1572868
  81.5 15.3 %copy-start.14 = (f32[512]{0:T(512)S(1)}, f32[512]{0:T(512)}, u32[]{:S(2)}) copy-start(f32[512]{0:T(512)} %param.27) | copy-start | bytes 6148
  82.3 14.8 %copy-start.1 = (f32[20,16,512]{2,1,0:T(8,128)S(1)}, f32[20,16,512]{2,1,0:T(8,128)}, u32[]{:S(2)}) copy-start(f32[20,16,512]{2,1,0:T(8,128)} %param.29) | copy-start | bytes 1966084
  82.3 14.2 %all-to-all-start.3 = ((bf16[16,20,544]{2,1,0:T(8,128)(2,1)}), bf16[16,20,544]{2,1,0:T(8,128)(2,1)S(1)}, u32[]{:S(2)}, u32[]{:S(2)}) async-start(bf16[16,20,544]{2,1,0:T(8,128)(2,1)} %broadcast_in_dim.19), calls=%async_computation.3 | async-start | bytes 983040 | tf_op jit(solution)/shard_map/all_to_all | solution.py:21
  118.5 11.3 %collective-permute-start.2 = (bf16[16,20,512]{2,1,0:T(8,128)(2,1)S(1)}, bf16[16,20,512]{2,1,0:T(8,128)(2,1)S(1)}, u32[]{:S(2)}, u32[]{:S(2)}) collective-permute-start(bf16[16,20,512]{2,1,0:T(8,128)(2,1)S(1)} %all_to_all.56), channel_id=1, source_target_pairs={{0,16},{16,0},{1,17},{17,1},{2,18},{18,2},{3,19},{19,3},{4,20},{20... | collective-permute-start | bytes 983048 | tf_op jit(solution)/shard_map/ppermute | solution.py:25
  130.8 12.4 %copy-start.10 = (bf16[40,256]{1,0:T(8,128)(2,1)S(1)}, bf16[40,256]{1,0:T(8,128)(2,1)}, u32[]{:S(2)}) copy-start(bf16[40,256]{1,0:T(8,128)(2,1)} %param.18) | copy-start | bytes 61444
  131.1 16.5 %copy-start.4 = (bf16[256,768]{1,0:T(8,128)(2,1)S(1)}, bf16[256,768]{1,0:T(8,128)(2,1)}, u32[]{:S(2)}) copy-start(bf16[256,768]{1,0:T(8,128)(2,1)} %param.34) | copy-start | bytes 1179652
  131.1 16.5 %copy-start.5 = (bf16[256,768]{1,0:T(8,128)(2,1)S(1)}, bf16[256,768]{1,0:T(8,128)(2,1)}, u32[]{:S(2)}) copy-start(bf16[256,768]{1,0:T(8,128)(2,1)} %param.33) | copy-start | bytes 1179652
  143.9 11.4 %copy-start.17 = (f32[256]{0:T(256)S(1)}, f32[256]{0:T(256)}, u32[]{:S(2)}) copy-start(f32[256]{0:T(256)} %param.32) | copy-start | bytes 3076
  143.9 11.4 %all-to-all-start.6 = ((bf16[16,40,256]{2,1,0:T(8,128)(2,1)}), bf16[16,40,256]{2,1,0:T(8,128)(2,1)S(1)}, u32[]{:S(2)}, u32[]{:S(2)}) async-start(bf16[16,40,256]{2,1,0:T(8,128)(2,1)} %broadcast_in_dim.21), calls=%async_computation.6 | async-start | bytes 655360 | tf_op jit(solution)/shard_map/all_to_all | solution.py:21
  156.1 6.7 %collective-permute-start.3 = (bf16[4,168,768]{2,1,0:T(8,128)(2,1)S(1)}, bf16[4,168,768]{2,1,0:T(8,128)(2,1)S(1)}, u32[]{:S(2)}, u32[]{:S(2)}) collective-permute-start(bf16[4,168,768]{2,1,0:T(8,128)(2,1)S(1)} %fusion.4), channel_id=1, source_target_pairs={{0,16},{16,0},{1,17},{17,1},{2,18},{18,2},{3,19},{19,3},{4,20},{20... | collective-permute-start | bytes 3096584 | tf_op jit(solution)/shard_map/ppermute | solution.py:25
  214.7 36.3 %copy-start.3 = (bf16[768,256]{1,0:T(8,128)(2,1)S(1)}, bf16[768,256]{1,0:T(8,128)(2,1)}, u32[]{:S(2)}) copy-start(bf16[768,256]{1,0:T(8,128)(2,1)} %param.35) | copy-start | bytes 1179652
  242.2 10.3 %collective-permute-start.4 = (bf16[16,40,384]{2,1,0:T(8,128)(2,1)S(1)}, bf16[16,40,384]{2,1,0:T(8,128)(2,1)S(1)}, u32[]{:S(2)}, u32[]{:S(2)}) collective-permute-start(bf16[16,40,384]{2,1,0:T(8,128)(2,1)S(1)} %all_to_all.60), channel_id=1, source_target_pairs={{0,16},{16,0},{1,17},{17,1},{2,18},{18,2},{3,19},{19,3},{4,20},{20... | collective-permute-start | bytes 1474568 | tf_op jit(solution)/shard_map/ppermute | solution.py:25
  253.5 12.4 %all-to-all-start.10 = ((bf16[16,40,256]{2,1,0:T(8,128)(2,1)}), bf16[16,40,256]{2,1,0:T(8,128)(2,1)S(1)}, u32[]{:S(2)}, u32[]{:S(2)}) async-start(bf16[16,40,256]{2,1,0:T(8,128)(2,1)} %bitcast.19), calls=%async_computation.10 | async-start | bytes 655360 | tf_op jit(solution)/shard_map/all_to_all | solution.py:143
  (4 other events, 16.4 us)

commit v2 on v1

v2 whole, which is shorter than its diff:
```python
import jax
import jax.numpy as jnp
import numpy as np
from jax import lax
from jax.sharding import Mesh, PartitionSpec as P

WIDTH = 8192
RANK = 512
STATE = 16

epsilon = 1e-06

F32 = jnp.float32
BF16 = jnp.bfloat16
TENSOR = ("y", "xm", "xp")
TENSOR_PAIRS = ("xp", "y", "xm")
RING = ("zh", "zm", "zp")
PAIRS = ("zh", "zm")


def spread(block, axes, count):
    return lax.all_to_all(jnp.broadcast_to(block[None], (count,) + block.shape), axes, 0, 0)


def swap(block, axis):
    return lax.ppermute(block, axis, [(0, 1), (1, 0)])


def dot(left, right):
    return jnp.dot(left, right, preferred_element_type=F32)


def add(left, right):
    return (left.astype(F32) + right.astype(F32)).astype(BF16)


def half_columns(weight, which):
    half = weight.shape[1] // 2
    return lax.dynamic_slice_in_dim(weight, which * half, half, 1)


def half_rows(block, which):
    half = block.shape[0] // 2
    return lax.dynamic_slice_in_dim(block, which * half, half, 0)


def reduce_rows(block, size, gain, left_weight, right_weight, axes):
    core, pair = lax.axis_index("c"), lax.axis_index("zp")
    groups, padded, depth = block.shape
    wide = spread(block.reshape(groups * padded, depth), TENSOR_PAIRS, 16).astype(F32)
    scaled = (wide * gain[None, None, :]).astype(BF16).reshape(16 * groups * padded, depth)
    squares = jnp.sum(wide * wide, axis=2).reshape(16 * groups, 1, padded)
    half = left_weight.shape[1] // 2
    columns = half + half
    marks = jnp.pad(squares.astype(BF16), ((0, 0), (0, 0), (0, columns - padded)))
    spare = lax.broadcasted_iota(jnp.int32, (1, padded, columns), 1) == size

    def partial(which):
        weight = jnp.concatenate(
            [half_columns(left_weight, which), half_columns(right_weight, which)], axis=1
        )
        return jnp.where(
            spare, marks, dot(scaled, weight).astype(BF16).reshape(16 * groups, padded, columns)
        )

    received = swap(partial(1 - core), "c")
    own = partial(core)
    sent = add(half_rows(own, 1 - pair), half_rows(received, 1 - pair))
    kept = add(half_rows(own, pair), half_rows(received, pair))
    total = add(kept, swap(sent, "zp"))
    far = lax.all_to_all(total, axes, 0, 0).astype(F32)
    return jnp.sum(far.reshape(8, groups, padded, columns), axis=0)


def on_device(
    tokens,
    norm_gain,
    in_x_weight,
    in_z_weight,
    conv_state,
    conv_weight,
    conv_bias,
    proj_weight,
    delta_weight,
    delta_bias,
    decay_log,
    ssm_state,
    skip_gain,
    out_weight,
    post_gain,
    gate_weight,
    up_weight,
    down_weight,
):
    core, pair = lax.axis_index("c"), lax.axis_index("zp")
    inner_dev = in_x_weight.shape[1]
    half = inner_dev // 2
    own_rows = conv_state.shape[1]
    token_rows, token_cols = tokens.shape

    block = jnp.pad(tokens.reshape(2, own_rows, token_cols), ((0, 0), (0, 4), (0, 0)))
    sums = reduce_rows(
        block, own_rows, norm_gain, in_x_weight, in_z_weight, ("zh", "zm", "c")
    )
    scale = lax.rsqrt(sums[0, own_rows, :own_rows] / WIDTH + epsilon)[:, None]
    mixed_in = (sums[:, :own_rows] * scale[None]).astype(BF16)
    inner_x = jnp.concatenate([mixed_in[0, :, :half], mixed_in[1, :, :half]], axis=1)
    gate_z = jnp.concatenate([mixed_in[0, :, half:], mixed_in[1, :, half:]], axis=1)
    window = jnp.concatenate([conv_state, inner_x[None]], axis=0)
    conv_pre = jnp.sum(window.astype(F32) * conv_weight[:, None, :], axis=0) + conv_bias[None, :]
    signal = jax.nn.silu(conv_pre).astype(BF16)
    projected = jnp.sum(
        spread(dot(signal, proj_weight).astype(BF16), TENSOR, 16).astype(F32), axis=0
    )
    delta_low = projected[:, :RANK]
    input_map = projected[:, RANK : RANK + STATE]
    output_map = projected[:, RANK + STATE :]
    delta_scale = lax.rsqrt(jnp.mean(delta_low * delta_low, axis=1, keepdims=True) + epsilon)
    delta_norm = (delta_low * delta_scale).astype(BF16)
    delta = jax.nn.softplus(dot(delta_norm, delta_weight) + delta_bias[None, :])
    signal_wide = signal.astype(F32)
    decay = jnp.exp(delta[:, None, :] * (-jnp.exp(decay_log))[None, :, :])
    new_state = decay * ssm_state + (delta * signal_wide)[:, None, :] * input_map[:, :, None]
    readout = jnp.sum(new_state * output_map[:, :, None], axis=1) + skip_gain[None, :] * signal_wide
    gated = (readout * jax.nn.silu(gate_z.astype(F32))).astype(BF16)

    dense = lax.optimization_barrier(gated).reshape(16, own_rows * inner_dev // 16)
    same = spread(dense, RING, 16).reshape(16, own_rows, inner_dev)
    same = lax.optimization_barrier(same)
    other = swap(same, "c")
    rows = jnp.concatenate(
        [jnp.where(core == 0, same, other), jnp.where(core == 0, other, same)], axis=1
    )
    out_terms = dot(rows.reshape(16 * token_rows, inner_dev), out_weight).astype(BF16)
    out_own = jnp.sum(
        lax.all_to_all(out_terms.reshape(16, token_rows, token_cols), TENSOR, 0, 0).astype(F32),
        axis=0,
    )
    residual = (tokens.astype(F32) + out_own).astype(BF16)

    block = jnp.pad(residual, ((0, 8), (0, 0)))[None]
    sums = reduce_rows(block, token_rows, post_gain, gate_weight, up_weight, PAIRS)[0]
    scale = lax.rsqrt(sums[token_rows, :token_rows] / WIDTH + epsilon)[:, None]
    hidden = gate_weight.shape[1] // 2
    both = sums[:token_rows] * scale
    active = (jax.nn.silu(both[:, :hidden]) * both[:, hidden:]).astype(BF16)
    near = spread(active, PAIRS, 8)
    next_to = swap(near, "zp")
    same = jnp.concatenate(
        [jnp.where(pair == 0, near, next_to), jnp.where(pair == 0, next_to, near)], axis=0
    )
    other = swap(same, "c")
    same = same.reshape(16 * token_rows, hidden)
    other = other.reshape(16 * token_rows, hidden)
    down_terms = dot(same, half_rows(down_weight, core)) + dot(
        other, half_rows(down_weight, 1 - core)
    )
    down_own = jnp.sum(
        lax.all_to_all(
            down_terms.astype(BF16).reshape(16, token_rows, token_cols), TENSOR_PAIRS, 0, 0
        ).astype(F32),
        axis=0,
    )
    mixed = (residual.astype(F32) + down_own).astype(BF16)
    return (mixed, window[1:], new_state)


def solution(mesh):
    fine = Mesh(
        np.asarray(mesh.devices).reshape(4, 2, 2, 2, 4, 2, 2),
        ("zh", "zm", "zp", "c", "y", "xm", "xp"),
    )
    batch, tensor = ("zh", "zm", "zp", "c"), TENSOR
    return jax.shard_map(
        on_device,
        mesh=fine,
        in_specs=(
            P(tensor, batch),
            P(batch),
            P(batch, tensor),
            P(batch, tensor),
            P(None, batch, tensor),
            P(None, tensor),
            P(tensor),
            P(tensor, None),
            P(None, tensor),
            P(tensor),
            P(None, tensor),
            P(batch, None, tensor),
            P(tensor),
            P(tensor, batch),
            P(batch),
            P(batch, tensor),
            P(batch, tensor),
            P(tensor, batch),
        ),
        out_specs=(P(tensor, batch), P(None, batch, tensor), P(batch, None, tensor)),
        check_vma=False,
    )
```

time: 268 us -> 272 us (1.015)
  waiting for transfers between devices: 53.2 us -> 66.8 us
  starting transfers between devices: 66.5 us -> 55.3 us
    ppermute x5 -> x7, waiting for transfers between devices: 6.49 us -> 34.6 us  [swap(): return lax.ppermute(block, axis, [(0, 1), (1, 0)])]
    all_to_all x1 -> x0, waiting for transfers between devices: 12.7 us -> none  [reduce_rows(): lax.all_to_all(jnp.concatenate([near_rows, near_tail], axis=1), 'zh', 0, 0)]
    all_to_all x1 -> x0, starting transfers between devices: 12.1 us -> none  [reduce_rows(): lax.all_to_all(jnp.concatenate([near_rows, near_tail], axis=1), 'zh', 0, 0)]
    ppermute x5 -> x7, starting transfers between devices: 35.9 us -> 36.8 us  [swap(): return lax.ppermute(block, axis, [(0, 1), (1, 0)])]
    all_to_all x4 -> x3, blocking collectives: 84.9 us -> 84.3 us  [the longest x2 72.6 us: reduce_rows(): far = lax.all_to_all(total, axes, 0, 0).astype(F32)]
  transfers between devices with their start and end apart: 10 -> 11, of which waited for: 10 -> 11; matrix products, arithmetic and copies ran while one was open for 1% -> 0% of each run, Pallas kernels for 0% -> 0%
where the time goes in v2:
time: 272 us; the launch traced here: 271 us
  blocking collectives  133 us (49%)
  waiting for transfers between devices  66.8 us (25%)
  starting transfers between devices  55.3 us (20%)
  other arithmetic  7.02 us (3%)
  local copies, waits for them, and re-layouts  4.03 us (1%)
  matrix products  3.89 us (1%)
    all_to_all x2, blocking collectives, reduce_rows(): far = lax.all_to_all(total, axes, 0, 0).astype(F32)  72.6 us
    all_to_all x2, blocking collectives, spread(): lax.all_to_all(jnp.broadcast_to(block[None], (count,) + block.shape), axe...  48.3 us
    ppermute x7, starting transfers between devices, swap(): return lax.ppermute(block, axis, [(0, 1), (1, 0)])  36.8 us
    ppermute x7, waiting for transfers between devices, swap(): return lax.ppermute(block, axis, [(0, 1), (1, 0)])  34.6 us
    all_to_all x3, waiting for transfers between devices, spread(): lax.all_to_all(jnp.broadcast_to(block[None], (count,) + block.shape), axe...  24.6 us
    all_to_all x3, starting transfers between devices, spread(): lax.all_to_all(jnp.broadcast_to(block[None], (count,) + block.shape), axe...  15 us
    all_to_all x1, blocking collectives, on_device(): lax.all_to_all(out_terms.reshape(16, token_rows, token_cols), TENSOR, 0, 0)  11.7 us
    all_to_all x1, waiting for transfers between devices, on_device(): lax.all_to_all(down_terms.astype(BF16).reshape(16, token_rows, token_cols...  7.55 us
  transfers between devices with their start and end apart: 11, of which 11 were waited for; matrix products, arithmetic and copies ran while one was open for 0% of the time, Pallas kernels for 0%

profile of v2, /device:TPU:1, one launch (start us, length us, event | category | flops | bytes accessed | tf_op | source)
XLA Modules:
  0.0 270.9 jit_solution(9562803207511080849)
XLA Ops:
  2.3 7.6 %all-to-all-start = ((bf16[16,48,256]{2,1,0:T(8,128)(2,1)}), bf16[16,48,256]{2,1,0:T(8,128)(2,1)S(1)}, u32[]{:S(2)}, u32[]{:S(2)}) async-start(bf16[16,48,256]{2,1,0:T(8,128)(2,1)} %broadcast_in_dim.102), calls=%async_computation | async-start | bytes 786432 | tf_op jit(solution)/shard_map/all_to_all | solution.py:22
  10.0 8.0 %all-to-all-done = bf16[16,48,256]{2,1,0:T(8,128)(2,1)S(1)} async-done(((bf16[16,48,256]{2,1,0:T(8,128)(2,1)}), bf16[16,48,256]{2,1,0:T(8,128)(2,1)S(1)}, u32[]{:S(2)}, u32[]{:S(2)}) %all-to-all-start) | async-done | bytes 393248 | tf_op jit(solution)/shard_map/all_to_all | solution.py:22
  19.2 5.7 %collective-permute-start = (bf16[32,24,512]{2,1,0:T(8,128)(2,1)S(1)}, bf16[32,24,512]{2,1,0:T(8,128)(2,1)S(1)}, u32[]{:S(2)}, u32[]{:S(2)}) collective-permute-start(bf16[32,24,512]{2,1,0:T(8,128)(2,1)S(1)} %get-tuple-element.28), channel_id=1, source_target_pairs={{0,16},{16,0},{1,17},{17,1},{2,18},{18,2},{3,19},{19,3},{4,20},{20... | collective-permute-start | bytes 2359304 | tf_op jit(solution)/shard_map/ppermute | solution.py:26
  26.9 2.4 collective-permute-start.1
  29.4 9.8 %collective-permute-done.1 = bf16[16,24,512]{2,1,0:T(8,128)(2,1)S(1)} collective-permute-done((bf16[16,24,512]{2,1,0:T(8,128)(2,1)S(1)}, bf16[16,24,512]{2,1,0:T(8,128)(2,1)S(1)}, u32[]{:S(2)}, u32[]{:S(2)}) %collective-permute-start.1) | collective-permute-done | bytes 393248 | tf_op jit(solution)/shard_map/ppermute | solution.py:26
  39.3 40.8 %all_to_all.45 = bf16[16,24,512]{2,1,0:T(8,128)(2,1)S(1)} all-to-all(bf16[16,24,512]{2,1,0:T(8,128)(2,1)S(1)} %add_convert_fusion.3), channel_id=1, replica_groups=mesh['zh'=4,'zm'=2,'zp'=2,'c'=2,'y'=4,'xm'=2,'xp'=2] {'zh','zm','c'}, dimensions={0} | all-to-all | bytes 786432 | tf_op jit(solution)/shard_map/all_to_all | solution.py:71
  81.5 3.7 %all-to-all-start.2 = ((bf16[16,20,544]{2,1,0:T(8,128)(2,1)}), bf16[16,20,544]{2,1,0:T(8,128)(2,1)S(1)}, u32[]{:S(2)}, u32[]{:S(2)}) async-start(bf16[16,20,544]{2,1,0:T(8,128)(2,1)} %broadcast_in_dim.106), calls=%async_computation.2 | async-start | bytes 983040 | tf_op jit(solution)/shard_map/all_to_all | solution.py:22
  85.2 8.7 %all-to-all-done.2 = bf16[16,20,544]{2,1,0:T(8,128)(2,1)S(1)} async-done(((bf16[16,20,544]{2,1,0:T(8,128)(2,1)}), bf16[16,20,544]{2,1,0:T(8,128)(2,1)S(1)}, u32[]{:S(2)}, u32[]{:S(2)}) %all-to-all-start.2) | async-done | bytes 348192 | tf_op jit(solution)/shard_map/all_to_all | solution.py:22
  95.8 20.6 %all_to_all.46 = bf16[16,16,640]{2,1,0:T(8,128)(2,1)S(1)} all-to-all(bf16[16,16,640]{2,1,0:T(8,128)(2,1)S(1)} %broadcast_in_dim.108), channel_id=1, replica_groups=mesh['zh'=4,'zm'=2,'zp'=2,'c'=2,'y'=4,'xm'=2,'xp'=2] {'zh','zm','zp'}, dimensions={0} | all-to-all | bytes 655360 | tf_op jit(solution)/shard_map/all_to_all | solution.py:22
  116.7 9.4 %collective-permute-start.2 = (bf16[16,20,512]{2,1,0:T(8,128)(2,1)S(1)}, bf16[16,20,512]{2,1,0:T(8,128)(2,1)S(1)}, u32[]{:S(2)}, u32[]{:S(2)}) collective-permute-start(bf16[16,20,512]{2,1,0:T(8,128)(2,1)S(1)} %reshape.133), channel_id=1, source_target_pairs={{0,16},{16,0},{1,17},{17,1},{2,18},{18,2},{3,19},{19,3},{4,20},{20... | collective-permute-start | bytes 983048 | tf_op jit(solution)/shard_map/ppermute | solution.py:26
  128.0 11.7 %all_to_all.47 = bf16[16,40,256]{2,1,0:T(8,128)(2,1)S(1)} all-to-all(bf16[16,40,256]{2,1,0:T(8,128)(2,1)S(1)} %bitcast.61), channel_id=1, replica_groups=mesh['zh'=4,'zm'=2,'zp'=2,'c'=2,'y'=4,'xm'=2,'xp'=2] {'y','xm','xp'}, dimensions={0} | all-to-all | bytes 655360 | tf_op jit(solution)/shard_map/all_to_all | solution.py:136
  140.6 3.7 %all-to-all-start.5 = ((bf16[16,48,256]{2,1,0:T(8,128)(2,1)}), bf16[16,48,256]{2,1,0:T(8,128)(2,1)S(1)}, u32[]{:S(2)}, u32[]{:S(2)}) async-start(bf16[16,48,256]{2,1,0:T(8,128)(2,1)} %broadcast_in_dim.110), calls=%async_computation.5 | async-start | bytes 786432 | tf_op jit(solution)/shard_map/all_to_all | solution.py:22
  144.4 7.9 %all-to-all-done.5 = bf16[16,48,256]{2,1,0:T(8,128)(2,1)S(1)} async-done(((bf16[16,48,256]{2,1,0:T(8,128)(2,1)}), bf16[16,48,256]{2,1,0:T(8,128)(2,1)S(1)}, u32[]{:S(2)}, u32[]{:S(2)}) %all-to-all-start.5) | async-done | bytes 393248 | tf_op jit(solution)/shard_map/all_to_all | solution.py:22
  153.7 4.6 %collective-permute-start.3 = (bf16[16,48,768]{2,1,0:T(8,128)(2,1)S(1)}, bf16[16,48,768]{2,1,0:T(8,128)(2,1)}, u32[]{:S(2)}, u32[]{:S(2)}) collective-permute-start(bf16[16,48,768]{2,1,0:T(8,128)(2,1)S(1)} %get-tuple-element.30), channel_id=1, source_target_pairs={{0,16},{16,0},{1,17},{17,1},{2,18},{18,2},{3,19},{19,3},{4,20},{20... | collective-permute-start | bytes 3538952 | tf_op jit(solution)/shard_map/ppermute | solution.py:26
  158.3 2.6 collective-permute-done.3
  162.1 2.4 collective-permute-start.4
  164.5 14.0 %collective-permute-done.4 = bf16[8,48,768]{2,1,0:T(8,128)(2,1)S(1)} collective-permute-done((bf16[8,48,768]{2,1,0:T(8,128)(2,1)S(1)}, bf16[8,48,768]{2,1,0:T(8,128)(2,1)S(1)}, u32[]{:S(2)}, u32[]{:S(2)}) %collective-permute-start.4) | collective-permute-done | bytes 589856 | tf_op jit(solution)/shard_map/ppermute | solution.py:26
  179.8 31.9 %all_to_all.48 = bf16[8,48,768]{2,1,0:T(8,128)(2,1)S(1)} all-to-all(bf16[8,48,768]{2,1,0:T(8,128)(2,1)S(1)} %add_convert_fusion), channel_id=1, replica_groups=mesh['zh'=4,'zm'=2,'zp'=2,'c'=2,'y'=4,'xm'=2,'xp'=2] {'zh','zm'}, dimensions={0} | all-to-all | bytes 1179648 | tf_op jit(solution)/shard_map/all_to_all | solution.py:71
  211.9 27.7 %all_to_all.49 = bf16[8,40,384]{2,1,0:T(8,128)(2,1)S(1)} all-to-all(bf16[8,40,384]{2,1,0:T(8,128)(2,1)S(1)} %broadcast_in_dim.113), channel_id=1, replica_groups=mesh['zh'=4,'zm'=2,'zp'=2,'c'=2,'y'=4,'xm'=2,'xp'=2] {'zh','zm'}, dimensions={0} | all-to-all | bytes 491520 | tf_op jit(solution)/shard_map/all_to_all | solution.py:22
  239.6 5.0 %collective-permute-start.5 = (bf16[8,40,384]{2,1,0:T(8,128)(2,1)S(1)}, bf16[8,40,384]{2,1,0:T(8,128)(2,1)S(1)}, u32[]{:S(2)}, u32[]{:S(2)}) collective-permute-start(bf16[8,40,384]{2,1,0:T(8,128)(2,1)S(1)} %all_to_all.49), channel_id=1, source_target_pairs={{0,32},{32,0},{1,33},{33,1},{2,34},{34,2},{3,35},{35,3},{4,36},{36... | collective-permute-start | bytes 737288 | tf_op jit(solution)/shard_map/ppermute | solution.py:26
  244.6 3.6 %collective-permute-done.5 = bf16[8,40,384]{2,1,0:T(8,128)(2,1)S(1)} collective-permute-done((bf16[8,40,384]{2,1,0:T(8,128)(2,1)S(1)}, bf16[8,40,384]{2,1,0:T(8,128)(2,1)S(1)}, u32[]{:S(2)}, u32[]{:S(2)}) %collective-permute-start.5) | collective-permute-done | bytes 245792 | tf_op jit(solution)/shard_map/ppermute | solution.py:26
  248.3 7.3 %collective-permute-start.6 = (bf16[16,40,384]{2,1,0:T(8,128)(2,1)S(1)}, bf16[16,40,384]{2,1,0:T(8,128)(2,1)S(1)}, u32[]{:S(2)}, u32[]{:S(2)}) collective-permute-start(bf16[16,40,384]{2,1,0:T(8,128)(2,1)S(1)} %pad_maximum_fusion.1), channel_id=1, source_target_pairs={{0,16},{16,0},{1,17},{17,1},{2,18},{18,2},{3,19},{19,3},{4,20},{20... | collective-permute-start | bytes 1474568 | tf_op jit(solution)/shard_map/ppermute | solution.py:26
  258.4 3.5 %all-to-all-start.8 = ((bf16[16,40,256]{2,1,0:T(8,128)(2,1)}), bf16[16,40,256]{2,1,0:T(8,128)(2,1)S(1)}, u32[]{:S(2)}, u32[]{:S(2)}) async-start(bf16[16,40,256]{2,1,0:T(8,128)(2,1)} %bitcast.24), calls=%async_computation.8 | async-start | bytes 655360 | tf_op jit(solution)/shard_map/all_to_all | solution.py:159
  262.6 7.5 %all-to-all-done.8 = bf16[16,40,256]{2,1,0:T(8,128)(2,1)S(1)} async-done(((bf16[16,40,256]{2,1,0:T(8,128)(2,1)}), bf16[16,40,256]{2,1,0:T(8,128)(2,1)S(1)}, u32[]{:S(2)}, u32[]{:S(2)}) %all-to-all-start.8) | async-done | bytes 327712 | tf_op jit(solution)/shard_map/all_to_all | solution.py:159
  (99 shorter events, 19.6 us)
Async XLA Ops:
  0.6 79.7 %copy-start = (bf16[512,544]{0,1:T(8,128)(2,1)S(1)}, bf16[512,544]{0,1:T(8,128)(2,1)}, u32[]{:S(2)}) copy-start(bf16[512,544]{0,1:T(8,128)(2,1)} %param.25) | copy-start | bytes 1671172
  0.7 17.3 %copy-start.16 = (f32[256]{0:T(256)S(1)}, f32[256]{0:T(256)}, u32[]{:S(2)}) copy-start(f32[256]{0:T(256)} %param.19) | copy-start | bytes 3076
  2.3 15.7 %all-to-all-start = ((bf16[16,48,256]{2,1,0:T(8,128)(2,1)}), bf16[16,48,256]{2,1,0:T(8,128)(2,1)S(1)}, u32[]{:S(2)}, u32[]{:S(2)}) async-start(bf16[16,48,256]{2,1,0:T(8,128)(2,1)} %broadcast_in_dim.102), calls=%async_computation | async-start | bytes 786432 | tf_op jit(solution)/shard_map/all_to_all | solution.py:22
  19.2 7.6 %collective-permute-start = (bf16[32,24,512]{2,1,0:T(8,128)(2,1)S(1)}, bf16[32,24,512]{2,1,0:T(8,128)(2,1)S(1)}, u32[]{:S(2)}, u32[]{:S(2)}) collective-permute-start(bf16[32,24,512]{2,1,0:T(8,128)(2,1)S(1)} %get-tuple-element.28), channel_id=1, source_target_pairs={{0,16},{16,0},{1,17},{17,1},{2,18},{18,2},{3,19},{19,3},{4,20},{20... | collective-permute-start | bytes 2359304 | tf_op jit(solution)/shard_map/ppermute | solution.py:26
  26.9 12.2 %collective-permute-start.1 = (bf16[16,24,512]{2,1,0:T(8,128)(2,1)S(1)}, bf16[16,24,512]{2,1,0:T(8,128)(2,1)S(1)}, u32[]{:S(2)}, u32[]{:S(2)}) collective-permute-start(bf16[16,24,512]{2,1,0:T(8,128)(2,1)S(1)} %add_convert_fusion.4), channel_id=1, source_target_pairs={{0,32},{32,0},{1,33},{33,1},{2,34},{34,2},{3,35},{35,3},{4,36},{36... | collective-permute-start | bytes 1179656 | tf_op jit(solution)/shard_map/ppermute | solution.py:26
  39.3 41.0 %copy-start.6 = (bf16[3,20,512]{2,1,0:T(8,128)(2,1)S(1)}, bf16[3,20,512]{2,1,0:T(8,128)(2,1)}, u32[]{:S(2)}) copy-start(bf16[3,20,512]{2,1,0:T(8,128)(2,1)} %param.22) | copy-start | bytes 184324
  39.3 41.0 %copy-start.13 = (f32[4,512]{1,0:T(4,128)S(1)}, f32[4,512]{1,0:T(4,128)}, u32[]{:S(2)}) copy-start(f32[4,512]{1,0:T(4,128)} %param.23) | copy-start | bytes 24580
  39.3 41.0 %copy-start.12 = (f32[512]{0:T(512)S(1)}, f32[512]{0:T(512)}, u32[]{:S(2)}) copy-start(f32[512]{0:T(512)} %param.24) | copy-start | bytes 6148
  80.6 13.6 %copy-start.2 = (bf16[512,512]{1,0:T(8,128)(2,1)S(1)}, bf16[512,512]{1,0:T(8,128)(2,1)}, u32[]{:S(2)}) copy-start(bf16[512,512]{1,0:T(8,128)(2,1)} %param.26) | copy-start | bytes 1572868
  80.6 13.6 %copy-start.14 = (f32[512]{0:T(512)S(1)}, f32[512]{0:T(512)}, u32[]{:S(2)}) copy-start(f32[512]{0:T(512)} %param.27) | copy-start | bytes 6148
  81.5 13.1 %copy-start.1 = (f32[20,16,512]{2,1,0:T(8,128)S(1)}, f32[20,16,512]{2,1,0:T(8,128)}, u32[]{:S(2)}) copy-start(f32[20,16,512]{2,1,0:T(8,128)} %param.29) | copy-start | bytes 1966084
  81.5 12.4 %all-to-all-start.2 = ((bf16[16,20,544]{2,1,0:T(8,128)(2,1)}), bf16[16,20,544]{2,1,0:T(8,128)(2,1)S(1)}, u32[]{:S(2)}, u32[]{:S(2)}) async-start(bf16[16,20,544]{2,1,0:T(8,128)(2,1)} %broadcast_in_dim.106), calls=%async_computation.2 | async-start | bytes 983040 | tf_op jit(solution)/shard_map/all_to_all | solution.py:22
  116.7 10.8 %collective-permute-start.2 = (bf16[16,20,512]{2,1,0:T(8,128)(2,1)S(1)}, bf16[16,20,512]{2,1,0:T(8,128)(2,1)S(1)}, u32[]{:S(2)}, u32[]{:S(2)}) collective-permute-start(bf16[16,20,512]{2,1,0:T(8,128)(2,1)S(1)} %reshape.133), channel_id=1, source_target_pairs={{0,16},{16,0},{1,17},{17,1},{2,18},{18,2},{3,19},{19,3},{4,20},{20... | collective-permute-start | bytes 983048 | tf_op jit(solution)/shard_map/ppermute | solution.py:26
  127.6 12.1 %copy-start.10 = (bf16[40,256]{1,0:T(8,128)(2,1)S(1)}, bf16[40,256]{1,0:T(8,128)(2,1)}, u32[]{:S(2)}) copy-start(bf16[40,256]{1,0:T(8,128)(2,1)} %param.18) | copy-start | bytes 61444
  128.0 16.3 %copy-start.4 = (bf16[256,768]{1,0:T(8,128)(2,1)S(1)}, bf16[256,768]{1,0:T(8,128)(2,1)}, u32[]{:S(2)}) copy-start(bf16[256,768]{1,0:T(8,128)(2,1)} %param.34) | copy-start | bytes 1179652
  128.0 16.3 %copy-start.5 = (bf16[256,768]{1,0:T(8,128)(2,1)S(1)}, bf16[256,768]{1,0:T(8,128)(2,1)}, u32[]{:S(2)}) copy-start(bf16[256,768]{1,0:T(8,128)(2,1)} %param.33) | copy-start | bytes 1179652
  140.6 11.7 %copy-start.17 = (f32[256]{0:T(256)S(1)}, f32[256]{0:T(256)}, u32[]{:S(2)}) copy-start(f32[256]{0:T(256)} %param.32) | copy-start | bytes 3076
  140.6 11.7 %all-to-all-start.5 = ((bf16[16,48,256]{2,1,0:T(8,128)(2,1)}), bf16[16,48,256]{2,1,0:T(8,128)(2,1)S(1)}, u32[]{:S(2)}, u32[]{:S(2)}) async-start(bf16[16,48,256]{2,1,0:T(8,128)(2,1)} %broadcast_in_dim.110), calls=%async_computation.5 | async-start | bytes 786432 | tf_op jit(solution)/shard_map/all_to_all | solution.py:22
  153.7 7.2 %collective-permute-start.3 = (bf16[16,48,768]{2,1,0:T(8,128)(2,1)S(1)}, bf16[16,48,768]{2,1,0:T(8,128)(2,1)}, u32[]{:S(2)}, u32[]{:S(2)}) collective-permute-start(bf16[16,48,768]{2,1,0:T(8,128)(2,1)S(1)} %get-tuple-element.30), channel_id=1, source_target_pairs={{0,16},{16,0},{1,17},{17,1},{2,18},{18,2},{3,19},{19,3},{4,20},{20... | collective-permute-start | bytes 3538952 | tf_op jit(solution)/shard_map/ppermute | solution.py:26
  162.1 16.4 %collective-permute-start.4 = (bf16[8,48,768]{2,1,0:T(8,128)(2,1)S(1)}, bf16[8,48,768]{2,1,0:T(8,128)(2,1)S(1)}, u32[]{:S(2)}, u32[]{:S(2)}) collective-permute-start(bf16[8,48,768]{2,1,0:T(8,128)(2,1)S(1)} %add_convert_fusion.1), channel_id=1, source_target_pairs={{0,32},{32,0},{1,33},{33,1},{2,34},{34,2},{3,35},{35,3},{4,36},{36... | collective-permute-start | bytes 1769480 | tf_op jit(solution)/shard_map/ppermute | solution.py:26
  211.9 45.2 %copy-start.3 = (bf16[768,256]{1,0:T(8,128)(2,1)S(1)}, bf16[768,256]{1,0:T(8,128)(2,1)}, u32[]{:S(2)}) copy-start(bf16[768,256]{1,0:T(8,128)(2,1)} %param.35) | copy-start | bytes 1179652
  239.6 8.5 %collective-permute-start.5 = (bf16[8,40,384]{2,1,0:T(8,128)(2,1)S(1)}, bf16[8,40,384]{2,1,0:T(8,128)(2,1)S(1)}, u32[]{:S(2)}, u32[]{:S(2)}) collective-permute-start(bf16[8,40,384]{2,1,0:T(8,128)(2,1)S(1)} %all_to_all.49), channel_id=1, source_target_pairs={{0,32},{32,0},{1,33},{33,1},{2,34},{34,2},{3,35},{35,3},{4,36},{36... | collective-permute-start | bytes 737288 | tf_op jit(solution)/shard_map/ppermute | solution.py:26
  248.3 8.8 %collective-permute-start.6 = (bf16[16,40,384]{2,1,0:T(8,128)(2,1)S(1)}, bf16[16,40,384]{2,1,0:T(8,128)(2,1)S(1)}, u32[]{:S(2)}, u32[]{:S(2)}) collective-permute-start(bf16[16,40,384]{2,1,0:T(8,128)(2,1)S(1)} %pad_maximum_fusion.1), channel_id=1, source_target_pairs={{0,16},{16,0},{1,17},{17,1},{2,18},{18,2},{3,19},{19,3},{4,20},{20... | collective-permute-start | bytes 1474568 | tf_op jit(solution)/shard_map/ppermute | solution.py:26
  258.4 11.7 %all-to-all-start.8 = ((bf16[16,40,256]{2,1,0:T(8,128)(2,1)}), bf16[16,40,256]{2,1,0:T(8,128)(2,1)S(1)}, u32[]{:S(2)}, u32[]{:S(2)}) async-start(bf16[16,40,256]{2,1,0:T(8,128)(2,1)} %bitcast.24), calls=%async_computation.8 | async-start | bytes 655360 | tf_op jit(solution)/shard_map/all_to_all | solution.py:159
  (5 other events, 26.6 us)

commit v3 on v2

--- a/solution.py
+++ b/solution.py
@@ -26,6 +26,15 @@
     return lax.ppermute(block, axis, [(0, 1), (1, 0)])
 
 
+def swap_pairs(block):
+    moves = []
+    for z in range(16):
+        step = 1 if z % 2 == 0 else -1
+        moves.append((2 * z, 2 * (z + step)))
+        moves.append((2 * z + 1, 2 * ((z - step) % 16) + 1))
+    return lax.ppermute(block, RING + ("c",), moves)
+
+
 def dot(left, right):
     return jnp.dot(left, right, preferred_element_type=F32)
 
@@ -47,7 +56,12 @@
 def reduce_rows(block, size, gain, left_weight, right_weight, axes):
     core, pair = lax.axis_index("c"), lax.axis_index("zp")
     groups, padded, depth = block.shape
-    wide = spread(block.reshape(groups * padded, depth), TENSOR_PAIRS, 16).astype(F32)
+    rows = spread(block.reshape(groups * padded, depth), TENSOR_PAIRS, 16)
+    low, high = rows[:8], rows[8:]
+    rows = jnp.concatenate(
+        [jnp.where(pair == 0, high, low), jnp.where(pair == 0, low, high)], axis=0
+    )
+    wide = rows.astype(F32)
     scaled = (wide * gain[None, None, :]).astype(BF16).reshape(16 * groups * padded, depth)
     squares = jnp.sum(wide * wide, axis=2).reshape(16 * groups, 1, padded)
     half = left_weight.shape[1] // 2
@@ -64,10 +78,8 @@
         )
 
     received = swap(partial(1 - core), "c")
-    own = partial(core)
-    sent = add(half_rows(own, 1 - pair), half_rows(received, 1 - pair))
-    kept = add(half_rows(own, pair), half_rows(received, pair))
-    total = add(kept, swap(sent, "zp"))
+    both = add(partial(core), received)
+    total = add(both[8 * groups :], swap_pairs(both[: 8 * groups]))
     far = lax.all_to_all(total, axes, 0, 0).astype(F32)
     return jnp.sum(far.reshape(8, groups, padded, columns), axis=0)
 
@@ -145,7 +157,7 @@
     both = sums[:token_rows] * scale
     active = (jax.nn.silu(both[:, :hidden]) * both[:, hidden:]).astype(BF16)
     near = spread(active, PAIRS, 8)
-    next_to = swap(near, "zp")
+    next_to = swap_pairs(near)
     same = jnp.concatenate(
         [jnp.where(pair == 0, near, next_to), jnp.where(pair == 0, next_to, near)], axis=0
     )

time: 272 us -> 261 us (0.960)
  waiting for transfers between devices: 66.8 us -> 57.1 us
  starting transfers between devices: 55.3 us -> 62.6 us
  blocking collectives: 133 us -> 126 us
    ppermute x7 -> x4, waiting for transfers between devices: 34.6 us -> 6.27 us  [swap(): return lax.ppermute(block, axis, [(0, 1), (1, 0)])]
    ppermute x0 -> x3, waiting for transfers between devices: none -> 18.6 us  [swap_pairs(): return lax.ppermute(block, RING + ('c',), moves)]
    ppermute x0 -> x3, starting transfers between devices: none -> 17.6 us  [swap_pairs(): return lax.ppermute(block, RING + ('c',), moves)]
    ppermute x7 -> x4, starting transfers between devices: 36.8 us -> 26.6 us  [swap(): return lax.ppermute(block, axis, [(0, 1), (1, 0)])]
    all_to_all x2, blocking collectives: 48.3 us -> 43.6 us  [spread(): lax.all_to_all(jnp.broadcast_to(block[None], (count,) + block.shape), axe...]
  transfers between devices with their start and end apart: 11 -> 11, of which waited for: 11 -> 11; matrix products, arithmetic and copies ran while one was open for 0% -> 1% of each run, Pallas kernels for 0% -> 0%
where the time goes in v3:
time: 261 us; the launch traced here: 260 us
  blocking collectives  126 us (48%)
  starting transfers between devices  62.6 us (24%)
  waiting for transfers between devices  57.1 us (22%)
  other arithmetic  5.62 us (2%)
  local copies, waits for them, and re-layouts  4.1 us (2%)
  matrix products  3.9 us (1%)
    all_to_all x2, blocking collectives, reduce_rows(): far = lax.all_to_all(total, axes, 0, 0).astype(F32)  70.3 us
    all_to_all x2, blocking collectives, spread(): lax.all_to_all(jnp.broadcast_to(block[None], (count,) + block.shape), axe...  43.6 us
    ppermute x4, starting transfers between devices, swap(): return lax.ppermute(block, axis, [(0, 1), (1, 0)])  26.6 us
    all_to_all x3, waiting for transfers between devices, spread(): lax.all_to_all(jnp.broadcast_to(block[None], (count,) + block.shape), axe...  24.6 us
    ppermute x3, waiting for transfers between devices, swap_pairs(): return lax.ppermute(block, RING + ('c',), moves)  18.6 us
    ppermute x3, starting transfers between devices, swap_pairs(): return lax.ppermute(block, RING + ('c',), moves)  17.6 us
    all_to_all x3, starting transfers between devices, spread(): lax.all_to_all(jnp.broadcast_to(block[None], (count,) + block.shape), axe...  14.8 us
    all_to_all x1, blocking collectives, on_device(): lax.all_to_all(out_terms.reshape(16, token_rows, token_cols), TENSOR, 0, 0)  11.7 us
  transfers between devices with their start and end apart: 11, of which 11 were waited for; matrix products, arithmetic and copies ran while one was open for 1% of the time, Pallas kernels for 0%

profile of v3, /device:TPU:1, one launch (start us, length us, event | category | flops | bytes accessed | tf_op | source)
XLA Modules:
  0.0 260.2 jit_solution(8939620209159478561)
XLA Ops:
  2.3 7.6 %all-to-all-start = ((bf16[16,48,256]{2,1,0:T(8,128)(2,1)}), bf16[16,48,256]{2,1,0:T(8,128)(2,1)S(1)}, u32[]{:S(2)}, u32[]{:S(2)}) async-start(bf16[16,48,256]{2,1,0:T(8,128)(2,1)} %broadcast_in_dim.102), calls=%async_computation | async-start | bytes 786432 | tf_op jit(solution)/shard_map/all_to_all | solution.py:22
  10.0 8.0 %all-to-all-done = bf16[16,48,256]{2,1,0:T(8,128)(2,1)S(1)} async-done(((bf16[16,48,256]{2,1,0:T(8,128)(2,1)}), bf16[16,48,256]{2,1,0:T(8,128)(2,1)S(1)}, u32[]{:S(2)}, u32[]{:S(2)}) %all-to-all-start) | async-done | bytes 393248 | tf_op jit(solution)/shard_map/all_to_all | solution.py:22
  18.9 5.7 %collective-permute-start = (bf16[32,24,512]{2,1,0:T(8,128)(2,1)S(1)}, bf16[32,24,512]{2,1,0:T(8,128)(2,1)S(1)}, u32[]{:S(2)}, u32[]{:S(2)}) collective-permute-start(bf16[32,24,512]{2,1,0:T(8,128)(2,1)S(1)} %broadcast_select_fusion.1), channel_id=1, source_target_pairs={{0,16},{16,0},{1,17},{17,1},{2,18},{18,2},{3,19},{19,3},{4,20},{20... | collective-permute-start | bytes 2359304 | tf_op jit(solution)/shard_map/ppermute | solution.py:26
  27.1 10.1 %collective-permute-start.1 = (bf16[16,24,512]{2,1,0:T(8,128)(2,1)S(1)}, bf16[16,24,512]{2,1,0:T(8,128)(2,1)S(1)}, u32[]{:S(2)}, u32[]{:S(2)}) collective-permute-start(bf16[16,24,512]{2,1,0:T(8,128)(2,1)S(1)} %slice.95), channel_id=1, source_target_pairs={{0,32},{16,496},{32,0},{48,80},{64,96},{80,48},{96,64},{112,144},{... | collective-permute-start | bytes 1179656 | tf_op jit(solution)/shard_map/ppermute | solution.py:35
  37.2 5.2 %collective-permute-done.1 = bf16[16,24,512]{2,1,0:T(8,128)(2,1)S(1)} collective-permute-done((bf16[16,24,512]{2,1,0:T(8,128)(2,1)S(1)}, bf16[16,24,512]{2,1,0:T(8,128)(2,1)S(1)}, u32[]{:S(2)}, u32[]{:S(2)}) %collective-permute-start.1) | collective-permute-done | bytes 393248 | tf_op jit(solution)/shard_map/ppermute | solution.py:35
  42.5 34.3 %all_to_all.45 = bf16[16,24,512]{2,1,0:T(8,128)(2,1)S(1)} all-to-all(bf16[16,24,512]{2,1,0:T(8,128)(2,1)S(1)} %add_convert_fusion.3), channel_id=1, replica_groups=mesh['zh'=4,'zm'=2,'zp'=2,'c'=2,'y'=4,'xm'=2,'xp'=2] {'zh','zm','c'}, dimensions={0} | all-to-all | bytes 786432 | tf_op jit(solution)/shard_map/all_to_all | solution.py:83
  78.2 3.7 %all-to-all-start.2 = ((bf16[16,20,544]{2,1,0:T(8,128)(2,1)}), bf16[16,20,544]{2,1,0:T(8,128)(2,1)S(1)}, u32[]{:S(2)}, u32[]{:S(2)}) async-start(bf16[16,20,544]{2,1,0:T(8,128)(2,1)} %broadcast_in_dim.106), calls=%async_computation.2 | async-start | bytes 983040 | tf_op jit(solution)/shard_map/all_to_all | solution.py:22
  81.9 8.7 %all-to-all-done.2 = bf16[16,20,544]{2,1,0:T(8,128)(2,1)S(1)} async-done(((bf16[16,20,544]{2,1,0:T(8,128)(2,1)}), bf16[16,20,544]{2,1,0:T(8,128)(2,1)S(1)}, u32[]{:S(2)}, u32[]{:S(2)}) %all-to-all-start.2) | async-done | bytes 348192 | tf_op jit(solution)/shard_map/all_to_all | solution.py:22
  92.5 20.5 %all_to_all.46 = bf16[16,16,640]{2,1,0:T(8,128)(2,1)S(1)} all-to-all(bf16[16,16,640]{2,1,0:T(8,128)(2,1)S(1)} %broadcast_in_dim.108), channel_id=1, replica_groups=mesh['zh'=4,'zm'=2,'zp'=2,'c'=2,'y'=4,'xm'=2,'xp'=2] {'zh','zm','zp'}, dimensions={0} | all-to-all | bytes 655360 | tf_op jit(solution)/shard_map/all_to_all | solution.py:22
  113.4 9.4 %collective-permute-start.2 = (bf16[16,20,512]{2,1,0:T(8,128)(2,1)S(1)}, bf16[16,20,512]{2,1,0:T(8,128)(2,1)S(1)}, u32[]{:S(2)}, u32[]{:S(2)}) collective-permute-start(bf16[16,20,512]{2,1,0:T(8,128)(2,1)S(1)} %reshape.134), channel_id=1, source_target_pairs={{0,16},{16,0},{1,17},{17,1},{2,18},{18,2},{3,19},{19,3},{4,20},{20... | collective-permute-start | bytes 983048 | tf_op jit(solution)/shard_map/ppermute | solution.py:26
  124.7 11.7 %all_to_all.47 = bf16[16,40,256]{2,1,0:T(8,128)(2,1)S(1)} all-to-all(bf16[16,40,256]{2,1,0:T(8,128)(2,1)S(1)} %bitcast.63), channel_id=1, replica_groups=mesh['zh'=4,'zm'=2,'zp'=2,'c'=2,'y'=4,'xm'=2,'xp'=2] {'y','xm','xp'}, dimensions={0} | all-to-all | bytes 655360 | tf_op jit(solution)/shard_map/all_to_all | solution.py:148
  137.2 3.6 %all-to-all-start.5 = ((bf16[16,48,256]{2,1,0:T(8,128)(2,1)}), bf16[16,48,256]{2,1,0:T(8,128)(2,1)S(1)}, u32[]{:S(2)}, u32[]{:S(2)}) async-start(bf16[16,48,256]{2,1,0:T(8,128)(2,1)} %broadcast_in_dim.110), calls=%async_computation.5 | async-start | bytes 786432 | tf_op jit(solution)/shard_map/all_to_all | solution.py:22
  140.9 7.9 %all-to-all-done.5 = bf16[16,48,256]{2,1,0:T(8,128)(2,1)S(1)} async-done(((bf16[16,48,256]{2,1,0:T(8,128)(2,1)}), bf16[16,48,256]{2,1,0:T(8,128)(2,1)S(1)}, u32[]{:S(2)}, u32[]{:S(2)}) %all-to-all-start.5) | async-done | bytes 393248 | tf_op jit(solution)/shard_map/all_to_all | solution.py:22
  149.8 4.6 %collective-permute-start.3 = (bf16[16,48,768]{2,1,0:T(8,128)(2,1)S(1)}, bf16[16,48,768]{2,1,0:T(8,128)(2,1)S(1)}, u32[]{:S(2)}, u32[]{:S(2)}) collective-permute-start(bf16[16,48,768]{2,1,0:T(8,128)(2,1)S(1)} %broadcast_select_fusion), channel_id=1, source_target_pairs={{0,16},{16,0},{1,17},{17,1},{2,18},{18,2},{3,19},{19,3},{4,20},{20... | collective-permute-start | bytes 3538952 | tf_op jit(solution)/shard_map/ppermute | solution.py:26
  154.9 2.0 collective-permute-done.3
  157.4 5.5 %collective-permute-start.4 = (bf16[8,48,768]{2,1,0:T(8,128)(2,1)S(1)}, bf16[8,48,768]{2,1,0:T(8,128)(2,1)S(1)}, u32[]{:S(2)}, u32[]{:S(2)}) collective-permute-start(bf16[8,48,768]{2,1,0:T(8,128)(2,1)S(1)} %slice.108), channel_id=1, source_target_pairs={{0,32},{16,496},{32,0},{48,80},{64,96},{80,48},{96,64},{112,144},{... | collective-permute-start | bytes 1769480 | tf_op jit(solution)/shard_map/ppermute | solution.py:35
  162.9 7.3 %collective-permute-done.4 = bf16[8,48,768]{2,1,0:T(8,128)(2,1)S(1)} collective-permute-done((bf16[8,48,768]{2,1,0:T(8,128)(2,1)S(1)}, bf16[8,48,768]{2,1,0:T(8,128)(2,1)S(1)}, u32[]{:S(2)}, u32[]{:S(2)}) %collective-permute-start.4) | collective-permute-done | bytes 589856 | tf_op jit(solution)/shard_map/ppermute | solution.py:35
  170.3 36.0 %all_to_all.48 = bf16[8,48,768]{2,1,0:T(8,128)(2,1)S(1)} all-to-all(bf16[8,48,768]{2,1,0:T(8,128)(2,1)S(1)} %add_convert_fusion.2), channel_id=1, replica_groups=mesh['zh'=4,'zm'=2,'zp'=2,'c'=2,'y'=4,'xm'=2,'xp'=2] {'zh','zm'}, dimensions={0} | all-to-all | bytes 1179648 | tf_op jit(solution)/shard_map/all_to_all | solution.py:83
  206.6 23.1 %all_to_all.49 = bf16[8,40,384]{2,1,0:T(8,128)(2,1)S(1)} all-to-all(bf16[8,40,384]{2,1,0:T(8,128)(2,1)S(1)} %broadcast_in_dim.113), channel_id=1, replica_groups=mesh['zh'=4,'zm'=2,'zp'=2,'c'=2,'y'=4,'xm'=2,'xp'=2] {'zh','zm'}, dimensions={0} | all-to-all | bytes 491520 | tf_op jit(solution)/shard_map/all_to_all | solution.py:22
  229.7 1.9 collective-permute-start.5
  231.6 6.2 %collective-permute-done.5 = bf16[8,40,384]{2,1,0:T(8,128)(2,1)S(1)} collective-permute-done((bf16[8,40,384]{2,1,0:T(8,128)(2,1)S(1)}, bf16[8,40,384]{2,1,0:T(8,128)(2,1)S(1)}, u32[]{:S(2)}, u32[]{:S(2)}) %collective-permute-start.5) | collective-permute-done | bytes 245792 | tf_op jit(solution)/shard_map/ppermute | solution.py:35
  237.9 6.9 %collective-permute-start.6 = (bf16[16,40,384]{2,1,0:T(8,128)(2,1)S(1)}, bf16[16,40,384]{2,1,0:T(8,128)(2,1)S(1)}, u32[]{:S(2)}, u32[]{:S(2)}) collective-permute-start(bf16[16,40,384]{2,1,0:T(8,128)(2,1)S(1)} %pad_maximum_fusion.1), channel_id=1, source_target_pairs={{0,16},{16,0},{1,17},{17,1},{2,18},{18,2},{3,19},{19,3},{4,20},{20... | collective-permute-start | bytes 1474568 | tf_op jit(solution)/shard_map/ppermute | solution.py:26
  247.7 3.5 %all-to-all-start.8 = ((bf16[16,40,256]{2,1,0:T(8,128)(2,1)}), bf16[16,40,256]{2,1,0:T(8,128)(2,1)S(1)}, u32[]{:S(2)}, u32[]{:S(2)}) async-start(bf16[16,40,256]{2,1,0:T(8,128)(2,1)} %bitcast.24), calls=%async_computation.8 | async-start | bytes 655360 | tf_op jit(solution)/shard_map/all_to_all | solution.py:171
  251.9 7.6 %all-to-all-done.8 = bf16[16,40,256]{2,1,0:T(8,128)(2,1)S(1)} async-done(((bf16[16,40,256]{2,1,0:T(8,128)(2,1)}), bf16[16,40,256]{2,1,0:T(8,128)(2,1)S(1)}, u32[]{:S(2)}, u32[]{:S(2)}) %all-to-all-start.8) | async-done | bytes 327712 | tf_op jit(solution)/shard_map/all_to_all | solution.py:171
  (107 shorter events, 17.9 us)
Async XLA Ops:
  0.6 76.4 %copy-start = (bf16[512,544]{0,1:T(8,128)(2,1)S(1)}, bf16[512,544]{0,1:T(8,128)(2,1)}, u32[]{:S(2)}) copy-start(bf16[512,544]{0,1:T(8,128)(2,1)} %param.25) | copy-start | bytes 1671172
  0.6 9.2 %copy-start.8 = (bf16[256,512]{1,0:T(8,128)(2,1)S(1)}, bf16[256,512]{1,0:T(8,128)(2,1)}, u32[]{:S(2)}) copy-start(bf16[256,512]{1,0:T(8,128)(2,1)} %param.20) | copy-start | bytes 786436
  0.7 9.2 %copy-start.7 = (bf16[256,512]{1,0:T(8,128)(2,1)S(1)}, bf16[256,512]{1,0:T(8,128)(2,1)}, u32[]{:S(2)}) copy-start(bf16[256,512]{1,0:T(8,128)(2,1)} %param.21) | copy-start | bytes 786436
  2.3 15.7 %all-to-all-start = ((bf16[16,48,256]{2,1,0:T(8,128)(2,1)}), bf16[16,48,256]{2,1,0:T(8,128)(2,1)S(1)}, u32[]{:S(2)}, u32[]{:S(2)}) async-start(bf16[16,48,256]{2,1,0:T(8,128)(2,1)} %broadcast_in_dim.102), calls=%async_computation | async-start | bytes 786432 | tf_op jit(solution)/shard_map/all_to_all | solution.py:22
  18.9 7.6 %collective-permute-start = (bf16[32,24,512]{2,1,0:T(8,128)(2,1)S(1)}, bf16[32,24,512]{2,1,0:T(8,128)(2,1)S(1)}, u32[]{:S(2)}, u32[]{:S(2)}) collective-permute-start(bf16[32,24,512]{2,1,0:T(8,128)(2,1)S(1)} %broadcast_select_fusion.1), channel_id=1, source_target_pairs={{0,16},{16,0},{1,17},{17,1},{2,18},{18,2},{3,19},{19,3},{4,20},{20... | collective-permute-start | bytes 2359304 | tf_op jit(solution)/shard_map/ppermute | solution.py:26
  27.0 50.0 %copy-start.6 = (bf16[3,20,512]{2,1,0:T(8,128)(2,1)S(1)}, bf16[3,20,512]{2,1,0:T(8,128)(2,1)}, u32[]{:S(2)}) copy-start(bf16[3,20,512]{2,1,0:T(8,128)(2,1)} %param.22) | copy-start | bytes 184324
  27.0 50.0 %copy-start.13 = (f32[4,512]{1,0:T(4,128)S(1)}, f32[4,512]{1,0:T(4,128)}, u32[]{:S(2)}) copy-start(f32[4,512]{1,0:T(4,128)} %param.23) | copy-start | bytes 24580
  27.1 50.0 %copy-start.12 = (f32[512]{0:T(512)S(1)}, f32[512]{0:T(512)}, u32[]{:S(2)}) copy-start(f32[512]{0:T(512)} %param.24) | copy-start | bytes 6148
  27.1 15.3 %collective-permute-start.1 = (bf16[16,24,512]{2,1,0:T(8,128)(2,1)S(1)}, bf16[16,24,512]{2,1,0:T(8,128)(2,1)S(1)}, u32[]{:S(2)}, u32[]{:S(2)}) collective-permute-start(bf16[16,24,512]{2,1,0:T(8,128)(2,1)S(1)} %slice.95), channel_id=1, source_target_pairs={{0,32},{16,496},{32,0},{48,80},{64,96},{80,48},{96,64},{112,144},{... | collective-permute-start | bytes 1179656 | tf_op jit(solution)/shard_map/ppermute | solution.py:35
  77.3 13.6 %copy-start.2 = (bf16[512,512]{1,0:T(8,128)(2,1)S(1)}, bf16[512,512]{1,0:T(8,128)(2,1)}, u32[]{:S(2)}) copy-start(bf16[512,512]{1,0:T(8,128)(2,1)} %param.26) | copy-start | bytes 1572868
  77.3 13.6 %copy-start.14 = (f32[512]{0:T(512)S(1)}, f32[512]{0:T(512)}, u32[]{:S(2)}) copy-start(f32[512]{0:T(512)} %param.27) | copy-start | bytes 6148
  78.2 13.1 %copy-start.1 = (f32[20,16,512]{2,1,0:T(8,128)S(1)}, f32[20,16,512]{2,1,0:T(8,128)}, u32[]{:S(2)}) copy-start(f32[20,16,512]{2,1,0:T(8,128)} %param.29) | copy-start | bytes 1966084
  78.2 12.4 %all-to-all-start.2 = ((bf16[16,20,544]{2,1,0:T(8,128)(2,1)}), bf16[16,20,544]{2,1,0:T(8,128)(2,1)S(1)}, u32[]{:S(2)}, u32[]{:S(2)}) async-start(bf16[16,20,544]{2,1,0:T(8,128)(2,1)} %broadcast_in_dim.106), calls=%async_computation.2 | async-start | bytes 983040 | tf_op jit(solution)/shard_map/all_to_all | solution.py:22
  113.4 10.7 %collective-permute-start.2 = (bf16[16,20,512]{2,1,0:T(8,128)(2,1)S(1)}, bf16[16,20,512]{2,1,0:T(8,128)(2,1)S(1)}, u32[]{:S(2)}, u32[]{:S(2)}) collective-permute-start(bf16[16,20,512]{2,1,0:T(8,128)(2,1)S(1)} %reshape.134), channel_id=1, source_target_pairs={{0,16},{16,0},{1,17},{17,1},{2,18},{18,2},{3,19},{19,3},{4,20},{20... | collective-permute-start | bytes 983048 | tf_op jit(solution)/shard_map/ppermute | solution.py:26
  124.3 12.1 %copy-start.10 = (bf16[40,256]{1,0:T(8,128)(2,1)S(1)}, bf16[40,256]{1,0:T(8,128)(2,1)}, u32[]{:S(2)}) copy-start(bf16[40,256]{1,0:T(8,128)(2,1)} %param.18) | copy-start | bytes 61444
  124.7 16.1 %copy-start.4 = (bf16[256,768]{1,0:T(8,128)(2,1)S(1)}, bf16[256,768]{1,0:T(8,128)(2,1)}, u32[]{:S(2)}) copy-start(bf16[256,768]{1,0:T(8,128)(2,1)} %param.34) | copy-start | bytes 1179652
  124.7 16.1 %copy-start.5 = (bf16[256,768]{1,0:T(8,128)(2,1)S(1)}, bf16[256,768]{1,0:T(8,128)(2,1)}, u32[]{:S(2)}) copy-start(bf16[256,768]{1,0:T(8,128)(2,1)} %param.33) | copy-start | bytes 1179652
  137.2 11.6 %all-to-all-start.5 = ((bf16[16,48,256]{2,1,0:T(8,128)(2,1)}), bf16[16,48,256]{2,1,0:T(8,128)(2,1)S(1)}, u32[]{:S(2)}, u32[]{:S(2)}) async-start(bf16[16,48,256]{2,1,0:T(8,128)(2,1)} %broadcast_in_dim.110), calls=%async_computation.5 | async-start | bytes 786432 | tf_op jit(solution)/shard_map/all_to_all | solution.py:22
  149.8 7.0 %collective-permute-start.3 = (bf16[16,48,768]{2,1,0:T(8,128)(2,1)S(1)}, bf16[16,48,768]{2,1,0:T(8,128)(2,1)S(1)}, u32[]{:S(2)}, u32[]{:S(2)}) collective-permute-start(bf16[16,48,768]{2,1,0:T(8,128)(2,1)S(1)} %broadcast_select_fusion), channel_id=1, source_target_pairs={{0,16},{16,0},{1,17},{17,1},{2,18},{18,2},{3,19},{19,3},{4,20},{20... | collective-permute-start | bytes 3538952 | tf_op jit(solution)/shard_map/ppermute | solution.py:26
  157.4 12.8 %collective-permute-start.4 = (bf16[8,48,768]{2,1,0:T(8,128)(2,1)S(1)}, bf16[8,48,768]{2,1,0:T(8,128)(2,1)S(1)}, u32[]{:S(2)}, u32[]{:S(2)}) collective-permute-start(bf16[8,48,768]{2,1,0:T(8,128)(2,1)S(1)} %slice.108), channel_id=1, source_target_pairs={{0,32},{16,496},{32,0},{48,80},{64,96},{80,48},{96,64},{112,144},{... | collective-permute-start | bytes 1769480 | tf_op jit(solution)/shard_map/ppermute | solution.py:35
  206.6 39.8 %copy-start.3 = (bf16[768,256]{1,0:T(8,128)(2,1)S(1)}, bf16[768,256]{1,0:T(8,128)(2,1)}, u32[]{:S(2)}) copy-start(bf16[768,256]{1,0:T(8,128)(2,1)} %param.35) | copy-start | bytes 1179652
  229.7 8.1 %collective-permute-start.5 = (bf16[8,40,384]{2,1,0:T(8,128)(2,1)S(1)}, bf16[8,40,384]{2,1,0:T(8,128)(2,1)S(1)}, u32[]{:S(2)}, u32[]{:S(2)}) collective-permute-start(bf16[8,40,384]{2,1,0:T(8,128)(2,1)S(1)} %all_to_all.49), channel_id=1, source_target_pairs={{0,32},{16,496},{32,0},{48,80},{64,96},{80,48},{96,64},{112,144},{... | collective-permute-start | bytes 737288 | tf_op jit(solution)/shard_map/ppermute | solution.py:35
  237.9 8.4 %collective-permute-start.6 = (bf16[16,40,384]{2,1,0:T(8,128)(2,1)S(1)}, bf16[16,40,384]{2,1,0:T(8,128)(2,1)S(1)}, u32[]{:S(2)}, u32[]{:S(2)}) collective-permute-start(bf16[16,40,384]{2,1,0:T(8,128)(2,1)S(1)} %pad_maximum_fusion.1), channel_id=1, source_target_pairs={{0,16},{16,0},{1,17},{17,1},{2,18},{18,2},{3,19},{19,3},{4,20},{20... | collective-permute-start | bytes 1474568 | tf_op jit(solution)/shard_map/ppermute | solution.py:26
  247.7 11.8 %all-to-all-start.8 = ((bf16[16,40,256]{2,1,0:T(8,128)(2,1)}), bf16[16,40,256]{2,1,0:T(8,128)(2,1)S(1)}, u32[]{:S(2)}, u32[]{:S(2)}) async-start(bf16[16,40,256]{2,1,0:T(8,128)(2,1)} %bitcast.24), calls=%async_computation.8 | async-start | bytes 655360 | tf_op jit(solution)/shard_map/all_to_all | solution.py:171
  (5 other events, 24.7 us)

commit v4 on v3

--- a/solution.py
+++ b/solution.py
@@ -7,6 +7,7 @@
 WIDTH = 8192
 RANK = 512
 STATE = 16
+TILE = 256
 
 epsilon = 1e-06
 
@@ -82,6 +83,37 @@
     total = add(both[8 * groups :], swap_pairs(both[: 8 * groups]))
     far = lax.all_to_all(total, axes, 0, 0).astype(F32)
     return jnp.sum(far.reshape(8, groups, padded, columns), axis=0)
+
+
+def reduce_wide_rows(block, gain, left_weight, right_weight):
+    core, pair = lax.axis_index("c"), lax.axis_index("zp")
+    size, depth = block.shape
+    rows = spread(block, TENSOR_PAIRS, 16)
+    low, high = rows[:8], rows[8:]
+    rows = jnp.concatenate(
+        [jnp.where(pair == 0, high, low), jnp.where(pair == 0, low, high)], axis=0
+    )
+    wide = rows.astype(F32)
+    scaled = (wide * gain[None, None, :]).astype(BF16).reshape(16 * size, depth)
+    squares = jnp.sum(wide * wide, axis=2).astype(BF16)[:, None, :]
+    marks = jnp.pad(squares, ((0, 0), (0, 7), (0, TILE - size)))
+    tiles = left_weight.shape[1] // TILE
+
+    def partial(which):
+        weight = jnp.concatenate(
+            [half_columns(left_weight, which), half_columns(right_weight, which)], axis=1
+        )
+        terms = dot(scaled, weight).astype(BF16).reshape(16, size, tiles * TILE)
+        return jnp.concatenate(
+            [terms[:, :, TILE * k : TILE * k + TILE] for k in range(tiles)] + [marks], axis=1
+        )
+
+    received = swap(partial(1 - core), "c")
+    both = add(partial(core), received)
+    total = add(both[8:], swap_pairs(both[:8]))
+    sums = jnp.sum(lax.all_to_all(total, PAIRS, 0, 0).astype(F32), axis=0)
+    columns = [sums[size * k : size * k + size] for k in range(tiles)]
+    return jnp.concatenate(columns, axis=1), sums[size * tiles, :size]
 
 
 def on_device(
@@ -150,11 +182,10 @@
     )
     residual = (tokens.astype(F32) + out_own).astype(BF16)
 
-    block = jnp.pad(residual, ((0, 8), (0, 0)))[None]
-    sums = reduce_rows(block, token_rows, post_gain, gate_weight, up_weight, PAIRS)[0]
-    scale = lax.rsqrt(sums[token_rows, :token_rows] / WIDTH + epsilon)[:, None]
+    sums, second = reduce_wide_rows(residual, post_gain, gate_weight, up_weight)
+    scale = lax.rsqrt(second / WIDTH + epsilon)[:, None]
     hidden = gate_weight.shape[1] // 2
-    both = sums[:token_rows] * scale
+    both = sums * scale
     active = (jax.nn.silu(both[:, :hidden]) * both[:, hidden:]).astype(BF16)
     near = spread(active, PAIRS, 8)
     next_to = swap_pairs(near)

time: 261 us -> 257 us (0.985)
  blocking collectives: 126 us -> 123 us
    all_to_all x2 -> x1, blocking collectives: 70.3 us -> 34.5 us  [reduce_rows(): far = lax.all_to_all(total, axes, 0, 0).astype(F32)]
    all_to_all x0 -> x1, blocking collectives: none -> 32.2 us  [reduce_wide_rows(): sums = jnp.sum(lax.all_to_all(total, PAIRS, 0, 0).astype(F32), axis=0)]
where the time goes in v4:
time: 257 us; the launch traced here: 256 us
  blocking collectives  123 us (48%)
  starting transfers between devices  62.3 us (24%)
  waiting for transfers between devices  55.1 us (21%)
  other arithmetic  5.36 us (2%)
  local copies, waits for them, and re-layouts  5 us (2%)
  matrix products  3.81 us (1%)
    all_to_all x2, blocking collectives, spread(): lax.all_to_all(jnp.broadcast_to(block[None], (count,) + block.shape), axe...  44.5 us
    all_to_all x1, blocking collectives, reduce_rows(): far = lax.all_to_all(total, axes, 0, 0).astype(F32)  34.5 us
    all_to_all x1, blocking collectives, reduce_wide_rows(): sums = jnp.sum(lax.all_to_all(total, PAIRS, 0, 0).astype(F32), axis=0)  32.2 us
    ppermute x4, starting transfers between devices, swap(): return lax.ppermute(block, axis, [(0, 1), (1, 0)])  25.3 us
    all_to_all x3, waiting for transfers between devices, spread(): lax.all_to_all(jnp.broadcast_to(block[None], (count,) + block.shape), axe...  24.4 us
    ppermute x3, starting transfers between devices, swap_pairs(): return lax.ppermute(block, RING + ('c',), moves)  18.6 us
    ppermute x3, waiting for transfers between devices, swap_pairs(): return lax.ppermute(block, RING + ('c',), moves)  17 us
    all_to_all x3, starting transfers between devices, spread(): lax.all_to_all(jnp.broadcast_to(block[None], (count,) + block.shape), axe...  14.8 us
  transfers between devices with their start and end apart: 11, of which 11 were waited for; matrix products, arithmetic and copies ran while one was open for 1% of the time, Pallas kernels for 0%

profile of v4, /device:TPU:1, one launch (start us, length us, event | category | flops | bytes accessed | tf_op | source)
XLA Modules:
  0.0 255.7 jit_solution(10984102941041809429)
XLA Ops:
  2.3 7.6 %all-to-all-start = ((bf16[16,48,256]{2,1,0:T(8,128)(2,1)}), bf16[16,48,256]{2,1,0:T(8,128)(2,1)S(1)}, u32[]{:S(2)}, u32[]{:S(2)}) async-start(bf16[16,48,256]{2,1,0:T(8,128)(2,1)} %broadcast_in_dim.44), calls=%async_computation | async-start | bytes 786432 | tf_op jit(solution)/shard_map/all_to_all | solution.py:23
  10.0 8.0 %all-to-all-done = bf16[16,48,256]{2,1,0:T(8,128)(2,1)S(1)} async-done(((bf16[16,48,256]{2,1,0:T(8,128)(2,1)}), bf16[16,48,256]{2,1,0:T(8,128)(2,1)S(1)}, u32[]{:S(2)}, u32[]{:S(2)}) %all-to-all-start) | async-done | bytes 393248 | tf_op jit(solution)/shard_map/all_to_all | solution.py:23
  18.9 5.7 %collective-permute-start = (bf16[32,24,512]{2,1,0:T(8,128)(2,1)S(1)}, bf16[32,24,512]{2,1,0:T(8,128)(2,1)S(1)}, u32[]{:S(2)}, u32[]{:S(2)}) collective-permute-start(bf16[32,24,512]{2,1,0:T(8,128)(2,1)S(1)} %broadcast_select_fusion), channel_id=1, source_target_pairs={{0,16},{16,0},{1,17},{17,1},{2,18},{18,2},{3,19},{19,3},{4,20},{20... | collective-permute-start | bytes 2359304 | tf_op jit(solution)/shard_map/ppermute | solution.py:27
  27.0 10.0 %collective-permute-start.1 = (bf16[16,24,512]{2,1,0:T(8,128)(2,1)S(1)}, bf16[16,24,512]{2,1,0:T(8,128)(2,1)S(1)}, u32[]{:S(2)}, u32[]{:S(2)}) collective-permute-start(bf16[16,24,512]{2,1,0:T(8,128)(2,1)S(1)} %slice.123), channel_id=1, source_target_pairs={{0,32},{16,496},{32,0},{48,80},{64,96},{80,48},{96,64},{112,144},{... | collective-permute-start | bytes 1179656 | tf_op jit(solution)/shard_map/ppermute | solution.py:36
  37.1 5.2 %collective-permute-done.1 = bf16[16,24,512]{2,1,0:T(8,128)(2,1)S(1)} collective-permute-done((bf16[16,24,512]{2,1,0:T(8,128)(2,1)S(1)}, bf16[16,24,512]{2,1,0:T(8,128)(2,1)S(1)}, u32[]{:S(2)}, u32[]{:S(2)}) %collective-permute-start.1) | collective-permute-done | bytes 393248 | tf_op jit(solution)/shard_map/ppermute | solution.py:36
  42.3 34.5 %all_to_all.45 = bf16[16,24,512]{2,1,0:T(8,128)(2,1)S(1)} all-to-all(bf16[16,24,512]{2,1,0:T(8,128)(2,1)S(1)} %add_convert_fusion.3), channel_id=1, replica_groups=mesh['zh'=4,'zm'=2,'zp'=2,'c'=2,'y'=4,'xm'=2,'xp'=2] {'zh','zm','c'}, dimensions={0} | all-to-all | bytes 786432 | tf_op jit(solution)/shard_map/all_to_all | solution.py:84
  78.2 3.7 %all-to-all-start.2 = ((bf16[16,20,544]{2,1,0:T(8,128)(2,1)}), bf16[16,20,544]{2,1,0:T(8,128)(2,1)S(1)}, u32[]{:S(2)}, u32[]{:S(2)}) async-start(bf16[16,20,544]{2,1,0:T(8,128)(2,1)} %broadcast_in_dim.81), calls=%async_computation.2 | async-start | bytes 983040 | tf_op jit(solution)/shard_map/all_to_all | solution.py:23
  81.9 8.7 %all-to-all-done.2 = bf16[16,20,544]{2,1,0:T(8,128)(2,1)S(1)} async-done(((bf16[16,20,544]{2,1,0:T(8,128)(2,1)}), bf16[16,20,544]{2,1,0:T(8,128)(2,1)S(1)}, u32[]{:S(2)}, u32[]{:S(2)}) %all-to-all-start.2) | async-done | bytes 348192 | tf_op jit(solution)/shard_map/all_to_all | solution.py:23
  92.5 20.5 %all_to_all.46 = bf16[16,16,640]{2,1,0:T(8,128)(2,1)S(1)} all-to-all(bf16[16,16,640]{2,1,0:T(8,128)(2,1)S(1)} %broadcast_in_dim.83), channel_id=1, replica_groups=mesh['zh'=4,'zm'=2,'zp'=2,'c'=2,'y'=4,'xm'=2,'xp'=2] {'zh','zm','zp'}, dimensions={0} | all-to-all | bytes 655360 | tf_op jit(solution)/shard_map/all_to_all | solution.py:23
  113.3 9.4 %collective-permute-start.2 = (bf16[16,20,512]{2,1,0:T(8,128)(2,1)S(1)}, bf16[16,20,512]{2,1,0:T(8,128)(2,1)S(1)}, u32[]{:S(2)}, u32[]{:S(2)}) collective-permute-start(bf16[16,20,512]{2,1,0:T(8,128)(2,1)S(1)} %reshape.128), channel_id=1, source_target_pairs={{0,16},{16,0},{1,17},{17,1},{2,18},{18,2},{3,19},{19,3},{4,20},{20... | collective-permute-start | bytes 983048 | tf_op jit(solution)/shard_map/ppermute | solution.py:27
  125.5 11.6 %all_to_all.47 = bf16[16,40,256]{2,1,0:T(8,128)(2,1)S(1)} all-to-all(bf16[16,40,256]{2,1,0:T(8,128)(2,1)S(1)} %bitcast.56), channel_id=1, replica_groups=mesh['zh'=4,'zm'=2,'zp'=2,'c'=2,'y'=4,'xm'=2,'xp'=2] {'y','xm','xp'}, dimensions={0} | all-to-all | bytes 655360 | tf_op jit(solution)/shard_map/all_to_all | solution.py:180
  137.9 3.5 %all-to-all-start.5 = ((bf16[16,40,256]{2,1,0:T(8,128)(2,1)}), bf16[16,40,256]{2,1,0:T(8,128)(2,1)S(1)}, u32[]{:S(2)}, u32[]{:S(2)}) async-start(bf16[16,40,256]{2,1,0:T(8,128)(2,1)} %broadcast_in_dim.84), calls=%async_computation.5 | async-start | bytes 655360 | tf_op jit(solution)/shard_map/all_to_all | solution.py:23
  141.6 7.7 %all-to-all-done.5 = bf16[16,40,256]{2,1,0:T(8,128)(2,1)S(1)} async-done(((bf16[16,40,256]{2,1,0:T(8,128)(2,1)}), bf16[16,40,256]{2,1,0:T(8,128)(2,1)S(1)}, u32[]{:S(2)}, u32[]{:S(2)}) %all-to-all-start.5) | async-done | bytes 327712 | tf_op jit(solution)/shard_map/all_to_all | solution.py:23
  150.3 4.3 %collective-permute-start.3 = (bf16[16,128,256]{2,1,0:T(8,128)(2,1)S(1)}, bf16[16,128,256]{2,1,0:T(8,128)(2,1)S(1)}, u32[]{:S(2)}, u32[]{:S(2)}) collective-permute-start(bf16[16,128,256]{2,1,0:T(8,128)(2,1)S(1)} %fusion.3), channel_id=1, source_target_pairs={{0,16},{16,0},{1,17},{17,1},{2,18},{18,2},{3,19},{19,3},{4,20},{20... | collective-permute-start | bytes 3145736 | tf_op jit(solution)/shard_map/ppermute | solution.py:27
  155.1 1.8 collective-permute-done.3
  157.2 5.6 %collective-permute-start.4 = (bf16[8,128,256]{2,1,0:T(8,128)(2,1)S(1)}, bf16[8,128,256]{2,1,0:T(8,128)(2,1)S(1)}, u32[]{:S(2)}, u32[]{:S(2)}) collective-permute-start(bf16[8,128,256]{2,1,0:T(8,128)(2,1)S(1)} %slice.142), channel_id=1, source_target_pairs={{0,32},{16,496},{32,0},{48,80},{64,96},{80,48},{96,64},{112,144},{... | collective-permute-start | bytes 1572872 | tf_op jit(solution)/shard_map/ppermute | solution.py:36
  162.9 6.6 %collective-permute-done.4 = bf16[8,128,256]{2,1,0:T(8,128)(2,1)S(1)} collective-permute-done((bf16[8,128,256]{2,1,0:T(8,128)(2,1)S(1)}, bf16[8,128,256]{2,1,0:T(8,128)(2,1)S(1)}, u32[]{:S(2)}, u32[]{:S(2)}) %collective-permute-start.4) | collective-permute-done | bytes 524320 | tf_op jit(solution)/shard_map/ppermute | solution.py:36
  169.6 32.2 %all_to_all.48 = bf16[8,128,256]{2,1,0:T(8,128)(2,1)S(1)} all-to-all(bf16[8,128,256]{2,1,0:T(8,128)(2,1)S(1)} %add_convert_fusion.2), channel_id=1, replica_groups=mesh['zh'=4,'zm'=2,'zp'=2,'c'=2,'y'=4,'xm'=2,'xp'=2] {'zh','zm'}, dimensions={0} | all-to-all | bytes 1048576 | tf_op jit(solution)/shard_map/all_to_all | solution.py:114
  202.0 24.0 %all_to_all.49 = bf16[8,40,384]{2,1,0:T(8,128)(2,1)S(1)} all-to-all(bf16[8,40,384]{2,1,0:T(8,128)(2,1)S(1)} %broadcast_in_dim.85), channel_id=1, replica_groups=mesh['zh'=4,'zm'=2,'zp'=2,'c'=2,'y'=4,'xm'=2,'xp'=2] {'zh','zm'}, dimensions={0} | all-to-all | bytes 491520 | tf_op jit(solution)/shard_map/all_to_all | solution.py:23
  226.0 3.0 %collective-permute-start.5 = (bf16[8,40,384]{2,1,0:T(8,128)(2,1)S(1)}, bf16[8,40,384]{2,1,0:T(8,128)(2,1)S(1)}, u32[]{:S(2)}, u32[]{:S(2)}) collective-permute-start(bf16[8,40,384]{2,1,0:T(8,128)(2,1)S(1)} %all_to_all.49), channel_id=1, source_target_pairs={{0,32},{16,496},{32,0},{48,80},{64,96},{80,48},{96,64},{112,144},{... | collective-permute-start | bytes 737288 | tf_op jit(solution)/shard_map/ppermute | solution.py:36
  229.0 5.3 %collective-permute-done.5 = bf16[8,40,384]{2,1,0:T(8,128)(2,1)S(1)} collective-permute-done((bf16[8,40,384]{2,1,0:T(8,128)(2,1)S(1)}, bf16[8,40,384]{2,1,0:T(8,128)(2,1)S(1)}, u32[]{:S(2)}, u32[]{:S(2)}) %collective-permute-start.5) | collective-permute-done | bytes 245792 | tf_op jit(solution)/shard_map/ppermute | solution.py:36
  234.4 5.9 %collective-permute-start.6 = (bf16[16,40,384]{2,1,0:T(8,128)(2,1)S(1)}, bf16[16,40,384]{2,1,0:T(8,128)(2,1)S(1)}, u32[]{:S(2)}, u32[]{:S(2)}) collective-permute-start(bf16[16,40,384]{2,1,0:T(8,128)(2,1)S(1)} %pad_maximum_fusion.1), channel_id=1, source_target_pairs={{0,16},{16,0},{1,17},{17,1},{2,18},{18,2},{3,19},{19,3},{4,20},{20... | collective-permute-start | bytes 1474568 | tf_op jit(solution)/shard_map/ppermute | solution.py:27
  243.2 3.5 %all-to-all-start.8 = ((bf16[16,40,256]{2,1,0:T(8,128)(2,1)}), bf16[16,40,256]{2,1,0:T(8,128)(2,1)S(1)}, u32[]{:S(2)}, u32[]{:S(2)}) async-start(bf16[16,40,256]{2,1,0:T(8,128)(2,1)} %bitcast.21), calls=%async_computation.8 | async-start | bytes 655360 | tf_op jit(solution)/shard_map/all_to_all | solution.py:202
  247.4 7.6 %all-to-all-done.8 = bf16[16,40,256]{2,1,0:T(8,128)(2,1)S(1)} async-done(((bf16[16,40,256]{2,1,0:T(8,128)(2,1)}), bf16[16,40,256]{2,1,0:T(8,128)(2,1)S(1)}, u32[]{:S(2)}, u32[]{:S(2)}) %all-to-all-start.8) | async-done | bytes 327712 | tf_op jit(solution)/shard_map/all_to_all | solution.py:202
  (108 shorter events, 18.5 us)
Async XLA Ops:
  0.6 76.4 %copy-start = (bf16[512,544]{0,1:T(8,128)(2,1)S(1)}, bf16[512,544]{0,1:T(8,128)(2,1)}, u32[]{:S(2)}) copy-start(bf16[512,544]{0,1:T(8,128)(2,1)} %param.25) | copy-start | bytes 1671172
  0.6 9.2 %copy-start.8 = (bf16[256,512]{1,0:T(8,128)(2,1)S(1)}, bf16[256,512]{1,0:T(8,128)(2,1)}, u32[]{:S(2)}) copy-start(bf16[256,512]{1,0:T(8,128)(2,1)} %param.20) | copy-start | bytes 786436
  0.7 9.2 %copy-start.7 = (bf16[256,512]{1,0:T(8,128)(2,1)S(1)}, bf16[256,512]{1,0:T(8,128)(2,1)}, u32[]{:S(2)}) copy-start(bf16[256,512]{1,0:T(8,128)(2,1)} %param.21) | copy-start | bytes 786436
  2.3 15.7 %all-to-all-start = ((bf16[16,48,256]{2,1,0:T(8,128)(2,1)}), bf16[16,48,256]{2,1,0:T(8,128)(2,1)S(1)}, u32[]{:S(2)}, u32[]{:S(2)}) async-start(bf16[16,48,256]{2,1,0:T(8,128)(2,1)} %broadcast_in_dim.44), calls=%async_computation | async-start | bytes 786432 | tf_op jit(solution)/shard_map/all_to_all | solution.py:23
  18.9 7.6 %collective-permute-start = (bf16[32,24,512]{2,1,0:T(8,128)(2,1)S(1)}, bf16[32,24,512]{2,1,0:T(8,128)(2,1)S(1)}, u32[]{:S(2)}, u32[]{:S(2)}) collective-permute-start(bf16[32,24,512]{2,1,0:T(8,128)(2,1)S(1)} %broadcast_select_fusion), channel_id=1, source_target_pairs={{0,16},{16,0},{1,17},{17,1},{2,18},{18,2},{3,19},{19,3},{4,20},{20... | collective-permute-start | bytes 2359304 | tf_op jit(solution)/shard_map/ppermute | solution.py:27
  27.0 15.2 %collective-permute-start.1 = (bf16[16,24,512]{2,1,0:T(8,128)(2,1)S(1)}, bf16[16,24,512]{2,1,0:T(8,128)(2,1)S(1)}, u32[]{:S(2)}, u32[]{:S(2)}) collective-permute-start(bf16[16,24,512]{2,1,0:T(8,128)(2,1)S(1)} %slice.123), channel_id=1, source_target_pairs={{0,32},{16,496},{32,0},{48,80},{64,96},{80,48},{96,64},{112,144},{... | collective-permute-start | bytes 1179656 | tf_op jit(solution)/shard_map/ppermute | solution.py:36
  42.3 34.7 %copy-start.6 = (bf16[3,20,512]{2,1,0:T(8,128)(2,1)S(1)}, bf16[3,20,512]{2,1,0:T(8,128)(2,1)}, u32[]{:S(2)}) copy-start(bf16[3,20,512]{2,1,0:T(8,128)(2,1)} %param.22) | copy-start | bytes 184324
  42.3 34.7 %copy-start.13 = (f32[4,512]{1,0:T(4,128)S(1)}, f32[4,512]{1,0:T(4,128)}, u32[]{:S(2)}) copy-start(f32[4,512]{1,0:T(4,128)} %param.23) | copy-start | bytes 24580
  42.3 34.7 %copy-start.12 = (f32[512]{0:T(512)S(1)}, f32[512]{0:T(512)}, u32[]{:S(2)}) copy-start(f32[512]{0:T(512)} %param.24) | copy-start | bytes 6148
  77.3 13.6 %copy-start.2 = (bf16[512,512]{1,0:T(8,128)(2,1)S(1)}, bf16[512,512]{1,0:T(8,128)(2,1)}, u32[]{:S(2)}) copy-start(bf16[512,512]{1,0:T(8,128)(2,1)} %param.26) | copy-start | bytes 1572868
  77.3 13.6 %copy-start.14 = (f32[512]{0:T(512)S(1)}, f32[512]{0:T(512)}, u32[]{:S(2)}) copy-start(f32[512]{0:T(512)} %param.27) | copy-start | bytes 6148
  78.2 13.1 %copy-start.1 = (f32[20,16,512]{2,1,0:T(8,128)S(1)}, f32[20,16,512]{2,1,0:T(8,128)}, u32[]{:S(2)}) copy-start(f32[20,16,512]{2,1,0:T(8,128)} %param.29) | copy-start | bytes 1966084
  78.2 12.4 %all-to-all-start.2 = ((bf16[16,20,544]{2,1,0:T(8,128)(2,1)}), bf16[16,20,544]{2,1,0:T(8,128)(2,1)S(1)}, u32[]{:S(2)}, u32[]{:S(2)}) async-start(bf16[16,20,544]{2,1,0:T(8,128)(2,1)} %broadcast_in_dim.81), calls=%async_computation.2 | async-start | bytes 983040 | tf_op jit(solution)/shard_map/all_to_all | solution.py:23
  113.3 10.7 %collective-permute-start.2 = (bf16[16,20,512]{2,1,0:T(8,128)(2,1)S(1)}, bf16[16,20,512]{2,1,0:T(8,128)(2,1)S(1)}, u32[]{:S(2)}, u32[]{:S(2)}) collective-permute-start(bf16[16,20,512]{2,1,0:T(8,128)(2,1)S(1)} %reshape.128), channel_id=1, source_target_pairs={{0,16},{16,0},{1,17},{17,1},{2,18},{18,2},{3,19},{19,3},{4,20},{20... | collective-permute-start | bytes 983048 | tf_op jit(solution)/shard_map/ppermute | solution.py:27
  125.1 12.1 %copy-start.10 = (bf16[40,256]{1,0:T(8,128)(2,1)S(1)}, bf16[40,256]{1,0:T(8,128)(2,1)}, u32[]{:S(2)}) copy-start(bf16[40,256]{1,0:T(8,128)(2,1)} %param.18) | copy-start | bytes 61444
  125.4 16.1 %copy-start.4 = (bf16[256,768]{1,0:T(8,128)(2,1)S(1)}, bf16[256,768]{1,0:T(8,128)(2,1)}, u32[]{:S(2)}) copy-start(bf16[256,768]{1,0:T(8,128)(2,1)} %param.34) | copy-start | bytes 1179652
  125.5 16.1 %copy-start.5 = (bf16[256,768]{1,0:T(8,128)(2,1)S(1)}, bf16[256,768]{1,0:T(8,128)(2,1)}, u32[]{:S(2)}) copy-start(bf16[256,768]{1,0:T(8,128)(2,1)} %param.33) | copy-start | bytes 1179652
  137.9 11.4 %all-to-all-start.5 = ((bf16[16,40,256]{2,1,0:T(8,128)(2,1)}), bf16[16,40,256]{2,1,0:T(8,128)(2,1)S(1)}, u32[]{:S(2)}, u32[]{:S(2)}) async-start(bf16[16,40,256]{2,1,0:T(8,128)(2,1)} %broadcast_in_dim.84), calls=%async_computation.5 | async-start | bytes 655360 | tf_op jit(solution)/shard_map/all_to_all | solution.py:23
  150.3 6.5 %collective-permute-start.3 = (bf16[16,128,256]{2,1,0:T(8,128)(2,1)S(1)}, bf16[16,128,256]{2,1,0:T(8,128)(2,1)S(1)}, u32[]{:S(2)}, u32[]{:S(2)}) collective-permute-start(bf16[16,128,256]{2,1,0:T(8,128)(2,1)S(1)} %fusion.3), channel_id=1, source_target_pairs={{0,16},{16,0},{1,17},{17,1},{2,18},{18,2},{3,19},{19,3},{4,20},{20... | collective-permute-start | bytes 3145736 | tf_op jit(solution)/shard_map/ppermute | solution.py:27
  157.2 12.2 %collective-permute-start.4 = (bf16[8,128,256]{2,1,0:T(8,128)(2,1)S(1)}, bf16[8,128,256]{2,1,0:T(8,128)(2,1)S(1)}, u32[]{:S(2)}, u32[]{:S(2)}) collective-permute-start(bf16[8,128,256]{2,1,0:T(8,128)(2,1)S(1)} %slice.142), channel_id=1, source_target_pairs={{0,32},{16,496},{32,0},{48,80},{64,96},{80,48},{96,64},{112,144},{... | collective-permute-start | bytes 1572872 | tf_op jit(solution)/shard_map/ppermute | solution.py:36
  226.0 15.8 %copy-start.3 = (bf16[768,256]{1,0:T(8,128)(2,1)S(1)}, bf16[768,256]{1,0:T(8,128)(2,1)}, u32[]{:S(2)}) copy-start(bf16[768,256]{1,0:T(8,128)(2,1)} %param.35) | copy-start | bytes 1179652
  226.0 8.3 %collective-permute-start.5 = (bf16[8,40,384]{2,1,0:T(8,128)(2,1)S(1)}, bf16[8,40,384]{2,1,0:T(8,128)(2,1)S(1)}, u32[]{:S(2)}, u32[]{:S(2)}) collective-permute-start(bf16[8,40,384]{2,1,0:T(8,128)(2,1)S(1)} %all_to_all.49), channel_id=1, source_target_pairs={{0,32},{16,496},{32,0},{48,80},{64,96},{80,48},{96,64},{112,144},{... | collective-permute-start | bytes 737288 | tf_op jit(solution)/shard_map/ppermute | solution.py:36
  234.4 7.4 %collective-permute-start.6 = (bf16[16,40,384]{2,1,0:T(8,128)(2,1)S(1)}, bf16[16,40,384]{2,1,0:T(8,128)(2,1)S(1)}, u32[]{:S(2)}, u32[]{:S(2)}) collective-permute-start(bf16[16,40,384]{2,1,0:T(8,128)(2,1)S(1)} %pad_maximum_fusion.1), channel_id=1, source_target_pairs={{0,16},{16,0},{1,17},{17,1},{2,18},{18,2},{3,19},{19,3},{4,20},{20... | collective-permute-start | bytes 1474568 | tf_op jit(solution)/shard_map/ppermute | solution.py:27
  243.2 11.8 %all-to-all-start.8 = ((bf16[16,40,256]{2,1,0:T(8,128)(2,1)}), bf16[16,40,256]{2,1,0:T(8,128)(2,1)S(1)}, u32[]{:S(2)}, u32[]{:S(2)}) async-start(bf16[16,40,256]{2,1,0:T(8,128)(2,1)} %bitcast.21), calls=%async_computation.8 | async-start | bytes 655360 | tf_op jit(solution)/shard_map/all_to_all | solution.py:202
  (5 other events, 23.6 us)

commit v5 on v4

--- a/solution.py
+++ b/solution.py
@@ -54,45 +54,40 @@
     return lax.dynamic_slice_in_dim(block, which * half, half, 0)
 
 
-def reduce_rows(block, size, gain, left_weight, right_weight, axes):
-    core, pair = lax.axis_index("c"), lax.axis_index("zp")
-    groups, padded, depth = block.shape
-    rows = spread(block.reshape(groups * padded, depth), TENSOR_PAIRS, 16)
-    low, high = rows[:8], rows[8:]
-    rows = jnp.concatenate(
-        [jnp.where(pair == 0, high, low), jnp.where(pair == 0, low, high)], axis=0
-    )
-    wide = rows.astype(F32)
-    scaled = (wide * gain[None, None, :]).astype(BF16).reshape(16 * groups * padded, depth)
-    squares = jnp.sum(wide * wide, axis=2).reshape(16 * groups, 1, padded)
-    half = left_weight.shape[1] // 2
-    columns = half + half
-    marks = jnp.pad(squares.astype(BF16), ((0, 0), (0, 0), (0, columns - padded)))
-    spare = lax.broadcasted_iota(jnp.int32, (1, padded, columns), 1) == size
-
-    def partial(which):
-        weight = jnp.concatenate(
-            [half_columns(left_weight, which), half_columns(right_weight, which)], axis=1
-        )
-        return jnp.where(
-            spare, marks, dot(scaled, weight).astype(BF16).reshape(16 * groups, padded, columns)
-        )
-
-    received = swap(partial(1 - core), "c")
-    both = add(partial(core), received)
-    total = add(both[8 * groups :], swap_pairs(both[: 8 * groups]))
-    far = lax.all_to_all(total, axes, 0, 0).astype(F32)
-    return jnp.sum(far.reshape(8, groups, padded, columns), axis=0)
-
-
-def reduce_wide_rows(block, gain, left_weight, right_weight):
-    core, pair = lax.axis_index("c"), lax.axis_index("zp")
-    size, depth = block.shape
+def spread_rows(block):
     rows = spread(block, TENSOR_PAIRS, 16)
     low, high = rows[:8], rows[8:]
-    rows = jnp.concatenate(
-        [jnp.where(pair == 0, high, low), jnp.where(pair == 0, low, high)], axis=0
-    )
+    even = lax.axis_index("zp") == 0
+    return jnp.concatenate([jnp.where(even, high, low), jnp.where(even, low, high)], axis=0)
+
+
+def reduce_rows(block, gain, weight):
+    first_core = lax.axis_index("c") == 0
+    rows = spread_rows(block)
+    size = rows.shape[1] // 2
+    columns = weight.shape[1]
+    padded = size + 4
+    spare = lax.broadcasted_iota(jnp.int32, (1, padded, columns), 1) == size
+    low, high = rows[:, :size], rows[:, size:]
+
+    def partial(part):
+        wide = jnp.pad(part, ((0, 0), (0, 4), (0, 0))).astype(F32)
+        scaled = (wide * gain[None, None, :]).astype(BF16).reshape(16 * padded, -1)
+        squares = jnp.sum(wide * wide, axis=2).astype(BF16)[:, None, :]
+        marks = jnp.pad(squares, ((0, 0), (0, 0), (0, columns - padded)))
+        return jnp.where(spare, marks, dot(scaled, weight).astype(BF16).reshape(16, padded, columns))
+
+    received = swap(partial(jnp.where(first_core, high, low)), "c")
+    both = add(partial(jnp.where(first_core, low, high)), received)
+    total = add(both[8:], swap_pairs(both[:8]))
+    sums = jnp.sum(lax.all_to_all(total, PAIRS, 0, 0).astype(F32), axis=0)
+    return sums[:size], sums[size, :size]
+
+
+def reduce_wide_rows(block, gain, left_weight, right_weight):
+    core = lax.axis_index("c")
+    size, depth = block.shape
+    rows = spread_rows(block)
     wide = rows.astype(F32)
     scaled = (wide * gain[None, None, :]).astype(BF16).reshape(16 * size, depth)
     squares = jnp.sum(wide * wide, axis=2).astype(BF16)[:, None, :]
@@ -138,18 +133,15 @@
 ):
     core, pair = lax.axis_index("c"), lax.axis_index("zp")
     inner_dev = in_x_weight.shape[1]
-    half = inner_dev // 2
     own_rows = conv_state.shape[1]
     token_rows, token_cols = tokens.shape
 
-    block = jnp.pad(tokens.reshape(2, own_rows, token_cols), ((0, 0), (0, 4), (0, 0)))
-    sums = reduce_rows(
-        block, own_rows, norm_gain, in_x_weight, in_z_weight, ("zh", "zm", "c")
-    )
-    scale = lax.rsqrt(sums[0, own_rows, :own_rows] / WIDTH + epsilon)[:, None]
-    mixed_in = (sums[:, :own_rows] * scale[None]).astype(BF16)
-    inner_x = jnp.concatenate([mixed_in[0, :, :half], mixed_in[1, :, :half]], axis=1)
-    gate_z = jnp.concatenate([mixed_in[0, :, half:], mixed_in[1, :, half:]], axis=1)
+    sums, first = reduce_rows(
+        tokens, norm_gain, jnp.concatenate([in_x_weight, in_z_weight], axis=1)
+    )
+    scale = lax.rsqrt(first / WIDTH + epsilon)[:, None]
+    inner_x = (sums[:, :inner_dev] * scale).astype(BF16)
+    gate_z = (sums[:, inner_dev:] * scale).astype(BF16)
     window = jnp.concatenate([conv_state, inner_x[None]], axis=0)
     conv_pre = jnp.sum(window.astype(F32) * conv_weight[:, None, :], axis=0) + conv_bias[None, :]
     signal = jax.nn.silu(conv_pre).astype(BF16)
@@ -189,14 +181,20 @@
     active = (jax.nn.silu(both[:, :hidden]) * both[:, hidden:]).astype(BF16)
     near = spread(active, PAIRS, 8)
     next_to = swap_pairs(near)
-    same = jnp.concatenate(
-        [jnp.where(pair == 0, near, next_to), jnp.where(pair == 0, next_to, near)], axis=0
-    )
-    other = swap(same, "c")
-    same = same.reshape(16 * token_rows, hidden)
-    other = other.reshape(16 * token_rows, hidden)
-    down_terms = dot(same, half_rows(down_weight, core)) + dot(
-        other, half_rows(down_weight, 1 - core)
+    own_part, other_part = half_rows(down_weight, core), half_rows(down_weight, 1 - core)
+
+    def down(same, other):
+        flat = (8 * token_rows, hidden)
+        return dot(same.reshape(flat), own_part) + dot(other.reshape(flat), other_part)
+
+    near_terms = down(near, swap(near, "c"))
+    next_terms = down(next_to, swap(next_to, "c"))
+    down_terms = jnp.concatenate(
+        [
+            jnp.where(pair == 0, near_terms, next_terms),
+            jnp.where(pair == 0, next_terms, near_terms),
+        ],
+        axis=0,
     )
     down_own = jnp.sum(
         lax.all_to_all(

time: 257 us -> 255 us (level)
  starting transfers between devices: 62.3 us -> 68.9 us
  waiting for transfers between devices: 55.1 us -> 49.5 us
  blocking collectives: 123 us -> 120 us
    ppermute x4 -> x5, starting transfers between devices: 25.3 us -> 33 us  [swap(): return lax.ppermute(block, axis, [(0, 1), (1, 0)])]
    ppermute x3, waiting for transfers between devices: 17 us -> 11.7 us  [swap_pairs(): return lax.ppermute(block, RING + ('c',), moves)]
    ppermute x4 -> x5, waiting for transfers between devices: 6.07 us -> 5.19 us  [swap(): return lax.ppermute(block, axis, [(0, 1), (1, 0)])]
  transfers between devices with their start and end apart: 11 -> 12, of which waited for: 11 -> 10; matrix products, arithmetic and copies ran while one was open for 1% -> 1% of each run, Pallas kernels for 0% -> 0%
where the time goes in v5:
time: 255 us; the launch traced here: 254 us
  blocking collectives  120 us (47%)
  starting transfers between devices  68.9 us (27%)
  waiting for transfers between devices  49.5 us (19%)
  other arithmetic  6.14 us (2%)
  local copies, waits for them, and re-layouts  4.87 us (2%)
  matrix products  3.42 us (1%)
    all_to_all x2, blocking collectives, spread(): lax.all_to_all(jnp.broadcast_to(block[None], (count,) + block.shape), axe...  42.1 us
    all_to_all x1, blocking collectives, reduce_rows(): sums = jnp.sum(lax.all_to_all(total, PAIRS, 0, 0).astype(F32), axis=0)  33.7 us
    ppermute x5, starting transfers between devices, swap(): return lax.ppermute(block, axis, [(0, 1), (1, 0)])  33 us
    all_to_all x1, blocking collectives, reduce_wide_rows(): sums = jnp.sum(lax.all_to_all(total, PAIRS, 0, 0).astype(F32), axis=0)  32.7 us
    all_to_all x3, waiting for transfers between devices, spread(): lax.all_to_all(jnp.broadcast_to(block[None], (count,) + block.shape), axe...  25 us
    ppermute x3, starting transfers between devices, swap_pairs(): return lax.ppermute(block, RING + ('c',), moves)  17.5 us
    all_to_all x3, starting transfers between devices, spread(): lax.all_to_all(jnp.broadcast_to(block[None], (count,) + block.shape), axe...  14.8 us
    all_to_all x1, blocking collectives, on_device(): lax.all_to_all(out_terms.reshape(16, token_rows, token_cols), TENSOR, 0, 0)  11.8 us
  transfers between devices with their start and end apart: 12, of which 10 were waited for; matrix products, arithmetic and copies ran while one was open for 1% of the time, Pallas kernels for 0%

profile of v5, /device:TPU:1, one launch (start us, length us, event | category | flops | bytes accessed | tf_op | source)
XLA Modules:
  0.0 254.4 jit_solution(9388513827814750396)
XLA Ops:
  2.2 7.6 %all-to-all-start = ((bf16[16,40,256]{2,1,0:T(8,128)(2,1)}), bf16[16,40,256]{2,1,0:T(8,128)(2,1)S(1)}, u32[]{:S(2)}, u32[]{:S(2)}) async-start(bf16[16,40,256]{2,1,0:T(8,128)(2,1)} %broadcast_in_dim.45), calls=%async_computation | async-start | bytes 655360 | tf_op jit(solution)/shard_map/all_to_all | solution.py:23
  9.9 7.7 %all-to-all-done = bf16[16,40,256]{2,1,0:T(8,128)(2,1)S(1)} async-done(((bf16[16,40,256]{2,1,0:T(8,128)(2,1)}), bf16[16,40,256]{2,1,0:T(8,128)(2,1)S(1)}, u32[]{:S(2)}, u32[]{:S(2)}) %all-to-all-start) | async-done | bytes 327712 | tf_op jit(solution)/shard_map/all_to_all | solution.py:23
  18.6 5.7 %collective-permute-start = (bf16[16,24,1024]{2,1,0:T(8,128)(2,1)S(1)}, bf16[16,24,1024]{2,1,0:T(8,128)(2,1)S(1)}, u32[]{:S(2)}, u32[]{:S(2)}) collective-permute-start(bf16[16,24,1024]{2,1,0:T(8,128)(2,1)S(1)} %broadcast_select_fusion), channel_id=1, source_target_pairs={{0,16},{16,0},{1,17},{17,1},{2,18},{18,2},{3,19},{19,3},{4,20},{20... | collective-permute-start | bytes 2359304 | tf_op jit(solution)/shard_map/ppermute | solution.py:27
  26.7 9.8 %collective-permute-start.1 = (bf16[8,24,1024]{2,1,0:T(8,128)(2,1)S(1)}, bf16[8,24,1024]{2,1,0:T(8,128)(2,1)S(1)}, u32[]{:S(2)}, u32[]{:S(2)}) collective-permute-start(bf16[8,24,1024]{2,1,0:T(8,128)(2,1)S(1)} %slice.124), channel_id=1, source_target_pairs={{0,32},{16,496},{32,0},{48,80},{64,96},{80,48},{96,64},{112,144},{... | collective-permute-start | bytes 1179656 | tf_op jit(solution)/shard_map/ppermute | solution.py:36
  36.5 5.2 %collective-permute-done.1 = bf16[8,24,1024]{2,1,0:T(8,128)(2,1)S(1)} collective-permute-done((bf16[8,24,1024]{2,1,0:T(8,128)(2,1)S(1)}, bf16[8,24,1024]{2,1,0:T(8,128)(2,1)S(1)}, u32[]{:S(2)}, u32[]{:S(2)}) %collective-permute-start.1) | collective-permute-done | bytes 393248 | tf_op jit(solution)/shard_map/ppermute | solution.py:36
  41.9 33.7 %all_to_all.45 = bf16[8,24,1024]{2,1,0:T(8,128)(2,1)S(1)} all-to-all(bf16[8,24,1024]{2,1,0:T(8,128)(2,1)S(1)} %add_convert_fusion.3), channel_id=1, replica_groups=mesh['zh'=4,'zm'=2,'zp'=2,'c'=2,'y'=4,'xm'=2,'xp'=2] {'zh','zm'}, dimensions={0} | all-to-all | bytes 786432 | tf_op jit(solution)/shard_map/all_to_all | solution.py:83
  76.8 3.7 %all-to-all-start.2 = ((bf16[16,20,544]{2,1,0:T(8,128)(2,1)}), bf16[16,20,544]{2,1,0:T(8,128)(2,1)S(1)}, u32[]{:S(2)}, u32[]{:S(2)}) async-start(bf16[16,20,544]{2,1,0:T(8,128)(2,1)} %broadcast_in_dim.89), calls=%async_computation.2 | async-start | bytes 983040 | tf_op jit(solution)/shard_map/all_to_all | solution.py:23
  80.6 9.6 %all-to-all-done.2 = bf16[16,20,544]{2,1,0:T(8,128)(2,1)S(1)} async-done(((bf16[16,20,544]{2,1,0:T(8,128)(2,1)}), bf16[16,20,544]{2,1,0:T(8,128)(2,1)S(1)}, u32[]{:S(2)}, u32[]{:S(2)}) %all-to-all-start.2) | async-done | bytes 348192 | tf_op jit(solution)/shard_map/all_to_all | solution.py:23
  92.2 18.4 %all_to_all.46 = bf16[16,16,640]{2,1,0:T(8,128)(2,1)S(1)} all-to-all(bf16[16,16,640]{2,1,0:T(8,128)(2,1)S(1)} %broadcast_in_dim.91), channel_id=1, replica_groups=mesh['zh'=4,'zm'=2,'zp'=2,'c'=2,'y'=4,'xm'=2,'xp'=2] {'zh','zm','zp'}, dimensions={0} | all-to-all | bytes 655360 | tf_op jit(solution)/shard_map/all_to_all | solution.py:23
  110.9 10.1 %collective-permute-start.2 = (bf16[16,20,512]{2,1,0:T(8,128)(2,1)S(1)}, bf16[16,20,512]{2,1,0:T(8,128)(2,1)S(1)}, u32[]{:S(2)}, u32[]{:S(2)}) collective-permute-start(bf16[16,20,512]{2,1,0:T(8,128)(2,1)S(1)} %reshape.128), channel_id=1, source_target_pairs={{0,16},{16,0},{1,17},{17,1},{2,18},{18,2},{3,19},{19,3},{4,20},{20... | collective-permute-start | bytes 983048 | tf_op jit(solution)/shard_map/ppermute | solution.py:27
  123.7 11.8 %all_to_all.47 = bf16[16,40,256]{2,1,0:T(8,128)(2,1)S(1)} all-to-all(bf16[16,40,256]{2,1,0:T(8,128)(2,1)S(1)} %bitcast.55), channel_id=1, replica_groups=mesh['zh'=4,'zm'=2,'zp'=2,'c'=2,'y'=4,'xm'=2,'xp'=2] {'y','xm','xp'}, dimensions={0} | all-to-all | bytes 655360 | tf_op jit(solution)/shard_map/all_to_all | solution.py:172
  136.4 3.5 %all-to-all-start.5 = ((bf16[16,40,256]{2,1,0:T(8,128)(2,1)}), bf16[16,40,256]{2,1,0:T(8,128)(2,1)S(1)}, u32[]{:S(2)}, u32[]{:S(2)}) async-start(bf16[16,40,256]{2,1,0:T(8,128)(2,1)} %broadcast_in_dim.92), calls=%async_computation.5 | async-start | bytes 655360 | tf_op jit(solution)/shard_map/all_to_all | solution.py:23
  140.1 7.6 %all-to-all-done.5 = bf16[16,40,256]{2,1,0:T(8,128)(2,1)S(1)} async-done(((bf16[16,40,256]{2,1,0:T(8,128)(2,1)}), bf16[16,40,256]{2,1,0:T(8,128)(2,1)S(1)}, u32[]{:S(2)}, u32[]{:S(2)}) %all-to-all-start.5) | async-done | bytes 327712 | tf_op jit(solution)/shard_map/all_to_all | solution.py:23
  148.6 4.5 %collective-permute-start.3 = (bf16[16,128,256]{2,1,0:T(8,128)(2,1)S(1)}, bf16[16,128,256]{2,1,0:T(8,128)(2,1)S(1)}, u32[]{:S(2)}, u32[]{:S(2)}) collective-permute-start(bf16[16,128,256]{2,1,0:T(8,128)(2,1)S(1)} %fusion.2), channel_id=1, source_target_pairs={{0,16},{16,0},{1,17},{17,1},{2,18},{18,2},{3,19},{19,3},{4,20},{20... | collective-permute-start | bytes 3145736 | tf_op jit(solution)/shard_map/ppermute | solution.py:27
  153.6 1.8 collective-permute-done.3
  155.7 5.5 %collective-permute-start.4 = (bf16[8,128,256]{2,1,0:T(8,128)(2,1)S(1)}, bf16[8,128,256]{2,1,0:T(8,128)(2,1)S(1)}, u32[]{:S(2)}, u32[]{:S(2)}) collective-permute-start(bf16[8,128,256]{2,1,0:T(8,128)(2,1)S(1)} %slice.140), channel_id=1, source_target_pairs={{0,32},{16,496},{32,0},{48,80},{64,96},{80,48},{96,64},{112,144},{... | collective-permute-start | bytes 1572872 | tf_op jit(solution)/shard_map/ppermute | solution.py:36
  161.3 6.6 %collective-permute-done.4 = bf16[8,128,256]{2,1,0:T(8,128)(2,1)S(1)} collective-permute-done((bf16[8,128,256]{2,1,0:T(8,128)(2,1)S(1)}, bf16[8,128,256]{2,1,0:T(8,128)(2,1)S(1)}, u32[]{:S(2)}, u32[]{:S(2)}) %collective-permute-start.4) | collective-permute-done | bytes 524320 | tf_op jit(solution)/shard_map/ppermute | solution.py:36
  168.0 32.7 %all_to_all.48 = bf16[8,128,256]{2,1,0:T(8,128)(2,1)S(1)} all-to-all(bf16[8,128,256]{2,1,0:T(8,128)(2,1)S(1)} %add_convert_fusion.2), channel_id=1, replica_groups=mesh['zh'=4,'zm'=2,'zp'=2,'c'=2,'y'=4,'xm'=2,'xp'=2] {'zh','zm'}, dimensions={0} | all-to-all | bytes 1048576 | tf_op jit(solution)/shard_map/all_to_all | solution.py:109
  201.0 23.6 %all_to_all.49 = bf16[8,40,384]{2,1,0:T(8,128)(2,1)S(1)} all-to-all(bf16[8,40,384]{2,1,0:T(8,128)(2,1)S(1)} %broadcast_in_dim.93), channel_id=1, replica_groups=mesh['zh'=4,'zm'=2,'zp'=2,'c'=2,'y'=4,'xm'=2,'xp'=2] {'zh','zm'}, dimensions={0} | all-to-all | bytes 491520 | tf_op jit(solution)/shard_map/all_to_all | solution.py:23
  224.6 2.1 collective-permute-start.6
  226.7 7.0 %collective-permute-start.5 = (bf16[8,40,384]{2,1,0:T(8,128)(2,1)S(1)}, bf16[8,40,384]{2,1,0:T(8,128)(2,1)S(1)}, u32[]{:S(2)}, u32[]{:S(2)}) collective-permute-start(bf16[8,40,384]{2,1,0:T(8,128)(2,1)S(1)} %all_to_all.49), channel_id=1, source_target_pairs={{0,16},{16,0},{1,17},{17,1},{2,18},{18,2},{3,19},{19,3},{4,20},{20... | collective-permute-start | bytes 737288 | tf_op jit(solution)/shard_map/ppermute | solution.py:27
  234.0 5.8 %collective-permute-start.7 = (bf16[8,40,384]{2,1,0:T(8,128)(2,1)S(1)}, bf16[8,40,384]{2,1,0:T(8,128)(2,1)S(1)}, u32[]{:S(2)}, u32[]{:S(2)}) collective-permute-start(bf16[8,40,384]{2,1,0:T(8,128)(2,1)S(1)} %collective-permute-done.6), channel_id=1, source_target_pairs={{0,16},{16,0},{1,17},{17,1},{2,18},{18,2},{3,19},{19,3},{4,20},{20... | collective-permute-start | bytes 737288 | tf_op jit(solution)/shard_map/ppermute | solution.py:27
  241.9 3.5 %all-to-all-start.8 = ((bf16[16,40,256]{2,1,0:T(8,128)(2,1)}), bf16[16,40,256]{2,1,0:T(8,128)(2,1)S(1)}, u32[]{:S(2)}, u32[]{:S(2)}) async-start(bf16[16,40,256]{2,1,0:T(8,128)(2,1)} %bitcast.21), calls=%async_computation.8 | async-start | bytes 655360 | tf_op jit(solution)/shard_map/all_to_all | solution.py:200
  246.1 7.6 %all-to-all-done.8 = bf16[16,40,256]{2,1,0:T(8,128)(2,1)S(1)} async-done(((bf16[16,40,256]{2,1,0:T(8,128)(2,1)}), bf16[16,40,256]{2,1,0:T(8,128)(2,1)S(1)}, u32[]{:S(2)}, u32[]{:S(2)}) %all-to-all-start.8) | async-done | bytes 327712 | tf_op jit(solution)/shard_map/all_to_all | solution.py:200
  (107 shorter events, 17.9 us)
Async XLA Ops:
  0.6 75.1 %copy-start = (bf16[512,544]{0,1:T(8,128)(2,1)S(1)}, bf16[512,544]{0,1:T(8,128)(2,1)}, u32[]{:S(2)}) copy-start(bf16[512,544]{0,1:T(8,128)(2,1)} %param.25) | copy-start | bytes 1671172
  0.7 9.2 %copy-start.9 = (bf16[256,512]{1,0:T(8,128)(2,1)S(1)}, bf16[256,512]{1,0:T(8,128)(2,1)}, u32[]{:S(2)}) copy-start(bf16[256,512]{1,0:T(8,128)(2,1)} %param.21) | copy-start | bytes 786436
  2.2 15.4 %all-to-all-start = ((bf16[16,40,256]{2,1,0:T(8,128)(2,1)}), bf16[16,40,256]{2,1,0:T(8,128)(2,1)S(1)}, u32[]{:S(2)}, u32[]{:S(2)}) async-start(bf16[16,40,256]{2,1,0:T(8,128)(2,1)} %broadcast_in_dim.45), calls=%async_computation | async-start | bytes 655360 | tf_op jit(solution)/shard_map/all_to_all | solution.py:23
  18.6 7.6 %collective-permute-start = (bf16[16,24,1024]{2,1,0:T(8,128)(2,1)S(1)}, bf16[16,24,1024]{2,1,0:T(8,128)(2,1)S(1)}, u32[]{:S(2)}, u32[]{:S(2)}) collective-permute-start(bf16[16,24,1024]{2,1,0:T(8,128)(2,1)S(1)} %broadcast_select_fusion), channel_id=1, source_target_pairs={{0,16},{16,0},{1,17},{17,1},{2,18},{18,2},{3,19},{19,3},{4,20},{20... | collective-permute-start | bytes 2359304 | tf_op jit(solution)/shard_map/ppermute | solution.py:27
  26.7 49.0 %copy-start.6 = (bf16[3,20,512]{2,1,0:T(8,128)(2,1)S(1)}, bf16[3,20,512]{2,1,0:T(8,128)(2,1)}, u32[]{:S(2)}) copy-start(bf16[3,20,512]{2,1,0:T(8,128)(2,1)} %param.22) | copy-start | bytes 184324
  26.7 48.9 %copy-start.13 = (f32[4,512]{1,0:T(4,128)S(1)}, f32[4,512]{1,0:T(4,128)}, u32[]{:S(2)}) copy-start(f32[4,512]{1,0:T(4,128)} %param.23) | copy-start | bytes 24580
  26.7 15.0 %collective-permute-start.1 = (bf16[8,24,1024]{2,1,0:T(8,128)(2,1)S(1)}, bf16[8,24,1024]{2,1,0:T(8,128)(2,1)S(1)}, u32[]{:S(2)}, u32[]{:S(2)}) collective-permute-start(bf16[8,24,1024]{2,1,0:T(8,128)(2,1)S(1)} %slice.124), channel_id=1, source_target_pairs={{0,32},{16,496},{32,0},{48,80},{64,96},{80,48},{96,64},{112,144},{... | collective-permute-start | bytes 1179656 | tf_op jit(solution)/shard_map/ppermute | solution.py:36
  41.8 33.9 %copy-start.12 = (f32[512]{0:T(512)S(1)}, f32[512]{0:T(512)}, u32[]{:S(2)}) copy-start(f32[512]{0:T(512)} %param.24) | copy-start | bytes 6148
  76.0 14.5 %copy-start.3 = (bf16[512,512]{1,0:T(8,128)(2,1)S(1)}, bf16[512,512]{1,0:T(8,128)(2,1)}, u32[]{:S(2)}) copy-start(bf16[512,512]{1,0:T(8,128)(2,1)} %param.26) | copy-start | bytes 1572868
  76.0 14.5 %copy-start.14 = (f32[512]{0:T(512)S(1)}, f32[512]{0:T(512)}, u32[]{:S(2)}) copy-start(f32[512]{0:T(512)} %param.27) | copy-start | bytes 6148
  76.8 14.0 %copy-start.2 = (f32[20,16,512]{2,1,0:T(8,128)S(1)}, f32[20,16,512]{2,1,0:T(8,128)}, u32[]{:S(2)}) copy-start(f32[20,16,512]{2,1,0:T(8,128)} %param.29) | copy-start | bytes 1966084
  76.8 13.4 %all-to-all-start.2 = ((bf16[16,20,544]{2,1,0:T(8,128)(2,1)}), bf16[16,20,544]{2,1,0:T(8,128)(2,1)S(1)}, u32[]{:S(2)}, u32[]{:S(2)}) async-start(bf16[16,20,544]{2,1,0:T(8,128)(2,1)} %broadcast_in_dim.89), calls=%async_computation.2 | async-start | bytes 983040 | tf_op jit(solution)/shard_map/all_to_all | solution.py:23
  110.9 11.4 %collective-permute-start.2 = (bf16[16,20,512]{2,1,0:T(8,128)(2,1)S(1)}, bf16[16,20,512]{2,1,0:T(8,128)(2,1)S(1)}, u32[]{:S(2)}, u32[]{:S(2)}) collective-permute-start(bf16[16,20,512]{2,1,0:T(8,128)(2,1)S(1)} %reshape.128), channel_id=1, source_target_pairs={{0,16},{16,0},{1,17},{17,1},{2,18},{18,2},{3,19},{19,3},{4,20},{20... | collective-permute-start | bytes 983048 | tf_op jit(solution)/shard_map/ppermute | solution.py:27
  123.3 12.3 %copy-start.10 = (bf16[40,256]{1,0:T(8,128)(2,1)S(1)}, bf16[40,256]{1,0:T(8,128)(2,1)}, u32[]{:S(2)}) copy-start(bf16[40,256]{1,0:T(8,128)(2,1)} %param.18) | copy-start | bytes 61444
  123.7 16.2 %copy-start.4 = (bf16[256,768]{1,0:T(8,128)(2,1)S(1)}, bf16[256,768]{1,0:T(8,128)(2,1)}, u32[]{:S(2)}) copy-start(bf16[256,768]{1,0:T(8,128)(2,1)} %param.34) | copy-start | bytes 1179652
  123.7 16.2 %copy-start.5 = (bf16[256,768]{1,0:T(8,128)(2,1)S(1)}, bf16[256,768]{1,0:T(8,128)(2,1)}, u32[]{:S(2)}) copy-start(bf16[256,768]{1,0:T(8,128)(2,1)} %param.33) | copy-start | bytes 1179652
  136.4 11.3 %all-to-all-start.5 = ((bf16[16,40,256]{2,1,0:T(8,128)(2,1)}), bf16[16,40,256]{2,1,0:T(8,128)(2,1)S(1)}, u32[]{:S(2)}, u32[]{:S(2)}) async-start(bf16[16,40,256]{2,1,0:T(8,128)(2,1)} %broadcast_in_dim.92), calls=%async_computation.5 | async-start | bytes 655360 | tf_op jit(solution)/shard_map/all_to_all | solution.py:23
  148.6 6.8 %collective-permute-start.3 = (bf16[16,128,256]{2,1,0:T(8,128)(2,1)S(1)}, bf16[16,128,256]{2,1,0:T(8,128)(2,1)S(1)}, u32[]{:S(2)}, u32[]{:S(2)}) collective-permute-start(bf16[16,128,256]{2,1,0:T(8,128)(2,1)S(1)} %fusion.2), channel_id=1, source_target_pairs={{0,16},{16,0},{1,17},{17,1},{2,18},{18,2},{3,19},{19,3},{4,20},{20... | collective-permute-start | bytes 3145736 | tf_op jit(solution)/shard_map/ppermute | solution.py:27
  155.7 12.1 %collective-permute-start.4 = (bf16[8,128,256]{2,1,0:T(8,128)(2,1)S(1)}, bf16[8,128,256]{2,1,0:T(8,128)(2,1)S(1)}, u32[]{:S(2)}, u32[]{:S(2)}) collective-permute-start(bf16[8,128,256]{2,1,0:T(8,128)(2,1)S(1)} %slice.140), channel_id=1, source_target_pairs={{0,32},{16,496},{32,0},{48,80},{64,96},{80,48},{96,64},{112,144},{... | collective-permute-start | bytes 1572872 | tf_op jit(solution)/shard_map/ppermute | solution.py:36
  200.7 33.1 %copy-start.1 = (bf16[768,256]{1,0:T(8,128)(2,1)S(1)}, bf16[768,256]{1,0:T(8,128)(2,1)}, u32[]{:S(2)}) copy-start(bf16[768,256]{1,0:T(8,128)(2,1)} %param.35) | copy-start | bytes 1179652
  224.6 9.4 %collective-permute-start.6 = (bf16[8,40,384]{2,1,0:T(8,128)(2,1)S(1)}, bf16[8,40,384]{2,1,0:T(8,128)(2,1)S(1)}, u32[]{:S(2)}, u32[]{:S(2)}) collective-permute-start(bf16[8,40,384]{2,1,0:T(8,128)(2,1)S(1)} %all_to_all.49), channel_id=1, source_target_pairs={{0,32},{16,496},{32,0},{48,80},{64,96},{80,48},{96,64},{112,144},{... | collective-permute-start | bytes 737288 | tf_op jit(solution)/shard_map/ppermute | solution.py:36
  226.7 13.3 %collective-permute-start.5 = (bf16[8,40,384]{2,1,0:T(8,128)(2,1)S(1)}, bf16[8,40,384]{2,1,0:T(8,128)(2,1)S(1)}, u32[]{:S(2)}, u32[]{:S(2)}) collective-permute-start(bf16[8,40,384]{2,1,0:T(8,128)(2,1)S(1)} %all_to_all.49), channel_id=1, source_target_pairs={{0,16},{16,0},{1,17},{17,1},{2,18},{18,2},{3,19},{19,3},{4,20},{20... | collective-permute-start | bytes 737288 | tf_op jit(solution)/shard_map/ppermute | solution.py:27
  234.0 6.9 %collective-permute-start.7 = (bf16[8,40,384]{2,1,0:T(8,128)(2,1)S(1)}, bf16[8,40,384]{2,1,0:T(8,128)(2,1)S(1)}, u32[]{:S(2)}, u32[]{:S(2)}) collective-permute-start(bf16[8,40,384]{2,1,0:T(8,128)(2,1)S(1)} %collective-permute-done.6), channel_id=1, source_target_pairs={{0,16},{16,0},{1,17},{17,1},{2,18},{18,2},{3,19},{19,3},{4,20},{20... | collective-permute-start | bytes 737288 | tf_op jit(solution)/shard_map/ppermute | solution.py:27
  241.9 11.8 %all-to-all-start.8 = ((bf16[16,40,256]{2,1,0:T(8,128)(2,1)}), bf16[16,40,256]{2,1,0:T(8,128)(2,1)S(1)}, u32[]{:S(2)}, u32[]{:S(2)}) async-start(bf16[16,40,256]{2,1,0:T(8,128)(2,1)} %bitcast.21), calls=%async_computation.8 | async-start | bytes 655360 | tf_op jit(solution)/shard_map/all_to_all | solution.py:200
  (6 other events, 32.2 us)

commit v6 on v5

--- a/solution.py
+++ b/solution.py
@@ -14,13 +14,25 @@
 F32 = jnp.float32
 BF16 = jnp.bfloat16
 TENSOR = ("y", "xm", "xp")
-TENSOR_PAIRS = ("xp", "y", "xm")
 RING = ("zh", "zm", "zp")
 PAIRS = ("zh", "zm")
 
 
 def spread(block, axes, count):
     return lax.all_to_all(jnp.broadcast_to(block[None], (count,) + block.shape), axes, 0, 0)
+
+
+def planes(first):
+    groups = []
+    for plane in range(32):
+        parity = (plane // 2) % 2 ^ first
+        tensor = list(range(parity, 16, 2)) + list(range(1 - parity, 16, 2))
+        groups.append([16 * plane + place for place in tensor])
+    return groups
+
+
+def exchange(blocks, first):
+    return lax.all_to_all(blocks, RING + ("c",) + TENSOR, 0, 0, axis_index_groups=planes(first))
 
 
 def swap(block, axis):
@@ -55,10 +67,7 @@
 
 
 def spread_rows(block):
-    rows = spread(block, TENSOR_PAIRS, 16)
-    low, high = rows[:8], rows[8:]
-    even = lax.axis_index("zp") == 0
-    return jnp.concatenate([jnp.where(even, high, low), jnp.where(even, low, high)], axis=0)
+    return exchange(jnp.broadcast_to(block[None], (16,) + block.shape), 1)
 
 
 def reduce_rows(block, gain, weight):
@@ -131,7 +140,7 @@
     up_weight,
     down_weight,
 ):
-    core, pair = lax.axis_index("c"), lax.axis_index("zp")
+    core = lax.axis_index("c")
     inner_dev = in_x_weight.shape[1]
     own_rows = conv_state.shape[1]
     token_rows, token_cols = tokens.shape
@@ -189,18 +198,9 @@
 
     near_terms = down(near, swap(near, "c"))
     next_terms = down(next_to, swap(next_to, "c"))
-    down_terms = jnp.concatenate(
-        [
-            jnp.where(pair == 0, near_terms, next_terms),
-            jnp.where(pair == 0, next_terms, near_terms),
-        ],
-        axis=0,
-    )
+    down_terms = jnp.concatenate([near_terms, next_terms], axis=0).astype(BF16)
     down_own = jnp.sum(
-        lax.all_to_all(
-            down_terms.astype(BF16).reshape(16, token_rows, token_cols), TENSOR_PAIRS, 0, 0
-        ).astype(F32),
-        axis=0,
+        exchange(down_terms.reshape(16, token_rows, token_cols), 0).astype(F32), axis=0
     )
     mixed = (residual.astype(F32) + down_own).astype(BF16)
     return (mixed, window[1:], new_state)

time: 255 us -> 254 us (level)
    all_to_all x3 -> x1, waiting for transfers between devices: 25 us -> 9 us  [spread(): lax.all_to_all(jnp.broadcast_to(block[None], (count,) + block.shape), axe...]
    all_to_all x1 -> x3, waiting for transfers between devices: 7.6 us -> 21.5 us  [exchange(): lax.all_to_all(blocks, RING + ('c',) + TENSOR, 0, 0, axis_index_groups=pl...]
    all_to_all x1 -> x3, starting transfers between devices: 3.54 us -> 15 us  [exchange(): lax.all_to_all(blocks, RING + ('c',) + TENSOR, 0, 0, axis_index_groups=pl...]
    all_to_all x3 -> x1, starting transfers between devices: 14.8 us -> 4.71 us  [spread(): lax.all_to_all(jnp.broadcast_to(block[None], (count,) + block.shape), axe...]
where the time goes in v6:
time: 254 us; the launch traced here: 253 us
  blocking collectives  119 us (47%)
  starting transfers between devices  70.9 us (28%)
  waiting for transfers between devices  47.4 us (19%)
  other arithmetic  5.93 us (2%)
  local copies, waits for them, and re-layouts  4.86 us (2%)
  matrix products  3.42 us (1%)
    all_to_all x2, blocking collectives, spread(): lax.all_to_all(jnp.broadcast_to(block[None], (count,) + block.shape), axe...  42.3 us
    all_to_all x1, blocking collectives, reduce_wide_rows(): sums = jnp.sum(lax.all_to_all(total, PAIRS, 0, 0).astype(F32), axis=0)  32.5 us
    all_to_all x1, blocking collectives, reduce_rows(): sums = jnp.sum(lax.all_to_all(total, PAIRS, 0, 0).astype(F32), axis=0)  31.9 us
    ppermute x5, starting transfers between devices, swap(): return lax.ppermute(block, axis, [(0, 1), (1, 0)])  31.9 us
    all_to_all x3, waiting for transfers between devices, exchange(): lax.all_to_all(blocks, RING + ('c',) + TENSOR, 0, 0, axis_index_groups=pl...  21.5 us
    ppermute x3, starting transfers between devices, swap_pairs(): return lax.ppermute(block, RING + ('c',), moves)  19.3 us
    all_to_all x3, starting transfers between devices, exchange(): lax.all_to_all(blocks, RING + ('c',) + TENSOR, 0, 0, axis_index_groups=pl...  15 us
    all_to_all x1, blocking collectives, on_device(): lax.all_to_all(out_terms.reshape(16, token_rows, token_cols), TENSOR, 0, 0)  12.4 us
  transfers between devices with their start and end apart: 12, of which 10 were waited for; matrix products, arithmetic and copies ran while one was open for 1% of the time, Pallas kernels for 0%

profile of v6, /device:TPU:1, one launch (start us, length us, event | category | flops | bytes accessed | tf_op | source)
XLA Modules:
  0.0 252.9 jit_solution(9650212726224670416)
XLA Ops:
  2.2 7.8 %all-to-all-start = ((bf16[16,40,256]{2,1,0:T(8,128)(2,1)}), bf16[16,40,256]{2,1,0:T(8,128)(2,1)S(1)}, u32[]{:S(2)}, u32[]{:S(2)}) async-start(bf16[16,40,256]{2,1,0:T(8,128)(2,1)} %broadcast_in_dim.45), calls=%async_computation | async-start | bytes 655360 | tf_op jit(solution)/shard_map/all_to_all | solution.py:35
  10.1 7.0 %all-to-all-done = bf16[16,40,256]{2,1,0:T(8,128)(2,1)S(1)} async-done(((bf16[16,40,256]{2,1,0:T(8,128)(2,1)}), bf16[16,40,256]{2,1,0:T(8,128)(2,1)S(1)}, u32[]{:S(2)}, u32[]{:S(2)}) %all-to-all-start) | async-done | bytes 327712 | tf_op jit(solution)/shard_map/all_to_all | solution.py:35
  17.9 4.9 %collective-permute-start = (bf16[16,24,1024]{2,1,0:T(8,128)(2,1)S(1)}, bf16[16,24,1024]{2,1,0:T(8,128)(2,1)S(1)}, u32[]{:S(2)}, u32[]{:S(2)}) collective-permute-start(bf16[16,24,1024]{2,1,0:T(8,128)(2,1)S(1)} %broadcast_select_fusion), channel_id=1, source_target_pairs={{0,16},{16,0},{1,17},{17,1},{2,18},{18,2},{3,19},{19,3},{4,20},{20... | collective-permute-start | bytes 2359304 | tf_op jit(solution)/shard_map/ppermute | solution.py:39
  25.3 11.1 %collective-permute-start.1 = (bf16[8,24,1024]{2,1,0:T(8,128)(2,1)S(1)}, bf16[8,24,1024]{2,1,0:T(8,128)(2,1)S(1)}, u32[]{:S(2)}, u32[]{:S(2)}) collective-permute-start(bf16[8,24,1024]{2,1,0:T(8,128)(2,1)S(1)} %slice.106), channel_id=1, source_target_pairs={{0,32},{16,496},{32,0},{48,80},{64,96},{80,48},{96,64},{112,144},{... | collective-permute-start | bytes 1179656 | tf_op jit(solution)/shard_map/ppermute | solution.py:48
  36.5 5.2 %collective-permute-done.1 = bf16[8,24,1024]{2,1,0:T(8,128)(2,1)S(1)} collective-permute-done((bf16[8,24,1024]{2,1,0:T(8,128)(2,1)S(1)}, bf16[8,24,1024]{2,1,0:T(8,128)(2,1)S(1)}, u32[]{:S(2)}, u32[]{:S(2)}) %collective-permute-start.1) | collective-permute-done | bytes 393248 | tf_op jit(solution)/shard_map/ppermute | solution.py:48
  41.8 31.9 %all_to_all.45 = bf16[8,24,1024]{2,1,0:T(8,128)(2,1)S(1)} all-to-all(bf16[8,24,1024]{2,1,0:T(8,128)(2,1)S(1)} %add_convert_fusion.3), channel_id=1, replica_groups=mesh['zh'=4,'zm'=2,'zp'=2,'c'=2,'y'=4,'xm'=2,'xp'=2] {'zh','zm'}, dimensions={0} | all-to-all | bytes 786432 | tf_op jit(solution)/shard_map/all_to_all | solution.py:92
  75.0 4.7 %all-to-all-start.2 = ((bf16[16,20,544]{2,1,0:T(8,128)(2,1)}), bf16[16,20,544]{2,1,0:T(8,128)(2,1)S(1)}, u32[]{:S(2)}, u32[]{:S(2)}) async-start(bf16[16,20,544]{2,1,0:T(8,128)(2,1)} %broadcast_in_dim.89), calls=%async_computation.2 | async-start | bytes 983040 | tf_op jit(solution)/shard_map/all_to_all | solution.py:22
  79.8 9.0 %all-to-all-done.2 = bf16[16,20,544]{2,1,0:T(8,128)(2,1)S(1)} async-done(((bf16[16,20,544]{2,1,0:T(8,128)(2,1)}), bf16[16,20,544]{2,1,0:T(8,128)(2,1)S(1)}, u32[]{:S(2)}, u32[]{:S(2)}) %all-to-all-start.2) | async-done | bytes 348192 | tf_op jit(solution)/shard_map/all_to_all | solution.py:22
  90.7 18.9 %all_to_all.46 = bf16[16,16,640]{2,1,0:T(8,128)(2,1)S(1)} all-to-all(bf16[16,16,640]{2,1,0:T(8,128)(2,1)S(1)} %broadcast_in_dim.91), channel_id=1, replica_groups=mesh['zh'=4,'zm'=2,'zp'=2,'c'=2,'y'=4,'xm'=2,'xp'=2] {'zh','zm','zp'}, dimensions={0} | all-to-all | bytes 655360 | tf_op jit(solution)/shard_map/all_to_all | solution.py:22
  109.9 9.9 %collective-permute-start.2 = (bf16[16,20,512]{2,1,0:T(8,128)(2,1)S(1)}, bf16[16,20,512]{2,1,0:T(8,128)(2,1)S(1)}, u32[]{:S(2)}, u32[]{:S(2)}) collective-permute-start(bf16[16,20,512]{2,1,0:T(8,128)(2,1)S(1)} %reshape.127), channel_id=1, source_target_pairs={{0,16},{16,0},{1,17},{17,1},{2,18},{18,2},{3,19},{19,3},{4,20},{20... | collective-permute-start | bytes 983048 | tf_op jit(solution)/shard_map/ppermute | solution.py:39
  122.5 12.4 %all_to_all.47 = bf16[16,40,256]{2,1,0:T(8,128)(2,1)S(1)} all-to-all(bf16[16,40,256]{2,1,0:T(8,128)(2,1)S(1)} %bitcast.54), channel_id=1, replica_groups=mesh['zh'=4,'zm'=2,'zp'=2,'c'=2,'y'=4,'xm'=2,'xp'=2] {'y','xm','xp'}, dimensions={0} | all-to-all | bytes 655360 | tf_op jit(solution)/shard_map/all_to_all | solution.py:181
  135.7 3.7 %all-to-all-start.5 = ((bf16[16,40,256]{2,1,0:T(8,128)(2,1)}), bf16[16,40,256]{2,1,0:T(8,128)(2,1)S(1)}, u32[]{:S(2)}, u32[]{:S(2)}) async-start(bf16[16,40,256]{2,1,0:T(8,128)(2,1)} %broadcast_in_dim.92), calls=%async_computation.5 | async-start | bytes 655360 | tf_op jit(solution)/shard_map/all_to_all | solution.py:35
  139.5 6.9 %all-to-all-done.5 = bf16[16,40,256]{2,1,0:T(8,128)(2,1)S(1)} async-done(((bf16[16,40,256]{2,1,0:T(8,128)(2,1)}), bf16[16,40,256]{2,1,0:T(8,128)(2,1)S(1)}, u32[]{:S(2)}, u32[]{:S(2)}) %all-to-all-start.5) | async-done | bytes 327712 | tf_op jit(solution)/shard_map/all_to_all | solution.py:35
  147.3 4.5 %collective-permute-start.3 = (bf16[16,128,256]{2,1,0:T(8,128)(2,1)S(1)}, bf16[16,128,256]{2,1,0:T(8,128)(2,1)S(1)}, u32[]{:S(2)}, u32[]{:S(2)}) collective-permute-start(bf16[16,128,256]{2,1,0:T(8,128)(2,1)S(1)} %fusion.4), channel_id=1, source_target_pairs={{0,16},{16,0},{1,17},{17,1},{2,18},{18,2},{3,19},{19,3},{4,20},{20... | collective-permute-start | bytes 3145736 | tf_op jit(solution)/shard_map/ppermute | solution.py:39
  152.2 1.8 collective-permute-done.3
  154.4 5.2 %collective-permute-start.4 = (bf16[8,128,256]{2,1,0:T(8,128)(2,1)S(1)}, bf16[8,128,256]{2,1,0:T(8,128)(2,1)S(1)}, u32[]{:S(2)}, u32[]{:S(2)}) collective-permute-start(bf16[8,128,256]{2,1,0:T(8,128)(2,1)S(1)} %slice.120), channel_id=1, source_target_pairs={{0,32},{16,496},{32,0},{48,80},{64,96},{80,48},{96,64},{112,144},{... | collective-permute-start | bytes 1572872 | tf_op jit(solution)/shard_map/ppermute | solution.py:48
  159.6 6.6 %collective-permute-done.4 = bf16[8,128,256]{2,1,0:T(8,128)(2,1)S(1)} collective-permute-done((bf16[8,128,256]{2,1,0:T(8,128)(2,1)S(1)}, bf16[8,128,256]{2,1,0:T(8,128)(2,1)S(1)}, u32[]{:S(2)}, u32[]{:S(2)}) %collective-permute-start.4) | collective-permute-done | bytes 524320 | tf_op jit(solution)/shard_map/ppermute | solution.py:48
  166.3 32.5 %all_to_all.48 = bf16[8,128,256]{2,1,0:T(8,128)(2,1)S(1)} all-to-all(bf16[8,128,256]{2,1,0:T(8,128)(2,1)S(1)} %add_convert_fusion.2), channel_id=1, replica_groups=mesh['zh'=4,'zm'=2,'zp'=2,'c'=2,'y'=4,'xm'=2,'xp'=2] {'zh','zm'}, dimensions={0} | all-to-all | bytes 1048576 | tf_op jit(solution)/shard_map/all_to_all | solution.py:118
  199.1 23.4 %all_to_all.49 = bf16[8,40,384]{2,1,0:T(8,128)(2,1)S(1)} all-to-all(bf16[8,40,384]{2,1,0:T(8,128)(2,1)S(1)} %broadcast_in_dim.93), channel_id=1, replica_groups=mesh['zh'=4,'zm'=2,'zp'=2,'c'=2,'y'=4,'xm'=2,'xp'=2] {'zh','zm'}, dimensions={0} | all-to-all | bytes 491520 | tf_op jit(solution)/shard_map/all_to_all | solution.py:22
  222.5 2.9 %collective-permute-start.6 = (bf16[8,40,384]{2,1,0:T(8,128)(2,1)S(1)}, bf16[8,40,384]{2,1,0:T(8,128)(2,1)S(1)}, u32[]{:S(2)}, u32[]{:S(2)}) collective-permute-start(bf16[8,40,384]{2,1,0:T(8,128)(2,1)S(1)} %all_to_all.49), channel_id=1, source_target_pairs={{0,32},{16,496},{32,0},{48,80},{64,96},{80,48},{96,64},{112,144},{... | collective-permute-start | bytes 737288 | tf_op jit(solution)/shard_map/ppermute | solution.py:48
  225.4 6.7 %collective-permute-start.5 = (bf16[8,40,384]{2,1,0:T(8,128)(2,1)S(1)}, bf16[8,40,384]{2,1,0:T(8,128)(2,1)S(1)}, u32[]{:S(2)}, u32[]{:S(2)}) collective-permute-start(bf16[8,40,384]{2,1,0:T(8,128)(2,1)S(1)} %all_to_all.49), channel_id=1, source_target_pairs={{0,16},{16,0},{1,17},{17,1},{2,18},{18,2},{3,19},{19,3},{4,20},{20... | collective-permute-start | bytes 737288 | tf_op jit(solution)/shard_map/ppermute | solution.py:39
  232.4 5.9 %collective-permute-start.7 = (bf16[8,40,384]{2,1,0:T(8,128)(2,1)S(1)}, bf16[8,40,384]{2,1,0:T(8,128)(2,1)S(1)}, u32[]{:S(2)}, u32[]{:S(2)}) collective-permute-start(bf16[8,40,384]{2,1,0:T(8,128)(2,1)S(1)} %collective-permute-done.6), channel_id=1, source_target_pairs={{0,16},{16,0},{1,17},{17,1},{2,18},{18,2},{3,19},{19,3},{4,20},{20... | collective-permute-start | bytes 737288 | tf_op jit(solution)/shard_map/ppermute | solution.py:39
  240.4 3.5 %all-to-all-start.8 = ((bf16[16,40,256]{2,1,0:T(8,128)(2,1)}), bf16[16,40,256]{2,1,0:T(8,128)(2,1)S(1)}, u32[]{:S(2)}, u32[]{:S(2)}) async-start(bf16[16,40,256]{2,1,0:T(8,128)(2,1)} %bitcast.21), calls=%async_computation.8 | async-start | bytes 655360 | tf_op jit(solution)/shard_map/all_to_all | solution.py:35
  244.6 7.6 %all-to-all-done.8 = bf16[16,40,256]{2,1,0:T(8,128)(2,1)S(1)} async-done(((bf16[16,40,256]{2,1,0:T(8,128)(2,1)}), bf16[16,40,256]{2,1,0:T(8,128)(2,1)S(1)}, u32[]{:S(2)}, u32[]{:S(2)}) %all-to-all-start.8) | async-done | bytes 327712 | tf_op jit(solution)/shard_map/all_to_all | solution.py:35
  (103 shorter events, 17.6 us)
Async XLA Ops:
  0.6 73.2 %copy-start = (bf16[512,544]{0,1:T(8,128)(2,1)S(1)}, bf16[512,544]{0,1:T(8,128)(2,1)}, u32[]{:S(2)}) copy-start(bf16[512,544]{0,1:T(8,128)(2,1)} %param.25) | copy-start | bytes 1671172
  2.2 14.9 %all-to-all-start = ((bf16[16,40,256]{2,1,0:T(8,128)(2,1)}), bf16[16,40,256]{2,1,0:T(8,128)(2,1)S(1)}, u32[]{:S(2)}, u32[]{:S(2)}) async-start(bf16[16,40,256]{2,1,0:T(8,128)(2,1)} %broadcast_in_dim.45), calls=%async_computation | async-start | bytes 655360 | tf_op jit(solution)/shard_map/all_to_all | solution.py:35
  17.9 6.8 %collective-permute-start = (bf16[16,24,1024]{2,1,0:T(8,128)(2,1)S(1)}, bf16[16,24,1024]{2,1,0:T(8,128)(2,1)S(1)}, u32[]{:S(2)}, u32[]{:S(2)}) collective-permute-start(bf16[16,24,1024]{2,1,0:T(8,128)(2,1)S(1)} %broadcast_select_fusion), channel_id=1, source_target_pairs={{0,16},{16,0},{1,17},{17,1},{2,18},{18,2},{3,19},{19,3},{4,20},{20... | collective-permute-start | bytes 2359304 | tf_op jit(solution)/shard_map/ppermute | solution.py:39
  25.3 48.6 %copy-start.6 = (bf16[3,20,512]{2,1,0:T(8,128)(2,1)S(1)}, bf16[3,20,512]{2,1,0:T(8,128)(2,1)}, u32[]{:S(2)}) copy-start(bf16[3,20,512]{2,1,0:T(8,128)(2,1)} %param.22) | copy-start | bytes 184324
  25.3 48.5 %copy-start.13 = (f32[4,512]{1,0:T(4,128)S(1)}, f32[4,512]{1,0:T(4,128)}, u32[]{:S(2)}) copy-start(f32[4,512]{1,0:T(4,128)} %param.23) | copy-start | bytes 24580
  25.3 16.3 %collective-permute-start.1 = (bf16[8,24,1024]{2,1,0:T(8,128)(2,1)S(1)}, bf16[8,24,1024]{2,1,0:T(8,128)(2,1)S(1)}, u32[]{:S(2)}, u32[]{:S(2)}) collective-permute-start(bf16[8,24,1024]{2,1,0:T(8,128)(2,1)S(1)} %slice.106), channel_id=1, source_target_pairs={{0,32},{16,496},{32,0},{48,80},{64,96},{80,48},{96,64},{112,144},{... | collective-permute-start | bytes 1179656 | tf_op jit(solution)/shard_map/ppermute | solution.py:48
  41.7 32.1 %copy-start.12 = (f32[512]{0:T(512)S(1)}, f32[512]{0:T(512)}, u32[]{:S(2)}) copy-start(f32[512]{0:T(512)} %param.24) | copy-start | bytes 6148
  74.2 14.9 %copy-start.3 = (bf16[512,512]{1,0:T(8,128)(2,1)S(1)}, bf16[512,512]{1,0:T(8,128)(2,1)}, u32[]{:S(2)}) copy-start(bf16[512,512]{1,0:T(8,128)(2,1)} %param.26) | copy-start | bytes 1572868
  74.2 14.9 %copy-start.14 = (f32[512]{0:T(512)S(1)}, f32[512]{0:T(512)}, u32[]{:S(2)}) copy-start(f32[512]{0:T(512)} %param.27) | copy-start | bytes 6148
  75.0 14.4 %copy-start.2 = (f32[20,16,512]{2,1,0:T(8,128)S(1)}, f32[20,16,512]{2,1,0:T(8,128)}, u32[]{:S(2)}) copy-start(f32[20,16,512]{2,1,0:T(8,128)} %param.29) | copy-start | bytes 1966084
  75.0 13.8 %all-to-all-start.2 = ((bf16[16,20,544]{2,1,0:T(8,128)(2,1)}), bf16[16,20,544]{2,1,0:T(8,128)(2,1)S(1)}, u32[]{:S(2)}, u32[]{:S(2)}) async-start(bf16[16,20,544]{2,1,0:T(8,128)(2,1)} %broadcast_in_dim.89), calls=%async_computation.2 | async-start | bytes 983040 | tf_op jit(solution)/shard_map/all_to_all | solution.py:22
  109.9 11.3 %collective-permute-start.2 = (bf16[16,20,512]{2,1,0:T(8,128)(2,1)S(1)}, bf16[16,20,512]{2,1,0:T(8,128)(2,1)S(1)}, u32[]{:S(2)}, u32[]{:S(2)}) collective-permute-start(bf16[16,20,512]{2,1,0:T(8,128)(2,1)S(1)} %reshape.127), channel_id=1, source_target_pairs={{0,16},{16,0},{1,17},{17,1},{2,18},{18,2},{3,19},{19,3},{4,20},{20... | collective-permute-start | bytes 983048 | tf_op jit(solution)/shard_map/ppermute | solution.py:39
  122.2 12.8 %copy-start.10 = (bf16[40,256]{1,0:T(8,128)(2,1)S(1)}, bf16[40,256]{1,0:T(8,128)(2,1)}, u32[]{:S(2)}) copy-start(bf16[40,256]{1,0:T(8,128)(2,1)} %param.18) | copy-start | bytes 61444
  122.5 16.9 %copy-start.4 = (bf16[256,768]{1,0:T(8,128)(2,1)S(1)}, bf16[256,768]{1,0:T(8,128)(2,1)}, u32[]{:S(2)}) copy-start(bf16[256,768]{1,0:T(8,128)(2,1)} %param.34) | copy-start | bytes 1179652
  122.5 16.9 %copy-start.5 = (bf16[256,768]{1,0:T(8,128)(2,1)S(1)}, bf16[256,768]{1,0:T(8,128)(2,1)}, u32[]{:S(2)}) copy-start(bf16[256,768]{1,0:T(8,128)(2,1)} %param.33) | copy-start | bytes 1179652
  135.7 10.7 %copy-start.17 = (f32[256]{0:T(256)S(1)}, f32[256]{0:T(256)}, u32[]{:S(2)}) copy-start(f32[256]{0:T(256)} %param.32) | copy-start | bytes 3076
  135.7 10.7 %all-to-all-start.5 = ((bf16[16,40,256]{2,1,0:T(8,128)(2,1)}), bf16[16,40,256]{2,1,0:T(8,128)(2,1)S(1)}, u32[]{:S(2)}, u32[]{:S(2)}) async-start(bf16[16,40,256]{2,1,0:T(8,128)(2,1)} %broadcast_in_dim.92), calls=%async_computation.5 | async-start | bytes 655360 | tf_op jit(solution)/shard_map/all_to_all | solution.py:35
  147.3 6.7 %collective-permute-start.3 = (bf16[16,128,256]{2,1,0:T(8,128)(2,1)S(1)}, bf16[16,128,256]{2,1,0:T(8,128)(2,1)S(1)}, u32[]{:S(2)}, u32[]{:S(2)}) collective-permute-start(bf16[16,128,256]{2,1,0:T(8,128)(2,1)S(1)} %fusion.4), channel_id=1, source_target_pairs={{0,16},{16,0},{1,17},{17,1},{2,18},{18,2},{3,19},{19,3},{4,20},{20... | collective-permute-start | bytes 3145736 | tf_op jit(solution)/shard_map/ppermute | solution.py:39
  154.4 11.8 %collective-permute-start.4 = (bf16[8,128,256]{2,1,0:T(8,128)(2,1)S(1)}, bf16[8,128,256]{2,1,0:T(8,128)(2,1)S(1)}, u32[]{:S(2)}, u32[]{:S(2)}) collective-permute-start(bf16[8,128,256]{2,1,0:T(8,128)(2,1)S(1)} %slice.120), channel_id=1, source_target_pairs={{0,32},{16,496},{32,0},{48,80},{64,96},{80,48},{96,64},{112,144},{... | collective-permute-start | bytes 1572872 | tf_op jit(solution)/shard_map/ppermute | solution.py:48
  198.8 33.3 %copy-start.1 = (bf16[768,256]{1,0:T(8,128)(2,1)S(1)}, bf16[768,256]{1,0:T(8,128)(2,1)}, u32[]{:S(2)}) copy-start(bf16[768,256]{1,0:T(8,128)(2,1)} %param.35) | copy-start | bytes 1179652
  222.5 9.9 %collective-permute-start.6 = (bf16[8,40,384]{2,1,0:T(8,128)(2,1)S(1)}, bf16[8,40,384]{2,1,0:T(8,128)(2,1)S(1)}, u32[]{:S(2)}, u32[]{:S(2)}) collective-permute-start(bf16[8,40,384]{2,1,0:T(8,128)(2,1)S(1)} %all_to_all.49), channel_id=1, source_target_pairs={{0,32},{16,496},{32,0},{48,80},{64,96},{80,48},{96,64},{112,144},{... | collective-permute-start | bytes 737288 | tf_op jit(solution)/shard_map/ppermute | solution.py:48
  225.4 13.1 %collective-permute-start.5 = (bf16[8,40,384]{2,1,0:T(8,128)(2,1)S(1)}, bf16[8,40,384]{2,1,0:T(8,128)(2,1)S(1)}, u32[]{:S(2)}, u32[]{:S(2)}) collective-permute-start(bf16[8,40,384]{2,1,0:T(8,128)(2,1)S(1)} %all_to_all.49), channel_id=1, source_target_pairs={{0,16},{16,0},{1,17},{17,1},{2,18},{18,2},{3,19},{19,3},{4,20},{20... | collective-permute-start | bytes 737288 | tf_op jit(solution)/shard_map/ppermute | solution.py:39
  232.4 7.0 %collective-permute-start.7 = (bf16[8,40,384]{2,1,0:T(8,128)(2,1)S(1)}, bf16[8,40,384]{2,1,0:T(8,128)(2,1)S(1)}, u32[]{:S(2)}, u32[]{:S(2)}) collective-permute-start(bf16[8,40,384]{2,1,0:T(8,128)(2,1)S(1)} %collective-permute-done.6), channel_id=1, source_target_pairs={{0,16},{16,0},{1,17},{17,1},{2,18},{18,2},{3,19},{19,3},{4,20},{20... | collective-permute-start | bytes 737288 | tf_op jit(solution)/shard_map/ppermute | solution.py:39
  240.4 11.8 %all-to-all-start.8 = ((bf16[16,40,256]{2,1,0:T(8,128)(2,1)}), bf16[16,40,256]{2,1,0:T(8,128)(2,1)S(1)}, u32[]{:S(2)}, u32[]{:S(2)}) async-start(bf16[16,40,256]{2,1,0:T(8,128)(2,1)} %bitcast.21), calls=%async_computation.8 | async-start | bytes 655360 | tf_op jit(solution)/shard_map/all_to_all | solution.py:35
  (6 other events, 34.3 us)

commit v7 on v6

--- a/solution.py
+++ b/solution.py
@@ -170,17 +170,20 @@
     gated = (readout * jax.nn.silu(gate_z.astype(F32))).astype(BF16)
 
     dense = lax.optimization_barrier(gated).reshape(16, own_rows * inner_dev // 16)
-    same = spread(dense, RING, 16).reshape(16, own_rows, inner_dev)
-    same = lax.optimization_barrier(same)
-    other = swap(same, "c")
-    rows = jnp.concatenate(
-        [jnp.where(core == 0, same, other), jnp.where(core == 0, other, same)], axis=1
-    )
-    out_terms = dot(rows.reshape(16 * token_rows, inner_dev), out_weight).astype(BF16)
-    out_own = jnp.sum(
-        lax.all_to_all(out_terms.reshape(16, token_rows, token_cols), TENSOR, 0, 0).astype(F32),
-        axis=0,
-    )
+    near = spread(dense, PAIRS, 8).reshape(8, own_rows, inner_dev)
+    near = lax.optimization_barrier(near)
+
+    def out(same):
+        rows = jnp.concatenate([same, swap(same, "c")], axis=1)
+        return dot(rows.reshape(8 * token_rows, inner_dev), out_weight).astype(BF16)
+
+    next_to = swap_pairs(near)
+    out_terms = jnp.concatenate([out(near), out(next_to)], axis=0)
+    out_sum = jnp.sum(
+        exchange(out_terms.reshape(16, token_rows, token_cols), 0).astype(F32), axis=0
+    )
+    turned = jnp.concatenate([out_sum[own_rows:], out_sum[:own_rows]], axis=0)
+    out_own = jnp.where(core == 0, out_sum, turned)
     residual = (tokens.astype(F32) + out_own).astype(BF16)
 
     sums, second = reduce_wide_rows(residual, post_gain, gate_weight, up_weight)

time: 254 us -> 255 us (level)
  waiting for transfers between devices: 47.4 us -> 58.3 us
  starting transfers between devices: 70.9 us -> 62.2 us
    ppermute x3 -> x4, waiting for transfers between devices: 11.7 us -> 22.8 us  [swap_pairs(): return lax.ppermute(block, RING + ('c',), moves)]
    ppermute x5 -> x6, starting transfers between devices: 31.9 us -> 24.5 us  [swap(): return lax.ppermute(block, axis, [(0, 1), (1, 0)])]
    ppermute x3 -> x4, starting transfers between devices: 19.3 us -> 16.9 us  [swap_pairs(): return lax.ppermute(block, RING + ('c',), moves)]
    ppermute x5 -> x6, waiting for transfers between devices: 5.19 us -> 5 us  [swap(): return lax.ppermute(block, axis, [(0, 1), (1, 0)])]
  transfers between devices with their start and end apart: 12 -> 14, of which waited for: 10 -> 12; matrix products, arithmetic and copies ran while one was open for 1% -> 1% of each run, Pallas kernels for 0% -> 0%
where the time goes in v7:
time: 255 us; the launch traced here: 254 us
  blocking collectives  119 us (47%)
  starting transfers between devices  62.2 us (24%)
  waiting for transfers between devices  58.3 us (23%)
  other arithmetic  5.9 us (2%)
  local copies, waits for them, and re-layouts  3.91 us (2%)
  matrix products  3.58 us (1%)
    all_to_all x2, blocking collectives, spread(): lax.all_to_all(jnp.broadcast_to(block[None], (count,) + block.shape), axe...  40.6 us
    all_to_all x1, blocking collectives, reduce_wide_rows(): sums = jnp.sum(lax.all_to_all(total, PAIRS, 0, 0).astype(F32), axis=0)  34.8 us
    all_to_all x1, blocking collectives, reduce_rows(): sums = jnp.sum(lax.all_to_all(total, PAIRS, 0, 0).astype(F32), axis=0)  31.9 us
    ppermute x6, starting transfers between devices, swap(): return lax.ppermute(block, axis, [(0, 1), (1, 0)])  24.5 us
    ppermute x4, waiting for transfers between devices, swap_pairs(): return lax.ppermute(block, RING + ('c',), moves)  22.8 us
    all_to_all x3, waiting for transfers between devices, exchange(): lax.all_to_all(blocks, RING + ('c',) + TENSOR, 0, 0, axis_index_groups=pl...  21.5 us
    ppermute x4, starting transfers between devices, swap_pairs(): return lax.ppermute(block, RING + ('c',), moves)  16.9 us
    all_to_all x3, starting transfers between devices, exchange(): lax.all_to_all(blocks, RING + ('c',) + TENSOR, 0, 0, axis_index_groups=pl...  16.1 us
  transfers between devices with their start and end apart: 14, of which 12 were waited for; matrix products, arithmetic and copies ran while one was open for 1% of the time, Pallas kernels for 0%

profile of v7, /device:TPU:1, one launch (start us, length us, event | category | flops | bytes accessed | tf_op | source)
XLA Modules:
  0.0 254.0 jit_solution(4133103780549996094)
XLA Ops:
  2.2 7.8 %all-to-all-start = ((bf16[16,40,256]{2,1,0:T(8,128)(2,1)}), bf16[16,40,256]{2,1,0:T(8,128)(2,1)S(1)}, u32[]{:S(2)}, u32[]{:S(2)}) async-start(bf16[16,40,256]{2,1,0:T(8,128)(2,1)} %broadcast_in_dim.45), calls=%async_computation | async-start | bytes 655360 | tf_op jit(solution)/shard_map/all_to_all | solution.py:35
  10.1 7.0 %all-to-all-done = bf16[16,40,256]{2,1,0:T(8,128)(2,1)S(1)} async-done(((bf16[16,40,256]{2,1,0:T(8,128)(2,1)}), bf16[16,40,256]{2,1,0:T(8,128)(2,1)S(1)}, u32[]{:S(2)}, u32[]{:S(2)}) %all-to-all-start) | async-done | bytes 327712 | tf_op jit(solution)/shard_map/all_to_all | solution.py:35
  17.9 4.9 %collective-permute-start = (bf16[16,24,1024]{2,1,0:T(8,128)(2,1)S(1)}, bf16[16,24,1024]{2,1,0:T(8,128)(2,1)S(1)}, u32[]{:S(2)}, u32[]{:S(2)}) collective-permute-start(bf16[16,24,1024]{2,1,0:T(8,128)(2,1)S(1)} %broadcast_select_fusion), channel_id=1, source_target_pairs={{0,16},{16,0},{1,17},{17,1},{2,18},{18,2},{3,19},{19,3},{4,20},{20... | collective-permute-start | bytes 2359304 | tf_op jit(solution)/shard_map/ppermute | solution.py:39
  25.3 11.1 %collective-permute-start.1 = (bf16[8,24,1024]{2,1,0:T(8,128)(2,1)S(1)}, bf16[8,24,1024]{2,1,0:T(8,128)(2,1)S(1)}, u32[]{:S(2)}, u32[]{:S(2)}) collective-permute-start(bf16[8,24,1024]{2,1,0:T(8,128)(2,1)S(1)} %slice.114), channel_id=1, source_target_pairs={{0,32},{16,496},{32,0},{48,80},{64,96},{80,48},{96,64},{112,144},{... | collective-permute-start | bytes 1179656 | tf_op jit(solution)/shard_map/ppermute | solution.py:48
  36.5 5.2 %collective-permute-done.1 = bf16[8,24,1024]{2,1,0:T(8,128)(2,1)S(1)} collective-permute-done((bf16[8,24,1024]{2,1,0:T(8,128)(2,1)S(1)}, bf16[8,24,1024]{2,1,0:T(8,128)(2,1)S(1)}, u32[]{:S(2)}, u32[]{:S(2)}) %collective-permute-start.1) | collective-permute-done | bytes 393248 | tf_op jit(solution)/shard_map/ppermute | solution.py:48
  41.8 31.9 %all_to_all.45 = bf16[8,24,1024]{2,1,0:T(8,128)(2,1)S(1)} all-to-all(bf16[8,24,1024]{2,1,0:T(8,128)(2,1)S(1)} %add_convert_fusion.3), channel_id=1, replica_groups=mesh['zh'=4,'zm'=2,'zp'=2,'c'=2,'y'=4,'xm'=2,'xp'=2] {'zh','zm'}, dimensions={0} | all-to-all | bytes 786432 | tf_op jit(solution)/shard_map/all_to_all | solution.py:92
  75.0 4.7 %all-to-all-start.2 = ((bf16[16,20,544]{2,1,0:T(8,128)(2,1)}), bf16[16,20,544]{2,1,0:T(8,128)(2,1)S(1)}, u32[]{:S(2)}, u32[]{:S(2)}) async-start(bf16[16,20,544]{2,1,0:T(8,128)(2,1)} %broadcast_in_dim.89), calls=%async_computation.2 | async-start | bytes 983040 | tf_op jit(solution)/shard_map/all_to_all | solution.py:22
  79.8 9.0 %all-to-all-done.2 = bf16[16,20,544]{2,1,0:T(8,128)(2,1)S(1)} async-done(((bf16[16,20,544]{2,1,0:T(8,128)(2,1)}), bf16[16,20,544]{2,1,0:T(8,128)(2,1)S(1)}, u32[]{:S(2)}, u32[]{:S(2)}) %all-to-all-start.2) | async-done | bytes 348192 | tf_op jit(solution)/shard_map/all_to_all | solution.py:22
  90.7 19.0 %all_to_all.46 = bf16[8,16,640]{2,1,0:T(8,128)(2,1)S(1)} all-to-all(bf16[8,16,640]{2,1,0:T(8,128)(2,1)S(1)} %broadcast_in_dim.91), channel_id=1, replica_groups=mesh['zh'=4,'zm'=2,'zp'=2,'c'=2,'y'=4,'xm'=2,'xp'=2] {'zh','zm'}, dimensions={0} | all-to-all | bytes 327680 | tf_op jit(solution)/shard_map/all_to_all | solution.py:22
  109.8 6.6 %collective-permute-start.2 = (bf16[8,20,512]{2,1,0:T(8,128)(2,1)S(1)}, bf16[8,20,512]{2,1,0:T(8,128)(2,1)S(1)}, u32[]{:S(2)}, u32[]{:S(2)}) collective-permute-start(bf16[8,20,512]{2,1,0:T(8,128)(2,1)S(1)} %reshape.130), channel_id=1, source_target_pairs={{0,16},{16,0},{1,17},{17,1},{2,18},{18,2},{3,19},{19,3},{4,20},{20... | collective-permute-start | bytes 491528 | tf_op jit(solution)/shard_map/ppermute | solution.py:39
  116.5 1.9 collective-permute-start.3
  118.5 5.6 %collective-permute-done.3 = bf16[8,20,512]{2,1,0:T(8,128)(2,1)S(1)} collective-permute-done((bf16[8,20,512]{2,1,0:T(8,128)(2,1)S(1)}, bf16[8,20,512]{2,1,0:T(8,128)(2,1)S(1)}, u32[]{:S(2)}, u32[]{:S(2)}) %collective-permute-start.3) | collective-permute-done | bytes 163872 | tf_op jit(solution)/shard_map/ppermute | solution.py:48
  127.8 11.5 %all_to_all.47 = bf16[16,40,256]{2,1,0:T(8,128)(2,1)S(1)} all-to-all(bf16[16,40,256]{2,1,0:T(8,128)(2,1)S(1)} %bitcast.58), channel_id=1, replica_groups={{0,2,4,6,8,10,12,14,1,3,5,7,9,11,13,15},{16,18,20,22,24,26,28,30,17,19,..., dimensions={0} | all-to-all | bytes 655360 | tf_op jit(solution)/shard_map/all_to_all | solution.py:35
  140.2 4.0 %all-to-all-start.5 = ((bf16[16,40,256]{2,1,0:T(8,128)(2,1)}), bf16[16,40,256]{2,1,0:T(8,128)(2,1)S(1)}, u32[]{:S(2)}, u32[]{:S(2)}) async-start(bf16[16,40,256]{2,1,0:T(8,128)(2,1)} %broadcast_in_dim.92), calls=%async_computation.5 | async-start | bytes 655360 | tf_op jit(solution)/shard_map/all_to_all | solution.py:35
  144.3 6.9 %all-to-all-done.5 = bf16[16,40,256]{2,1,0:T(8,128)(2,1)S(1)} async-done(((bf16[16,40,256]{2,1,0:T(8,128)(2,1)}), bf16[16,40,256]{2,1,0:T(8,128)(2,1)S(1)}, u32[]{:S(2)}, u32[]{:S(2)}) %all-to-all-start.5) | async-done | bytes 327712 | tf_op jit(solution)/shard_map/all_to_all | solution.py:35
  152.0 4.8 %collective-permute-start.5 = (bf16[16,128,256]{2,1,0:T(8,128)(2,1)S(1)}, bf16[16,128,256]{2,1,0:T(8,128)(2,1)S(1)}, u32[]{:S(2)}, u32[]{:S(2)}) collective-permute-start(bf16[16,128,256]{2,1,0:T(8,128)(2,1)S(1)} %fusion.4), channel_id=1, source_target_pairs={{0,16},{16,0},{1,17},{17,1},{2,18},{18,2},{3,19},{19,3},{4,20},{20... | collective-permute-start | bytes 3145736 | tf_op jit(solution)/shard_map/ppermute | solution.py:39
  161.4 9.2 %collective-permute-done.6 = bf16[8,128,256]{2,1,0:T(8,128)(2,1)S(1)} collective-permute-done((bf16[8,128,256]{2,1,0:T(8,128)(2,1)S(1)}, bf16[8,128,256]{2,1,0:T(8,128)(2,1)S(1)}, u32[]{:S(2)}, u32[]{:S(2)}) %collective-permute-start.6) | collective-permute-done | bytes 524320 | tf_op jit(solution)/shard_map/ppermute | solution.py:48
  170.7 34.8 %all_to_all.48 = bf16[8,128,256]{2,1,0:T(8,128)(2,1)S(1)} all-to-all(bf16[8,128,256]{2,1,0:T(8,128)(2,1)S(1)} %add_convert_fusion.2), channel_id=1, replica_groups=mesh['zh'=4,'zm'=2,'zp'=2,'c'=2,'y'=4,'xm'=2,'xp'=2] {'zh','zm'}, dimensions={0} | all-to-all | bytes 1048576 | tf_op jit(solution)/shard_map/all_to_all | solution.py:118
  205.8 21.6 %all_to_all.49 = bf16[8,40,384]{2,1,0:T(8,128)(2,1)S(1)} all-to-all(bf16[8,40,384]{2,1,0:T(8,128)(2,1)S(1)} %broadcast_in_dim.93), channel_id=1, replica_groups=mesh['zh'=4,'zm'=2,'zp'=2,'c'=2,'y'=4,'xm'=2,'xp'=2] {'zh','zm'}, dimensions={0} | all-to-all | bytes 491520 | tf_op jit(solution)/shard_map/all_to_all | solution.py:22
  229.3 3.1 %collective-permute-start.7 = (bf16[8,40,384]{2,1,0:T(8,128)(2,1)S(1)}, bf16[8,40,384]{2,1,0:T(8,128)(2,1)S(1)}, u32[]{:S(2)}, u32[]{:S(2)}) collective-permute-start(bf16[8,40,384]{2,1,0:T(8,128)(2,1)S(1)} %all_to_all.49), channel_id=1, source_target_pairs={{0,16},{16,0},{1,17},{17,1},{2,18},{18,2},{3,19},{19,3},{4,20},{20... | collective-permute-start | bytes 737288 | tf_op jit(solution)/shard_map/ppermute | solution.py:39
  232.7 2.8 %collective-permute-done.8 = bf16[8,40,384]{2,1,0:T(8,128)(2,1)S(1)} collective-permute-done((bf16[8,40,384]{2,1,0:T(8,128)(2,1)S(1)}, bf16[8,40,384]{2,1,0:T(8,128)(2,1)S(1)}, u32[]{:S(2)}, u32[]{:S(2)}) %collective-permute-start.8) | collective-permute-done | bytes 245792 | tf_op jit(solution)/shard_map/ppermute | solution.py:48
  235.5 3.1 %collective-permute-start.9 = (bf16[8,40,384]{2,1,0:T(8,128)(2,1)S(1)}, bf16[8,40,384]{2,1,0:T(8,128)(2,1)S(1)}, u32[]{:S(2)}, u32[]{:S(2)}) collective-permute-start(bf16[8,40,384]{2,1,0:T(8,128)(2,1)S(1)} %collective-permute-done.8), channel_id=1, source_target_pairs={{0,16},{16,0},{1,17},{17,1},{2,18},{18,2},{3,19},{19,3},{4,20},{20... | collective-permute-start | bytes 737288 | tf_op jit(solution)/shard_map/ppermute | solution.py:39
  240.7 4.3 %all-to-all-start.8 = ((bf16[16,40,256]{2,1,0:T(8,128)(2,1)}), bf16[16,40,256]{2,1,0:T(8,128)(2,1)S(1)}, u32[]{:S(2)}, u32[]{:S(2)}) async-start(bf16[16,40,256]{2,1,0:T(8,128)(2,1)} %bitcast.22), calls=%async_computation.8 | async-start | bytes 655360 | tf_op jit(solution)/shard_map/all_to_all | solution.py:35
  245.7 7.6 %all-to-all-done.8 = bf16[16,40,256]{2,1,0:T(8,128)(2,1)S(1)} async-done(((bf16[16,40,256]{2,1,0:T(8,128)(2,1)}), bf16[16,40,256]{2,1,0:T(8,128)(2,1)S(1)}, u32[]{:S(2)}, u32[]{:S(2)}) %all-to-all-start.8) | async-done | bytes 327712 | tf_op jit(solution)/shard_map/all_to_all | solution.py:35
  (110 shorter events, 24.1 us)
Async XLA Ops:
  0.6 73.2 %copy-start = (bf16[512,544]{0,1:T(8,128)(2,1)S(1)}, bf16[512,544]{0,1:T(8,128)(2,1)}, u32[]{:S(2)}) copy-start(bf16[512,544]{0,1:T(8,128)(2,1)} %param.25) | copy-start | bytes 1671172
  2.2 14.9 %all-to-all-start = ((bf16[16,40,256]{2,1,0:T(8,128)(2,1)}), bf16[16,40,256]{2,1,0:T(8,128)(2,1)S(1)}, u32[]{:S(2)}, u32[]{:S(2)}) async-start(bf16[16,40,256]{2,1,0:T(8,128)(2,1)} %broadcast_in_dim.45), calls=%async_computation | async-start | bytes 655360 | tf_op jit(solution)/shard_map/all_to_all | solution.py:35
  17.9 6.8 %collective-permute-start = (bf16[16,24,1024]{2,1,0:T(8,128)(2,1)S(1)}, bf16[16,24,1024]{2,1,0:T(8,128)(2,1)S(1)}, u32[]{:S(2)}, u32[]{:S(2)}) collective-permute-start(bf16[16,24,1024]{2,1,0:T(8,128)(2,1)S(1)} %broadcast_select_fusion), channel_id=1, source_target_pairs={{0,16},{16,0},{1,17},{17,1},{2,18},{18,2},{3,19},{19,3},{4,20},{20... | collective-permute-start | bytes 2359304 | tf_op jit(solution)/shard_map/ppermute | solution.py:39
  25.3 48.6 %copy-start.7 = (bf16[3,20,512]{2,1,0:T(8,128)(2,1)S(1)}, bf16[3,20,512]{2,1,0:T(8,128)(2,1)}, u32[]{:S(2)}) copy-start(bf16[3,20,512]{2,1,0:T(8,128)(2,1)} %param.22) | copy-start | bytes 184324
  25.3 48.5 %copy-start.13 = (f32[4,512]{1,0:T(4,128)S(1)}, f32[4,512]{1,0:T(4,128)}, u32[]{:S(2)}) copy-start(f32[4,512]{1,0:T(4,128)} %param.23) | copy-start | bytes 24580
  25.3 16.3 %collective-permute-start.1 = (bf16[8,24,1024]{2,1,0:T(8,128)(2,1)S(1)}, bf16[8,24,1024]{2,1,0:T(8,128)(2,1)S(1)}, u32[]{:S(2)}, u32[]{:S(2)}) collective-permute-start(bf16[8,24,1024]{2,1,0:T(8,128)(2,1)S(1)} %slice.114), channel_id=1, source_target_pairs={{0,32},{16,496},{32,0},{48,80},{64,96},{80,48},{96,64},{112,144},{... | collective-permute-start | bytes 1179656 | tf_op jit(solution)/shard_map/ppermute | solution.py:48
  41.7 32.1 %copy-start.12 = (f32[512]{0:T(512)S(1)}, f32[512]{0:T(512)}, u32[]{:S(2)}) copy-start(f32[512]{0:T(512)} %param.24) | copy-start | bytes 6148
  74.2 14.9 %copy-start.4 = (bf16[512,512]{1,0:T(8,128)(2,1)S(1)}, bf16[512,512]{1,0:T(8,128)(2,1)}, u32[]{:S(2)}) copy-start(bf16[512,512]{1,0:T(8,128)(2,1)} %param.26) | copy-start | bytes 1572868
  74.2 14.9 %copy-start.14 = (f32[512]{0:T(512)S(1)}, f32[512]{0:T(512)}, u32[]{:S(2)}) copy-start(f32[512]{0:T(512)} %param.27) | copy-start | bytes 6148
  75.0 13.8 %all-to-all-start.2 = ((bf16[16,20,544]{2,1,0:T(8,128)(2,1)}), bf16[16,20,544]{2,1,0:T(8,128)(2,1)S(1)}, u32[]{:S(2)}, u32[]{:S(2)}) async-start(bf16[16,20,544]{2,1,0:T(8,128)(2,1)} %broadcast_in_dim.89), calls=%async_computation.2 | async-start | bytes 983040 | tf_op jit(solution)/shard_map/all_to_all | solution.py:22
  90.5 35.5 %copy-start.2 = (bf16[512,256]{1,0:T(8,128)(2,1)S(1)}, bf16[512,256]{1,0:T(8,128)(2,1)}, u32[]{:S(2)}) copy-start(bf16[512,256]{1,0:T(8,128)(2,1)} %param.31) | copy-start | bytes 786436
  109.8 8.6 %collective-permute-start.2 = (bf16[8,20,512]{2,1,0:T(8,128)(2,1)S(1)}, bf16[8,20,512]{2,1,0:T(8,128)(2,1)S(1)}, u32[]{:S(2)}, u32[]{:S(2)}) collective-permute-start(bf16[8,20,512]{2,1,0:T(8,128)(2,1)S(1)} %reshape.130), channel_id=1, source_target_pairs={{0,16},{16,0},{1,17},{17,1},{2,18},{18,2},{3,19},{19,3},{4,20},{20... | collective-permute-start | bytes 491528 | tf_op jit(solution)/shard_map/ppermute | solution.py:39
  116.5 7.6 %collective-permute-start.3 = (bf16[8,20,512]{2,1,0:T(8,128)(2,1)S(1)}, bf16[8,20,512]{2,1,0:T(8,128)(2,1)S(1)}, u32[]{:S(2)}, u32[]{:S(2)}) collective-permute-start(bf16[8,20,512]{2,1,0:T(8,128)(2,1)S(1)} %reshape.130), channel_id=1, source_target_pairs={{0,32},{16,496},{32,0},{48,80},{64,96},{80,48},{96,64},{112,144},{... | collective-permute-start | bytes 491528 | tf_op jit(solution)/shard_map/ppermute | solution.py:48
  124.1 3.3 %collective-permute-start.4 = (bf16[8,20,512]{2,1,0:T(8,128)(2,1)S(1)}, bf16[8,20,512]{2,1,0:T(8,128)(2,1)S(1)}, u32[]{:S(2)}, u32[]{:S(2)}) collective-permute-start(bf16[8,20,512]{2,1,0:T(8,128)(2,1)S(1)} %collective-permute-done.3), channel_id=1, source_target_pairs={{0,16},{16,0},{1,17},{17,1},{2,18},{18,2},{3,19},{19,3},{4,20},{20... | collective-permute-start | bytes 491528 | tf_op jit(solution)/shard_map/ppermute | solution.py:39
  127.8 16.4 %copy-start.5 = (bf16[256,768]{1,0:T(8,128)(2,1)S(1)}, bf16[256,768]{1,0:T(8,128)(2,1)}, u32[]{:S(2)}) copy-start(bf16[256,768]{1,0:T(8,128)(2,1)} %param.34) | copy-start | bytes 1179652
  127.8 16.4 %copy-start.6 = (bf16[256,768]{1,0:T(8,128)(2,1)S(1)}, bf16[256,768]{1,0:T(8,128)(2,1)}, u32[]{:S(2)}) copy-start(bf16[256,768]{1,0:T(8,128)(2,1)} %param.33) | copy-start | bytes 1179652
  140.2 11.0 %all-to-all-start.5 = ((bf16[16,40,256]{2,1,0:T(8,128)(2,1)}), bf16[16,40,256]{2,1,0:T(8,128)(2,1)S(1)}, u32[]{:S(2)}, u32[]{:S(2)}) async-start(bf16[16,40,256]{2,1,0:T(8,128)(2,1)} %broadcast_in_dim.92), calls=%async_computation.5 | async-start | bytes 655360 | tf_op jit(solution)/shard_map/all_to_all | solution.py:35
  152.0 7.1 %collective-permute-start.5 = (bf16[16,128,256]{2,1,0:T(8,128)(2,1)S(1)}, bf16[16,128,256]{2,1,0:T(8,128)(2,1)S(1)}, u32[]{:S(2)}, u32[]{:S(2)}) collective-permute-start(bf16[16,128,256]{2,1,0:T(8,128)(2,1)S(1)} %fusion.4), channel_id=1, source_target_pairs={{0,16},{16,0},{1,17},{17,1},{2,18},{18,2},{3,19},{19,3},{4,20},{20... | collective-permute-start | bytes 3145736 | tf_op jit(solution)/shard_map/ppermute | solution.py:39
  159.5 11.1 %collective-permute-start.6 = (bf16[8,128,256]{2,1,0:T(8,128)(2,1)S(1)}, bf16[8,128,256]{2,1,0:T(8,128)(2,1)S(1)}, u32[]{:S(2)}, u32[]{:S(2)}) collective-permute-start(bf16[8,128,256]{2,1,0:T(8,128)(2,1)S(1)} %slice.130), channel_id=1, source_target_pairs={{0,32},{16,496},{32,0},{48,80},{64,96},{80,48},{96,64},{112,144},{... | collective-permute-start | bytes 1572872 | tf_op jit(solution)/shard_map/ppermute | solution.py:48
  205.6 26.9 %copy-start.1 = (bf16[768,256]{1,0:T(8,128)(2,1)S(1)}, bf16[768,256]{1,0:T(8,128)(2,1)}, u32[]{:S(2)}) copy-start(bf16[768,256]{1,0:T(8,128)(2,1)} %param.35) | copy-start | bytes 1179652
  227.4 8.1 %collective-permute-start.8 = (bf16[8,40,384]{2,1,0:T(8,128)(2,1)S(1)}, bf16[8,40,384]{2,1,0:T(8,128)(2,1)S(1)}, u32[]{:S(2)}, u32[]{:S(2)}) collective-permute-start(bf16[8,40,384]{2,1,0:T(8,128)(2,1)S(1)} %all_to_all.49), channel_id=1, source_target_pairs={{0,32},{16,496},{32,0},{48,80},{64,96},{80,48},{96,64},{112,144},{... | collective-permute-start | bytes 737288 | tf_op jit(solution)/shard_map/ppermute | solution.py:48
  229.3 9.6 %collective-permute-start.7 = (bf16[8,40,384]{2,1,0:T(8,128)(2,1)S(1)}, bf16[8,40,384]{2,1,0:T(8,128)(2,1)S(1)}, u32[]{:S(2)}, u32[]{:S(2)}) collective-permute-start(bf16[8,40,384]{2,1,0:T(8,128)(2,1)S(1)} %all_to_all.49), channel_id=1, source_target_pairs={{0,16},{16,0},{1,17},{17,1},{2,18},{18,2},{3,19},{19,3},{4,20},{20... | collective-permute-start | bytes 737288 | tf_op jit(solution)/shard_map/ppermute | solution.py:39
  235.5 4.2 %collective-permute-start.9 = (bf16[8,40,384]{2,1,0:T(8,128)(2,1)S(1)}, bf16[8,40,384]{2,1,0:T(8,128)(2,1)S(1)}, u32[]{:S(2)}, u32[]{:S(2)}) collective-permute-start(bf16[8,40,384]{2,1,0:T(8,128)(2,1)S(1)} %collective-permute-done.8), channel_id=1, source_target_pairs={{0,16},{16,0},{1,17},{17,1},{2,18},{18,2},{3,19},{19,3},{4,20},{20... | collective-permute-start | bytes 737288 | tf_op jit(solution)/shard_map/ppermute | solution.py:39
  240.7 12.6 %all-to-all-start.8 = ((bf16[16,40,256]{2,1,0:T(8,128)(2,1)}), bf16[16,40,256]{2,1,0:T(8,128)(2,1)S(1)}, u32[]{:S(2)}, u32[]{:S(2)}) async-start(bf16[16,40,256]{2,1,0:T(8,128)(2,1)} %bitcast.22), calls=%async_computation.8 | async-start | bytes 655360 | tf_op jit(solution)/shard_map/all_to_all | solution.py:35
  (8 other events, 70.3 us)

commit v8 on v6

--- a/solution.py
+++ b/solution.py
@@ -77,18 +77,21 @@
     columns = weight.shape[1]
     padded = size + 4
     spare = lax.broadcasted_iota(jnp.int32, (1, padded, columns), 1) == size
-    low, high = rows[:, :size], rows[:, size:]
 
     def partial(part):
         wide = jnp.pad(part, ((0, 0), (0, 4), (0, 0))).astype(F32)
-        scaled = (wide * gain[None, None, :]).astype(BF16).reshape(16 * padded, -1)
+        scaled = (wide * gain[None, None, :]).astype(BF16).reshape(8 * padded, -1)
         squares = jnp.sum(wide * wide, axis=2).astype(BF16)[:, None, :]
         marks = jnp.pad(squares, ((0, 0), (0, 0), (0, columns - padded)))
-        return jnp.where(spare, marks, dot(scaled, weight).astype(BF16).reshape(16, padded, columns))
-
-    received = swap(partial(jnp.where(first_core, high, low)), "c")
-    both = add(partial(jnp.where(first_core, low, high)), received)
-    total = add(both[8:], swap_pairs(both[:8]))
+        return jnp.where(spare, marks, dot(scaled, weight).astype(BF16).reshape(8, padded, columns))
+
+    def chip_sum(part):
+        low, high = part[:, :size], part[:, size:]
+        received = swap(partial(jnp.where(first_core, high, low)), "c")
+        return add(partial(jnp.where(first_core, low, high)), received)
+
+    met = swap_pairs(chip_sum(rows[:8]))
+    total = add(chip_sum(rows[8:]), met)
     sums = jnp.sum(lax.all_to_all(total, PAIRS, 0, 0).astype(F32), axis=0)
     return sums[:size], sums[size, :size]
 
@@ -97,24 +100,28 @@
     core = lax.axis_index("c")
     size, depth = block.shape
     rows = spread_rows(block)
-    wide = rows.astype(F32)
-    scaled = (wide * gain[None, None, :]).astype(BF16).reshape(16 * size, depth)
-    squares = jnp.sum(wide * wide, axis=2).astype(BF16)[:, None, :]
-    marks = jnp.pad(squares, ((0, 0), (0, 7), (0, TILE - size)))
     tiles = left_weight.shape[1] // TILE
 
-    def partial(which):
-        weight = jnp.concatenate(
-            [half_columns(left_weight, which), half_columns(right_weight, which)], axis=1
-        )
-        terms = dot(scaled, weight).astype(BF16).reshape(16, size, tiles * TILE)
-        return jnp.concatenate(
-            [terms[:, :, TILE * k : TILE * k + TILE] for k in range(tiles)] + [marks], axis=1
-        )
-
-    received = swap(partial(1 - core), "c")
-    both = add(partial(core), received)
-    total = add(both[8:], swap_pairs(both[:8]))
+    def chip_sum(part):
+        wide = part.astype(F32)
+        scaled = (wide * gain[None, None, :]).astype(BF16).reshape(8 * size, depth)
+        squares = jnp.sum(wide * wide, axis=2).astype(BF16)[:, None, :]
+        marks = jnp.pad(squares, ((0, 0), (0, 7), (0, TILE - size)))
+
+        def partial(which):
+            weight = jnp.concatenate(
+                [half_columns(left_weight, which), half_columns(right_weight, which)], axis=1
+            )
+            terms = dot(scaled, weight).astype(BF16).reshape(8, size, tiles * TILE)
+            return jnp.concatenate(
+                [terms[:, :, TILE * k : TILE * k + TILE] for k in range(tiles)] + [marks], axis=1
+            )
+
+        received = swap(partial(1 - core), "c")
+        return add(partial(core), received)
+
+    met = swap_pairs(chip_sum(rows[:8]))
+    total = add(chip_sum(rows[8:]), met)
     sums = jnp.sum(lax.all_to_all(total, PAIRS, 0, 0).astype(F32), axis=0)
     columns = [sums[size * k : size * k + size] for k in range(tiles)]
     return jnp.concatenate(columns, axis=1), sums[size * tiles, :size]

time: 254 us -> 254 us (level)
  waiting for transfers between devices: 47.4 us -> 43.5 us
  starting transfers between devices: 70.9 us -> 74.6 us
    ppermute x5 -> x7, starting transfers between devices: 31.9 us -> 35.6 us  [swap(): return lax.ppermute(block, axis, [(0, 1), (1, 0)])]
    ppermute x5 -> x7, waiting for transfers between devices: 5.19 us -> 1.94 us  [swap(): return lax.ppermute(block, axis, [(0, 1), (1, 0)])]
  transfers between devices with their start and end apart: 12 -> 14, of which waited for: 10 -> 8; matrix products, arithmetic and copies ran while one was open for 1% -> 1% of each run, Pallas kernels for 0% -> 0%
where the time goes in v8:
time: 254 us; the launch traced here: 253 us
  blocking collectives  119 us (47%)
  starting transfers between devices  74.6 us (29%)
  waiting for transfers between devices  43.5 us (17%)
  other arithmetic  5.82 us (2%)
  local copies, waits for them, and re-layouts  4.8 us (2%)
  matrix products  4.07 us (2%)
    all_to_all x2, blocking collectives, spread(): lax.all_to_all(jnp.broadcast_to(block[None], (count,) + block.shape), axe...  42.7 us
    ppermute x7, starting transfers between devices, swap(): return lax.ppermute(block, axis, [(0, 1), (1, 0)])  35.6 us
    all_to_all x1, blocking collectives, reduce_wide_rows(): sums = jnp.sum(lax.all_to_all(total, PAIRS, 0, 0).astype(F32), axis=0)  32.5 us
    all_to_all x1, blocking collectives, reduce_rows(): sums = jnp.sum(lax.all_to_all(total, PAIRS, 0, 0).astype(F32), axis=0)  31.8 us
    all_to_all x3, waiting for transfers between devices, exchange(): lax.all_to_all(blocks, RING + ('c',) + TENSOR, 0, 0, axis_index_groups=pl...  21.5 us
    ppermute x3, starting transfers between devices, swap_pairs(): return lax.ppermute(block, RING + ('c',), moves)  19.2 us
    all_to_all x3, starting transfers between devices, exchange(): lax.all_to_all(blocks, RING + ('c',) + TENSOR, 0, 0, axis_index_groups=pl...  15 us
    all_to_all x1, blocking collectives, on_device(): lax.all_to_all(out_terms.reshape(16, token_rows, token_cols), TENSOR, 0, 0)  12.2 us
  transfers between devices with their start and end apart: 14, of which 8 were waited for; matrix products, arithmetic and copies ran while one was open for 1% of the time, Pallas kernels for 0%

profile of v8, /device:TPU:1, one launch (start us, length us, event | category | flops | bytes accessed | tf_op | source)
XLA Modules:
  0.0 253.3 jit_solution(16721907356949351124)
XLA Ops:
  2.2 7.9 %all-to-all-start = ((bf16[16,40,256]{2,1,0:T(8,128)(2,1)}), bf16[16,40,256]{2,1,0:T(8,128)(2,1)S(1)}, u32[]{:S(2)}, u32[]{:S(2)}) async-start(bf16[16,40,256]{2,1,0:T(8,128)(2,1)} %broadcast_in_dim.113), calls=%async_computation | async-start | bytes 655360 | tf_op jit(solution)/shard_map/all_to_all | solution.py:35
  10.2 7.0 %all-to-all-done = bf16[16,40,256]{2,1,0:T(8,128)(2,1)S(1)} async-done(((bf16[16,40,256]{2,1,0:T(8,128)(2,1)}), bf16[16,40,256]{2,1,0:T(8,128)(2,1)S(1)}, u32[]{:S(2)}, u32[]{:S(2)}) %all-to-all-start) | async-done | bytes 327712 | tf_op jit(solution)/shard_map/all_to_all | solution.py:35
  18.3 4.9 %collective-permute-start.1 = (bf16[8,24,1024]{2,1,0:T(8,128)(2,1)S(1)}, bf16[8,24,1024]{2,1,0:T(8,128)(2,1)S(1)}, u32[]{:S(2)}, u32[]{:S(2)}) collective-permute-start(bf16[8,24,1024]{2,1,0:T(8,128)(2,1)S(1)} %get-tuple-element.47), channel_id=1, source_target_pairs={{0,16},{16,0},{1,17},{17,1},{2,18},{18,2},{3,19},{19,3},{4,20},{20... | collective-permute-start | bytes 1179656 | tf_op jit(solution)/shard_map/ppermute | solution.py:39
  23.2 1.9 collective-permute-start
  25.7 11.0 %collective-permute-start.2 = (bf16[8,24,1024]{2,1,0:T(8,128)(2,1)S(1)}, bf16[8,24,1024]{2,1,0:T(8,128)(2,1)S(1)}, u32[]{:S(2)}, u32[]{:S(2)}) collective-permute-start(bf16[8,24,1024]{2,1,0:T(8,128)(2,1)S(1)} %add_convert_fusion.4), channel_id=1, source_target_pairs={{0,32},{16,496},{32,0},{48,80},{64,96},{80,48},{96,64},{112,144},{... | collective-permute-start | bytes 1179656 | tf_op jit(solution)/shard_map/ppermute | solution.py:48
  37.0 4.8 %collective-permute-done.2 = bf16[8,24,1024]{2,1,0:T(8,128)(2,1)S(1)} collective-permute-done((bf16[8,24,1024]{2,1,0:T(8,128)(2,1)S(1)}, bf16[8,24,1024]{2,1,0:T(8,128)(2,1)S(1)}, u32[]{:S(2)}, u32[]{:S(2)}) %collective-permute-start.2) | collective-permute-done | bytes 393248 | tf_op jit(solution)/shard_map/ppermute | solution.py:48
  42.3 31.8 %all_to_all.45 = bf16[8,24,1024]{2,1,0:T(8,128)(2,1)S(1)} all-to-all(bf16[8,24,1024]{2,1,0:T(8,128)(2,1)S(1)} %add_convert_fusion.3), channel_id=1, replica_groups=mesh['zh'=4,'zm'=2,'zp'=2,'c'=2,'y'=4,'xm'=2,'xp'=2] {'zh','zm'}, dimensions={0} | all-to-all | bytes 786432 | tf_op jit(solution)/shard_map/all_to_all | solution.py:95
  75.4 4.7 %all-to-all-start.2 = ((bf16[16,20,544]{2,1,0:T(8,128)(2,1)}), bf16[16,20,544]{2,1,0:T(8,128)(2,1)S(1)}, u32[]{:S(2)}, u32[]{:S(2)}) async-start(bf16[16,20,544]{2,1,0:T(8,128)(2,1)} %broadcast_in_dim.123), calls=%async_computation.2 | async-start | bytes 983040 | tf_op jit(solution)/shard_map/all_to_all | solution.py:22
  80.1 9.0 %all-to-all-done.2 = bf16[16,20,544]{2,1,0:T(8,128)(2,1)S(1)} async-done(((bf16[16,20,544]{2,1,0:T(8,128)(2,1)}), bf16[16,20,544]{2,1,0:T(8,128)(2,1)S(1)}, u32[]{:S(2)}, u32[]{:S(2)}) %all-to-all-start.2) | async-done | bytes 348192 | tf_op jit(solution)/shard_map/all_to_all | solution.py:22
  91.1 19.1 %all_to_all.46 = bf16[16,16,640]{2,1,0:T(8,128)(2,1)S(1)} all-to-all(bf16[16,16,640]{2,1,0:T(8,128)(2,1)S(1)} %broadcast_in_dim.125), channel_id=1, replica_groups=mesh['zh'=4,'zm'=2,'zp'=2,'c'=2,'y'=4,'xm'=2,'xp'=2] {'zh','zm','zp'}, dimensions={0} | all-to-all | bytes 655360 | tf_op jit(solution)/shard_map/all_to_all | solution.py:22
  110.5 9.9 %collective-permute-start.3 = (bf16[16,20,512]{2,1,0:T(8,128)(2,1)S(1)}, bf16[16,20,512]{2,1,0:T(8,128)(2,1)S(1)}, u32[]{:S(2)}, u32[]{:S(2)}) collective-permute-start(bf16[16,20,512]{2,1,0:T(8,128)(2,1)S(1)} %reshape.176), channel_id=1, source_target_pairs={{0,16},{16,0},{1,17},{17,1},{2,18},{18,2},{3,19},{19,3},{4,20},{20... | collective-permute-start | bytes 983048 | tf_op jit(solution)/shard_map/ppermute | solution.py:39
  123.2 12.2 %all_to_all.47 = bf16[16,40,256]{2,1,0:T(8,128)(2,1)S(1)} all-to-all(bf16[16,40,256]{2,1,0:T(8,128)(2,1)S(1)} %bitcast.86), channel_id=1, replica_groups=mesh['zh'=4,'zm'=2,'zp'=2,'c'=2,'y'=4,'xm'=2,'xp'=2] {'y','xm','xp'}, dimensions={0} | all-to-all | bytes 655360 | tf_op jit(solution)/shard_map/all_to_all | solution.py:188
  136.2 3.5 %all-to-all-start.5 = ((bf16[16,40,256]{2,1,0:T(8,128)(2,1)}), bf16[16,40,256]{2,1,0:T(8,128)(2,1)S(1)}, u32[]{:S(2)}, u32[]{:S(2)}) async-start(bf16[16,40,256]{2,1,0:T(8,128)(2,1)} %broadcast_in_dim.126), calls=%async_computation.5 | async-start | bytes 655360 | tf_op jit(solution)/shard_map/all_to_all | solution.py:35
  139.9 6.9 %all-to-all-done.5 = bf16[16,40,256]{2,1,0:T(8,128)(2,1)S(1)} async-done(((bf16[16,40,256]{2,1,0:T(8,128)(2,1)}), bf16[16,40,256]{2,1,0:T(8,128)(2,1)S(1)}, u32[]{:S(2)}, u32[]{:S(2)}) %all-to-all-start.5) | async-done | bytes 327712 | tf_op jit(solution)/shard_map/all_to_all | solution.py:35
  147.4 4.5 %collective-permute-start.5 = (bf16[8,128,256]{2,1,0:T(8,128)(2,1)S(1)}, bf16[8,128,256]{2,1,0:T(8,128)(2,1)S(1)}, u32[]{:S(2)}, u32[]{:S(2)}) collective-permute-start(bf16[8,128,256]{2,1,0:T(8,128)(2,1)S(1)} %fusion.5), channel_id=1, source_target_pairs={{0,16},{16,0},{1,17},{17,1},{2,18},{18,2},{3,19},{19,3},{4,20},{20... | collective-permute-start | bytes 1572872 | tf_op jit(solution)/shard_map/ppermute | solution.py:39
  154.6 5.3 %collective-permute-start.6 = (bf16[8,128,256]{2,1,0:T(8,128)(2,1)S(1)}, bf16[8,128,256]{2,1,0:T(8,128)(2,1)S(1)}, u32[]{:S(2)}, u32[]{:S(2)}) collective-permute-start(bf16[8,128,256]{2,1,0:T(8,128)(2,1)S(1)} %add_convert_fusion.1), channel_id=1, source_target_pairs={{0,32},{16,496},{32,0},{48,80},{64,96},{80,48},{96,64},{112,144},{... | collective-permute-start | bytes 1572872 | tf_op jit(solution)/shard_map/ppermute | solution.py:48
  160.3 6.2 %collective-permute-done.6 = bf16[8,128,256]{2,1,0:T(8,128)(2,1)S(1)} collective-permute-done((bf16[8,128,256]{2,1,0:T(8,128)(2,1)S(1)}, bf16[8,128,256]{2,1,0:T(8,128)(2,1)S(1)}, u32[]{:S(2)}, u32[]{:S(2)}) %collective-permute-start.6) | collective-permute-done | bytes 524320 | tf_op jit(solution)/shard_map/ppermute | solution.py:48
  166.7 32.5 %all_to_all.48 = bf16[8,128,256]{2,1,0:T(8,128)(2,1)S(1)} all-to-all(bf16[8,128,256]{2,1,0:T(8,128)(2,1)S(1)} %add_convert_fusion), channel_id=1, replica_groups=mesh['zh'=4,'zm'=2,'zp'=2,'c'=2,'y'=4,'xm'=2,'xp'=2] {'zh','zm'}, dimensions={0} | all-to-all | bytes 1048576 | tf_op jit(solution)/shard_map/all_to_all | solution.py:125
  199.4 23.6 %all_to_all.49 = bf16[8,40,384]{2,1,0:T(8,128)(2,1)S(1)} all-to-all(bf16[8,40,384]{2,1,0:T(8,128)(2,1)S(1)} %broadcast_in_dim.127), channel_id=1, replica_groups=mesh['zh'=4,'zm'=2,'zp'=2,'c'=2,'y'=4,'xm'=2,'xp'=2] {'zh','zm'}, dimensions={0} | all-to-all | bytes 491520 | tf_op jit(solution)/shard_map/all_to_all | solution.py:22
  223.0 2.9 %collective-permute-start.8 = (bf16[8,40,384]{2,1,0:T(8,128)(2,1)S(1)}, bf16[8,40,384]{2,1,0:T(8,128)(2,1)S(1)}, u32[]{:S(2)}, u32[]{:S(2)}) collective-permute-start(bf16[8,40,384]{2,1,0:T(8,128)(2,1)S(1)} %all_to_all.49), channel_id=1, source_target_pairs={{0,32},{16,496},{32,0},{48,80},{64,96},{80,48},{96,64},{112,144},{... | collective-permute-start | bytes 737288 | tf_op jit(solution)/shard_map/ppermute | solution.py:48
  226.0 6.6 %collective-permute-start.7 = (bf16[8,40,384]{2,1,0:T(8,128)(2,1)S(1)}, bf16[8,40,384]{2,1,0:T(8,128)(2,1)S(1)}, u32[]{:S(2)}, u32[]{:S(2)}) collective-permute-start(bf16[8,40,384]{2,1,0:T(8,128)(2,1)S(1)} %all_to_all.49), channel_id=1, source_target_pairs={{0,16},{16,0},{1,17},{17,1},{2,18},{18,2},{3,19},{19,3},{4,20},{20... | collective-permute-start | bytes 737288 | tf_op jit(solution)/shard_map/ppermute | solution.py:39
  232.9 5.9 %collective-permute-start.9 = (bf16[8,40,384]{2,1,0:T(8,128)(2,1)S(1)}, bf16[8,40,384]{2,1,0:T(8,128)(2,1)S(1)}, u32[]{:S(2)}, u32[]{:S(2)}) collective-permute-start(bf16[8,40,384]{2,1,0:T(8,128)(2,1)S(1)} %collective-permute-done.8), channel_id=1, source_target_pairs={{0,16},{16,0},{1,17},{17,1},{2,18},{18,2},{3,19},{19,3},{4,20},{20... | collective-permute-start | bytes 737288 | tf_op jit(solution)/shard_map/ppermute | solution.py:39
  240.9 3.5 %all-to-all-start.8 = ((bf16[16,40,256]{2,1,0:T(8,128)(2,1)}), bf16[16,40,256]{2,1,0:T(8,128)(2,1)S(1)}, u32[]{:S(2)}, u32[]{:S(2)}) async-start(bf16[16,40,256]{2,1,0:T(8,128)(2,1)} %bitcast.33), calls=%async_computation.8 | async-start | bytes 655360 | tf_op jit(solution)/shard_map/all_to_all | solution.py:35
  245.1 7.6 %all-to-all-done.8 = bf16[16,40,256]{2,1,0:T(8,128)(2,1)S(1)} async-done(((bf16[16,40,256]{2,1,0:T(8,128)(2,1)}), bf16[16,40,256]{2,1,0:T(8,128)(2,1)S(1)}, u32[]{:S(2)}, u32[]{:S(2)}) %all-to-all-start.8) | async-done | bytes 327712 | tf_op jit(solution)/shard_map/all_to_all | solution.py:35
  (116 shorter events, 18.6 us)
Async XLA Ops:
  0.6 73.6 %copy-start = (bf16[512,544]{0,1:T(8,128)(2,1)S(1)}, bf16[512,544]{0,1:T(8,128)(2,1)}, u32[]{:S(2)}) copy-start(bf16[512,544]{0,1:T(8,128)(2,1)} %param.25) | copy-start | bytes 1671172
  0.6 9.5 %copy-start.8 = (bf16[256,512]{1,0:T(8,128)(2,1)S(1)}, bf16[256,512]{1,0:T(8,128)(2,1)}, u32[]{:S(2)}) copy-start(bf16[256,512]{1,0:T(8,128)(2,1)} %param.20) | copy-start | bytes 786436
  2.2 15.0 %all-to-all-start = ((bf16[16,40,256]{2,1,0:T(8,128)(2,1)}), bf16[16,40,256]{2,1,0:T(8,128)(2,1)S(1)}, u32[]{:S(2)}, u32[]{:S(2)}) async-start(bf16[16,40,256]{2,1,0:T(8,128)(2,1)} %broadcast_in_dim.113), calls=%async_computation | async-start | bytes 655360 | tf_op jit(solution)/shard_map/all_to_all | solution.py:35
  18.3 7.1 %collective-permute-start.1 = (bf16[8,24,1024]{2,1,0:T(8,128)(2,1)S(1)}, bf16[8,24,1024]{2,1,0:T(8,128)(2,1)S(1)}, u32[]{:S(2)}, u32[]{:S(2)}) collective-permute-start(bf16[8,24,1024]{2,1,0:T(8,128)(2,1)S(1)} %get-tuple-element.47), channel_id=1, source_target_pairs={{0,16},{16,0},{1,17},{17,1},{2,18},{18,2},{3,19},{19,3},{4,20},{20... | collective-permute-start | bytes 1179656 | tf_op jit(solution)/shard_map/ppermute | solution.py:39
  23.2 13.8 %collective-permute-start = (bf16[8,24,1024]{2,1,0:T(8,128)(2,1)S(1)}, bf16[8,24,1024]{2,1,0:T(8,128)(2,1)S(1)}, u32[]{:S(2)}, u32[]{:S(2)}) collective-permute-start(bf16[8,24,1024]{2,1,0:T(8,128)(2,1)S(1)} %get-tuple-element.46), channel_id=1, source_target_pairs={{0,16},{16,0},{1,17},{17,1},{2,18},{18,2},{3,19},{19,3},{4,20},{20... | collective-permute-start | bytes 1179656 | tf_op jit(solution)/shard_map/ppermute | solution.py:39
  25.7 16.2 %collective-permute-start.2 = (bf16[8,24,1024]{2,1,0:T(8,128)(2,1)S(1)}, bf16[8,24,1024]{2,1,0:T(8,128)(2,1)S(1)}, u32[]{:S(2)}, u32[]{:S(2)}) collective-permute-start(bf16[8,24,1024]{2,1,0:T(8,128)(2,1)S(1)} %add_convert_fusion.4), channel_id=1, source_target_pairs={{0,32},{16,496},{32,0},{48,80},{64,96},{80,48},{96,64},{112,144},{... | collective-permute-start | bytes 1179656 | tf_op jit(solution)/shard_map/ppermute | solution.py:48
  42.2 31.9 %copy-start.6 = (bf16[3,20,512]{2,1,0:T(8,128)(2,1)S(1)}, bf16[3,20,512]{2,1,0:T(8,128)(2,1)}, u32[]{:S(2)}) copy-start(bf16[3,20,512]{2,1,0:T(8,128)(2,1)} %param.22) | copy-start | bytes 184324
  42.3 31.9 %copy-start.13 = (f32[4,512]{1,0:T(4,128)S(1)}, f32[4,512]{1,0:T(4,128)}, u32[]{:S(2)}) copy-start(f32[4,512]{1,0:T(4,128)} %param.23) | copy-start | bytes 24580
  42.3 32.0 %copy-start.12 = (f32[512]{0:T(512)S(1)}, f32[512]{0:T(512)}, u32[]{:S(2)}) copy-start(f32[512]{0:T(512)} %param.24) | copy-start | bytes 6148
  75.3 14.1 %copy-start.3 = (bf16[512,512]{1,0:T(8,128)(2,1)S(1)}, bf16[512,512]{1,0:T(8,128)(2,1)}, u32[]{:S(2)}) copy-start(bf16[512,512]{1,0:T(8,128)(2,1)} %param.26) | copy-start | bytes 1572868
  75.4 14.1 %copy-start.15 = (f32[512]{0:T(512)S(1)}, f32[512]{0:T(512)}, u32[]{:S(2)}) copy-start(f32[512]{0:T(512)} %param.27) | copy-start | bytes 6148
  75.4 13.8 %all-to-all-start.2 = ((bf16[16,20,544]{2,1,0:T(8,128)(2,1)}), bf16[16,20,544]{2,1,0:T(8,128)(2,1)S(1)}, u32[]{:S(2)}, u32[]{:S(2)}) async-start(bf16[16,20,544]{2,1,0:T(8,128)(2,1)} %broadcast_in_dim.123), calls=%async_computation.2 | async-start | bytes 983040 | tf_op jit(solution)/shard_map/all_to_all | solution.py:22
  80.1 9.6 %copy-start.2 = (f32[20,16,512]{2,1,0:T(8,128)S(1)}, f32[20,16,512]{2,1,0:T(8,128)}, u32[]{:S(2)}) copy-start(f32[20,16,512]{2,1,0:T(8,128)} %param.29) | copy-start | bytes 1966084
  110.5 11.3 %collective-permute-start.3 = (bf16[16,20,512]{2,1,0:T(8,128)(2,1)S(1)}, bf16[16,20,512]{2,1,0:T(8,128)(2,1)S(1)}, u32[]{:S(2)}, u32[]{:S(2)}) collective-permute-start(bf16[16,20,512]{2,1,0:T(8,128)(2,1)S(1)} %reshape.176), channel_id=1, source_target_pairs={{0,16},{16,0},{1,17},{17,1},{2,18},{18,2},{3,19},{19,3},{4,20},{20... | collective-permute-start | bytes 983048 | tf_op jit(solution)/shard_map/ppermute | solution.py:39
  123.2 12.3 %copy-start.10 = (bf16[40,256]{1,0:T(8,128)(2,1)S(1)}, bf16[40,256]{1,0:T(8,128)(2,1)}, u32[]{:S(2)}) copy-start(bf16[40,256]{1,0:T(8,128)(2,1)} %param.18) | copy-start | bytes 61444
  136.2 10.6 %all-to-all-start.5 = ((bf16[16,40,256]{2,1,0:T(8,128)(2,1)}), bf16[16,40,256]{2,1,0:T(8,128)(2,1)S(1)}, u32[]{:S(2)}, u32[]{:S(2)}) async-start(bf16[16,40,256]{2,1,0:T(8,128)(2,1)} %broadcast_in_dim.126), calls=%async_computation.5 | async-start | bytes 655360 | tf_op jit(solution)/shard_map/all_to_all | solution.py:35
  147.4 7.1 %collective-permute-start.5 = (bf16[8,128,256]{2,1,0:T(8,128)(2,1)S(1)}, bf16[8,128,256]{2,1,0:T(8,128)(2,1)S(1)}, u32[]{:S(2)}, u32[]{:S(2)}) collective-permute-start(bf16[8,128,256]{2,1,0:T(8,128)(2,1)S(1)} %fusion.5), channel_id=1, source_target_pairs={{0,16},{16,0},{1,17},{17,1},{2,18},{18,2},{3,19},{19,3},{4,20},{20... | collective-permute-start | bytes 1572872 | tf_op jit(solution)/shard_map/ppermute | solution.py:39
  152.2 8.0 %collective-permute-start.4 = (bf16[8,128,256]{2,1,0:T(8,128)(2,1)S(1)}, bf16[8,128,256]{2,1,0:T(8,128)(2,1)S(1)}, u32[]{:S(2)}, u32[]{:S(2)}) collective-permute-start(bf16[8,128,256]{2,1,0:T(8,128)(2,1)S(1)} %fusion.7), channel_id=1, source_target_pairs={{0,16},{16,0},{1,17},{17,1},{2,18},{18,2},{3,19},{19,3},{4,20},{20... | collective-permute-start | bytes 1572872 | tf_op jit(solution)/shard_map/ppermute | solution.py:39
  154.6 11.8 %collective-permute-start.6 = (bf16[8,128,256]{2,1,0:T(8,128)(2,1)S(1)}, bf16[8,128,256]{2,1,0:T(8,128)(2,1)S(1)}, u32[]{:S(2)}, u32[]{:S(2)}) collective-permute-start(bf16[8,128,256]{2,1,0:T(8,128)(2,1)S(1)} %add_convert_fusion.1), channel_id=1, source_target_pairs={{0,32},{16,496},{32,0},{48,80},{64,96},{80,48},{96,64},{112,144},{... | collective-permute-start | bytes 1572872 | tf_op jit(solution)/shard_map/ppermute | solution.py:48
  199.3 33.4 %copy-start.1 = (bf16[768,256]{1,0:T(8,128)(2,1)S(1)}, bf16[768,256]{1,0:T(8,128)(2,1)}, u32[]{:S(2)}) copy-start(bf16[768,256]{1,0:T(8,128)(2,1)} %param.35) | copy-start | bytes 1179652
  223.0 9.9 %collective-permute-start.8 = (bf16[8,40,384]{2,1,0:T(8,128)(2,1)S(1)}, bf16[8,40,384]{2,1,0:T(8,128)(2,1)S(1)}, u32[]{:S(2)}, u32[]{:S(2)}) collective-permute-start(bf16[8,40,384]{2,1,0:T(8,128)(2,1)S(1)} %all_to_all.49), channel_id=1, source_target_pairs={{0,32},{16,496},{32,0},{48,80},{64,96},{80,48},{96,64},{112,144},{... | collective-permute-start | bytes 737288 | tf_op jit(solution)/shard_map/ppermute | solution.py:48
  226.0 13.1 %collective-permute-start.7 = (bf16[8,40,384]{2,1,0:T(8,128)(2,1)S(1)}, bf16[8,40,384]{2,1,0:T(8,128)(2,1)S(1)}, u32[]{:S(2)}, u32[]{:S(2)}) collective-permute-start(bf16[8,40,384]{2,1,0:T(8,128)(2,1)S(1)} %all_to_all.49), channel_id=1, source_target_pairs={{0,16},{16,0},{1,17},{17,1},{2,18},{18,2},{3,19},{19,3},{4,20},{20... | collective-permute-start | bytes 737288 | tf_op jit(solution)/shard_map/ppermute | solution.py:39
  232.9 7.0 %collective-permute-start.9 = (bf16[8,40,384]{2,1,0:T(8,128)(2,1)S(1)}, bf16[8,40,384]{2,1,0:T(8,128)(2,1)S(1)}, u32[]{:S(2)}, u32[]{:S(2)}) collective-permute-start(bf16[8,40,384]{2,1,0:T(8,128)(2,1)S(1)} %collective-permute-done.8), channel_id=1, source_target_pairs={{0,16},{16,0},{1,17},{17,1},{2,18},{18,2},{3,19},{19,3},{4,20},{20... | collective-permute-start | bytes 737288 | tf_op jit(solution)/shard_map/ppermute | solution.py:39
  240.9 11.8 %all-to-all-start.8 = ((bf16[16,40,256]{2,1,0:T(8,128)(2,1)}), bf16[16,40,256]{2,1,0:T(8,128)(2,1)S(1)}, u32[]{:S(2)}, u32[]{:S(2)}) async-start(bf16[16,40,256]{2,1,0:T(8,128)(2,1)} %bitcast.33), calls=%async_computation.8 | async-start | bytes 655360 | tf_op jit(solution)/shard_map/all_to_all | solution.py:35
  (8 other events, 38.5 us)

commit v9 on v6

--- a/solution.py
+++ b/solution.py
@@ -154,12 +154,13 @@
     window = jnp.concatenate([conv_state, inner_x[None]], axis=0)
     conv_pre = jnp.sum(window.astype(F32) * conv_weight[:, None, :], axis=0) + conv_bias[None, :]
     signal = jax.nn.silu(conv_pre).astype(BF16)
-    projected = jnp.sum(
-        spread(dot(signal, proj_weight).astype(BF16), TENSOR, 16).astype(F32), axis=0
-    )
-    delta_low = projected[:, :RANK]
-    input_map = projected[:, RANK : RANK + STATE]
-    output_map = projected[:, RANK + STATE :]
+    terms = dot(signal, proj_weight).astype(BF16)
+    maps = jnp.pad(terms[:, RANK:].reshape(4, -1), ((0, 0), (0, RANK - 8 * own_rows)))
+    packed = jnp.concatenate([terms[:, :RANK], maps], axis=0)
+    projected = jnp.sum(spread(packed, TENSOR, 16).astype(F32), axis=0)
+    delta_low = projected[:own_rows]
+    maps = projected[own_rows:, : 8 * own_rows].reshape(own_rows, 2 * STATE)
+    input_map, output_map = maps[:, :STATE], maps[:, STATE:]
     delta_scale = lax.rsqrt(jnp.mean(delta_low * delta_low, axis=1, keepdims=True) + epsilon)
     delta_norm = (delta_low * delta_scale).astype(BF16)
     delta = jax.nn.softplus(dot(delta_norm, delta_weight) + delta_bias[None, :])

time: 254 us -> 253 us (level)
  no operation moved by 1% of the time
where the time goes in v9:
time: 253 us; the launch traced here: 252 us
  blocking collectives  119 us (47%)
  starting transfers between devices  70.9 us (28%)
  waiting for transfers between devices  46.8 us (18%)
  other arithmetic  5.87 us (2%)
  local copies, waits for them, and re-layouts  4.99 us (2%)
  matrix products  3.43 us (1%)
    all_to_all x2, blocking collectives, spread(): lax.all_to_all(jnp.broadcast_to(block[None], (count,) + block.shape), axe...  41.9 us
    all_to_all x1, blocking collectives, reduce_wide_rows(): sums = jnp.sum(lax.all_to_all(total, PAIRS, 0, 0).astype(F32), axis=0)  32.8 us
    ppermute x5, starting transfers between devices, swap(): return lax.ppermute(block, axis, [(0, 1), (1, 0)])  32.1 us
    all_to_all x1, blocking collectives, reduce_rows(): sums = jnp.sum(lax.all_to_all(total, PAIRS, 0, 0).astype(F32), axis=0)  31.9 us
    all_to_all x3, waiting for transfers between devices, exchange(): lax.all_to_all(blocks, RING + ('c',) + TENSOR, 0, 0, axis_index_groups=pl...  21.5 us
    ppermute x3, starting transfers between devices, swap_pairs(): return lax.ppermute(block, RING + ('c',), moves)  19.1 us
    all_to_all x3, starting transfers between devices, exchange(): lax.all_to_all(blocks, RING + ('c',) + TENSOR, 0, 0, axis_index_groups=pl...  15 us
    all_to_all x1, blocking collectives, on_device(): lax.all_to_all(out_terms.reshape(16, token_rows, token_cols), TENSOR, 0, 0)  12 us
  transfers between devices with their start and end apart: 12, of which 10 were waited for; matrix products, arithmetic and copies ran while one was open for 1% of the time, Pallas kernels for 0%

profile of v9, /device:TPU:1, one launch (start us, length us, event | category | flops | bytes accessed | tf_op | source)
XLA Modules:
  0.0 251.8 jit_solution(3544451601071596786)
XLA Ops:
  2.2 7.8 %all-to-all-start = ((bf16[16,40,256]{2,1,0:T(8,128)(2,1)}), bf16[16,40,256]{2,1,0:T(8,128)(2,1)S(1)}, u32[]{:S(2)}, u32[]{:S(2)}) async-start(bf16[16,40,256]{2,1,0:T(8,128)(2,1)} %broadcast_in_dim.45), calls=%async_computation | async-start | bytes 655360 | tf_op jit(solution)/shard_map/all_to_all | solution.py:35
  10.1 7.0 %all-to-all-done = bf16[16,40,256]{2,1,0:T(8,128)(2,1)S(1)} async-done(((bf16[16,40,256]{2,1,0:T(8,128)(2,1)}), bf16[16,40,256]{2,1,0:T(8,128)(2,1)S(1)}, u32[]{:S(2)}, u32[]{:S(2)}) %all-to-all-start) | async-done | bytes 327712 | tf_op jit(solution)/shard_map/all_to_all | solution.py:35
  17.9 4.9 %collective-permute-start = (bf16[16,24,1024]{2,1,0:T(8,128)(2,1)S(1)}, bf16[16,24,1024]{2,1,0:T(8,128)(2,1)S(1)}, u32[]{:S(2)}, u32[]{:S(2)}) collective-permute-start(bf16[16,24,1024]{2,1,0:T(8,128)(2,1)S(1)} %broadcast_select_fusion), channel_id=1, source_target_pairs={{0,16},{16,0},{1,17},{17,1},{2,18},{18,2},{3,19},{19,3},{4,20},{20... | collective-permute-start | bytes 2359304 | tf_op jit(solution)/shard_map/ppermute | solution.py:39
  25.3 11.1 %collective-permute-start.1 = (bf16[8,24,1024]{2,1,0:T(8,128)(2,1)S(1)}, bf16[8,24,1024]{2,1,0:T(8,128)(2,1)S(1)}, u32[]{:S(2)}, u32[]{:S(2)}) collective-permute-start(bf16[8,24,1024]{2,1,0:T(8,128)(2,1)S(1)} %slice.118), channel_id=1, source_target_pairs={{0,32},{16,496},{32,0},{48,80},{64,96},{80,48},{96,64},{112,144},{... | collective-permute-start | bytes 1179656 | tf_op jit(solution)/shard_map/ppermute | solution.py:48
  36.5 5.2 %collective-permute-done.1 = bf16[8,24,1024]{2,1,0:T(8,128)(2,1)S(1)} collective-permute-done((bf16[8,24,1024]{2,1,0:T(8,128)(2,1)S(1)}, bf16[8,24,1024]{2,1,0:T(8,128)(2,1)S(1)}, u32[]{:S(2)}, u32[]{:S(2)}) %collective-permute-start.1) | collective-permute-done | bytes 393248 | tf_op jit(solution)/shard_map/ppermute | solution.py:48
  41.8 31.9 %all_to_all.45 = bf16[8,24,1024]{2,1,0:T(8,128)(2,1)S(1)} all-to-all(bf16[8,24,1024]{2,1,0:T(8,128)(2,1)S(1)} %add_convert_fusion.3), channel_id=1, replica_groups=mesh['zh'=4,'zm'=2,'zp'=2,'c'=2,'y'=4,'xm'=2,'xp'=2] {'zh','zm'}, dimensions={0} | all-to-all | bytes 786432 | tf_op jit(solution)/shard_map/all_to_all | solution.py:92
  75.1 4.7 %all-to-all-start.2 = ((bf16[16,24,512]{2,1,0:T(8,128)(2,1)}), bf16[16,24,512]{2,1,0:T(8,128)(2,1)S(1)}, u32[]{:S(2)}, u32[]{:S(2)}) async-start(bf16[16,24,512]{2,1,0:T(8,128)(2,1)} %broadcast_in_dim.89), calls=%async_computation.2 | async-start | bytes 786432 | tf_op jit(solution)/shard_map/all_to_all | solution.py:22
  79.8 8.4 %all-to-all-done.2 = bf16[16,24,512]{2,1,0:T(8,128)(2,1)S(1)} async-done(((bf16[16,24,512]{2,1,0:T(8,128)(2,1)}), bf16[16,24,512]{2,1,0:T(8,128)(2,1)S(1)}, u32[]{:S(2)}, u32[]{:S(2)}) %all-to-all-start.2) | async-done | bytes 393248 | tf_op jit(solution)/shard_map/all_to_all | solution.py:22
  90.2 18.5 %all_to_all.46 = bf16[16,16,640]{2,1,0:T(8,128)(2,1)S(1)} all-to-all(bf16[16,16,640]{2,1,0:T(8,128)(2,1)S(1)} %broadcast_in_dim.91), channel_id=1, replica_groups=mesh['zh'=4,'zm'=2,'zp'=2,'c'=2,'y'=4,'xm'=2,'xp'=2] {'zh','zm','zp'}, dimensions={0} | all-to-all | bytes 655360 | tf_op jit(solution)/shard_map/all_to_all | solution.py:22
  109.0 10.2 %collective-permute-start.2 = (bf16[16,20,512]{2,1,0:T(8,128)(2,1)S(1)}, bf16[16,20,512]{2,1,0:T(8,128)(2,1)S(1)}, u32[]{:S(2)}, u32[]{:S(2)}) collective-permute-start(bf16[16,20,512]{2,1,0:T(8,128)(2,1)S(1)} %reshape.135), channel_id=1, source_target_pairs={{0,16},{16,0},{1,17},{17,1},{2,18},{18,2},{3,19},{19,3},{4,20},{20... | collective-permute-start | bytes 983048 | tf_op jit(solution)/shard_map/ppermute | solution.py:39
  121.8 12.0 %all_to_all.47 = bf16[16,40,256]{2,1,0:T(8,128)(2,1)S(1)} all-to-all(bf16[16,40,256]{2,1,0:T(8,128)(2,1)S(1)} %bitcast.54), channel_id=1, replica_groups=mesh['zh'=4,'zm'=2,'zp'=2,'c'=2,'y'=4,'xm'=2,'xp'=2] {'y','xm','xp'}, dimensions={0} | all-to-all | bytes 655360 | tf_op jit(solution)/shard_map/all_to_all | solution.py:182
  134.7 3.7 %all-to-all-start.5 = ((bf16[16,40,256]{2,1,0:T(8,128)(2,1)}), bf16[16,40,256]{2,1,0:T(8,128)(2,1)S(1)}, u32[]{:S(2)}, u32[]{:S(2)}) async-start(bf16[16,40,256]{2,1,0:T(8,128)(2,1)} %broadcast_in_dim.92), calls=%async_computation.5 | async-start | bytes 655360 | tf_op jit(solution)/shard_map/all_to_all | solution.py:35
  138.5 6.9 %all-to-all-done.5 = bf16[16,40,256]{2,1,0:T(8,128)(2,1)S(1)} async-done(((bf16[16,40,256]{2,1,0:T(8,128)(2,1)}), bf16[16,40,256]{2,1,0:T(8,128)(2,1)S(1)}, u32[]{:S(2)}, u32[]{:S(2)}) %all-to-all-start.5) | async-done | bytes 327712 | tf_op jit(solution)/shard_map/all_to_all | solution.py:35
  146.2 4.5 %collective-permute-start.3 = (bf16[16,128,256]{2,1,0:T(8,128)(2,1)S(1)}, bf16[16,128,256]{2,1,0:T(8,128)(2,1)S(1)}, u32[]{:S(2)}, u32[]{:S(2)}) collective-permute-start(bf16[16,128,256]{2,1,0:T(8,128)(2,1)S(1)} %fusion.4), channel_id=1, source_target_pairs={{0,16},{16,0},{1,17},{17,1},{2,18},{18,2},{3,19},{19,3},{4,20},{20... | collective-permute-start | bytes 3145736 | tf_op jit(solution)/shard_map/ppermute | solution.py:39
  151.2 1.8 collective-permute-done.3
  153.3 5.0 %collective-permute-start.4 = (bf16[8,128,256]{2,1,0:T(8,128)(2,1)S(1)}, bf16[8,128,256]{2,1,0:T(8,128)(2,1)S(1)}, u32[]{:S(2)}, u32[]{:S(2)}) collective-permute-start(bf16[8,128,256]{2,1,0:T(8,128)(2,1)S(1)} %slice.135), channel_id=1, source_target_pairs={{0,32},{16,496},{32,0},{48,80},{64,96},{80,48},{96,64},{112,144},{... | collective-permute-start | bytes 1572872 | tf_op jit(solution)/shard_map/ppermute | solution.py:48
  158.3 6.6 %collective-permute-done.4 = bf16[8,128,256]{2,1,0:T(8,128)(2,1)S(1)} collective-permute-done((bf16[8,128,256]{2,1,0:T(8,128)(2,1)S(1)}, bf16[8,128,256]{2,1,0:T(8,128)(2,1)S(1)}, u32[]{:S(2)}, u32[]{:S(2)}) %collective-permute-start.4) | collective-permute-done | bytes 524320 | tf_op jit(solution)/shard_map/ppermute | solution.py:48
  165.0 32.8 %all_to_all.48 = bf16[8,128,256]{2,1,0:T(8,128)(2,1)S(1)} all-to-all(bf16[8,128,256]{2,1,0:T(8,128)(2,1)S(1)} %add_convert_fusion.2), channel_id=1, replica_groups=mesh['zh'=4,'zm'=2,'zp'=2,'c'=2,'y'=4,'xm'=2,'xp'=2] {'zh','zm'}, dimensions={0} | all-to-all | bytes 1048576 | tf_op jit(solution)/shard_map/all_to_all | solution.py:118
  198.1 23.4 %all_to_all.49 = bf16[8,40,384]{2,1,0:T(8,128)(2,1)S(1)} all-to-all(bf16[8,40,384]{2,1,0:T(8,128)(2,1)S(1)} %broadcast_in_dim.93), channel_id=1, replica_groups=mesh['zh'=4,'zm'=2,'zp'=2,'c'=2,'y'=4,'xm'=2,'xp'=2] {'zh','zm'}, dimensions={0} | all-to-all | bytes 491520 | tf_op jit(solution)/shard_map/all_to_all | solution.py:22
  221.4 2.9 %collective-permute-start.6 = (bf16[8,40,384]{2,1,0:T(8,128)(2,1)S(1)}, bf16[8,40,384]{2,1,0:T(8,128)(2,1)S(1)}, u32[]{:S(2)}, u32[]{:S(2)}) collective-permute-start(bf16[8,40,384]{2,1,0:T(8,128)(2,1)S(1)} %all_to_all.49), channel_id=1, source_target_pairs={{0,32},{16,496},{32,0},{48,80},{64,96},{80,48},{96,64},{112,144},{... | collective-permute-start | bytes 737288 | tf_op jit(solution)/shard_map/ppermute | solution.py:48
  224.4 6.7 %collective-permute-start.5 = (bf16[8,40,384]{2,1,0:T(8,128)(2,1)S(1)}, bf16[8,40,384]{2,1,0:T(8,128)(2,1)S(1)}, u32[]{:S(2)}, u32[]{:S(2)}) collective-permute-start(bf16[8,40,384]{2,1,0:T(8,128)(2,1)S(1)} %all_to_all.49), channel_id=1, source_target_pairs={{0,16},{16,0},{1,17},{17,1},{2,18},{18,2},{3,19},{19,3},{4,20},{20... | collective-permute-start | bytes 737288 | tf_op jit(solution)/shard_map/ppermute | solution.py:39
  231.3 5.9 %collective-permute-start.7 = (bf16[8,40,384]{2,1,0:T(8,128)(2,1)S(1)}, bf16[8,40,384]{2,1,0:T(8,128)(2,1)S(1)}, u32[]{:S(2)}, u32[]{:S(2)}) collective-permute-start(bf16[8,40,384]{2,1,0:T(8,128)(2,1)S(1)} %collective-permute-done.6), channel_id=1, source_target_pairs={{0,16},{16,0},{1,17},{17,1},{2,18},{18,2},{3,19},{19,3},{4,20},{20... | collective-permute-start | bytes 737288 | tf_op jit(solution)/shard_map/ppermute | solution.py:39
  239.3 3.5 %all-to-all-start.8 = ((bf16[16,40,256]{2,1,0:T(8,128)(2,1)}), bf16[16,40,256]{2,1,0:T(8,128)(2,1)S(1)}, u32[]{:S(2)}, u32[]{:S(2)}) async-start(bf16[16,40,256]{2,1,0:T(8,128)(2,1)} %bitcast.21), calls=%async_computation.8 | async-start | bytes 655360 | tf_op jit(solution)/shard_map/all_to_all | solution.py:35
  243.5 7.6 %all-to-all-done.8 = bf16[16,40,256]{2,1,0:T(8,128)(2,1)S(1)} async-done(((bf16[16,40,256]{2,1,0:T(8,128)(2,1)}), bf16[16,40,256]{2,1,0:T(8,128)(2,1)S(1)}, u32[]{:S(2)}, u32[]{:S(2)}) %all-to-all-start.8) | async-done | bytes 327712 | tf_op jit(solution)/shard_map/all_to_all | solution.py:35
  (109 shorter events, 17.7 us)
Async XLA Ops:
  0.6 73.3 %copy-start = (bf16[512,544]{0,1:T(8,128)(2,1)S(1)}, bf16[512,544]{0,1:T(8,128)(2,1)}, u32[]{:S(2)}) copy-start(bf16[512,544]{0,1:T(8,128)(2,1)} %param.25) | copy-start | bytes 1671172
  2.2 14.9 %all-to-all-start = ((bf16[16,40,256]{2,1,0:T(8,128)(2,1)}), bf16[16,40,256]{2,1,0:T(8,128)(2,1)S(1)}, u32[]{:S(2)}, u32[]{:S(2)}) async-start(bf16[16,40,256]{2,1,0:T(8,128)(2,1)} %broadcast_in_dim.45), calls=%async_computation | async-start | bytes 655360 | tf_op jit(solution)/shard_map/all_to_all | solution.py:35
  17.9 6.8 %collective-permute-start = (bf16[16,24,1024]{2,1,0:T(8,128)(2,1)S(1)}, bf16[16,24,1024]{2,1,0:T(8,128)(2,1)S(1)}, u32[]{:S(2)}, u32[]{:S(2)}) collective-permute-start(bf16[16,24,1024]{2,1,0:T(8,128)(2,1)S(1)} %broadcast_select_fusion), channel_id=1, source_target_pairs={{0,16},{16,0},{1,17},{17,1},{2,18},{18,2},{3,19},{19,3},{4,20},{20... | collective-permute-start | bytes 2359304 | tf_op jit(solution)/shard_map/ppermute | solution.py:39
  25.3 48.6 %copy-start.6 = (bf16[3,20,512]{2,1,0:T(8,128)(2,1)S(1)}, bf16[3,20,512]{2,1,0:T(8,128)(2,1)}, u32[]{:S(2)}) copy-start(bf16[3,20,512]{2,1,0:T(8,128)(2,1)} %param.22) | copy-start | bytes 184324
  25.3 48.5 %copy-start.13 = (f32[4,512]{1,0:T(4,128)S(1)}, f32[4,512]{1,0:T(4,128)}, u32[]{:S(2)}) copy-start(f32[4,512]{1,0:T(4,128)} %param.23) | copy-start | bytes 24580
  25.3 16.3 %collective-permute-start.1 = (bf16[8,24,1024]{2,1,0:T(8,128)(2,1)S(1)}, bf16[8,24,1024]{2,1,0:T(8,128)(2,1)S(1)}, u32[]{:S(2)}, u32[]{:S(2)}) collective-permute-start(bf16[8,24,1024]{2,1,0:T(8,128)(2,1)S(1)} %slice.118), channel_id=1, source_target_pairs={{0,32},{16,496},{32,0},{48,80},{64,96},{80,48},{96,64},{112,144},{... | collective-permute-start | bytes 1179656 | tf_op jit(solution)/shard_map/ppermute | solution.py:48
  41.7 32.2 %copy-start.12 = (f32[512]{0:T(512)S(1)}, f32[512]{0:T(512)}, u32[]{:S(2)}) copy-start(f32[512]{0:T(512)} %param.24) | copy-start | bytes 6148
  74.2 14.4 %copy-start.3 = (bf16[512,512]{1,0:T(8,128)(2,1)S(1)}, bf16[512,512]{1,0:T(8,128)(2,1)}, u32[]{:S(2)}) copy-start(bf16[512,512]{1,0:T(8,128)(2,1)} %param.26) | copy-start | bytes 1572868
  74.2 14.4 %copy-start.14 = (f32[512]{0:T(512)S(1)}, f32[512]{0:T(512)}, u32[]{:S(2)}) copy-start(f32[512]{0:T(512)} %param.27) | copy-start | bytes 6148
  75.1 13.8 %copy-start.2 = (f32[20,16,512]{2,1,0:T(8,128)S(1)}, f32[20,16,512]{2,1,0:T(8,128)}, u32[]{:S(2)}) copy-start(f32[20,16,512]{2,1,0:T(8,128)} %param.29) | copy-start | bytes 1966084
  75.1 13.1 %all-to-all-start.2 = ((bf16[16,24,512]{2,1,0:T(8,128)(2,1)}), bf16[16,24,512]{2,1,0:T(8,128)(2,1)S(1)}, u32[]{:S(2)}, u32[]{:S(2)}) async-start(bf16[16,24,512]{2,1,0:T(8,128)(2,1)} %broadcast_in_dim.89), calls=%async_computation.2 | async-start | bytes 786432 | tf_op jit(solution)/shard_map/all_to_all | solution.py:22
  109.0 11.5 %collective-permute-start.2 = (bf16[16,20,512]{2,1,0:T(8,128)(2,1)S(1)}, bf16[16,20,512]{2,1,0:T(8,128)(2,1)S(1)}, u32[]{:S(2)}, u32[]{:S(2)}) collective-permute-start(bf16[16,20,512]{2,1,0:T(8,128)(2,1)S(1)} %reshape.135), channel_id=1, source_target_pairs={{0,16},{16,0},{1,17},{17,1},{2,18},{18,2},{3,19},{19,3},{4,20},{20... | collective-permute-start | bytes 983048 | tf_op jit(solution)/shard_map/ppermute | solution.py:39
  121.5 12.4 %copy-start.10 = (bf16[40,256]{1,0:T(8,128)(2,1)S(1)}, bf16[40,256]{1,0:T(8,128)(2,1)}, u32[]{:S(2)}) copy-start(bf16[40,256]{1,0:T(8,128)(2,1)} %param.18) | copy-start | bytes 61444
  121.8 16.5 %copy-start.4 = (bf16[256,768]{1,0:T(8,128)(2,1)S(1)}, bf16[256,768]{1,0:T(8,128)(2,1)}, u32[]{:S(2)}) copy-start(bf16[256,768]{1,0:T(8,128)(2,1)} %param.34) | copy-start | bytes 1179652
  121.8 16.5 %copy-start.5 = (bf16[256,768]{1,0:T(8,128)(2,1)S(1)}, bf16[256,768]{1,0:T(8,128)(2,1)}, u32[]{:S(2)}) copy-start(bf16[256,768]{1,0:T(8,128)(2,1)} %param.33) | copy-start | bytes 1179652
  134.7 10.7 %copy-start.17 = (f32[256]{0:T(256)S(1)}, f32[256]{0:T(256)}, u32[]{:S(2)}) copy-start(f32[256]{0:T(256)} %param.32) | copy-start | bytes 3076
  134.7 10.7 %all-to-all-start.5 = ((bf16[16,40,256]{2,1,0:T(8,128)(2,1)}), bf16[16,40,256]{2,1,0:T(8,128)(2,1)S(1)}, u32[]{:S(2)}, u32[]{:S(2)}) async-start(bf16[16,40,256]{2,1,0:T(8,128)(2,1)} %broadcast_in_dim.92), calls=%async_computation.5 | async-start | bytes 655360 | tf_op jit(solution)/shard_map/all_to_all | solution.py:35
  146.2 6.7 %collective-permute-start.3 = (bf16[16,128,256]{2,1,0:T(8,128)(2,1)S(1)}, bf16[16,128,256]{2,1,0:T(8,128)(2,1)S(1)}, u32[]{:S(2)}, u32[]{:S(2)}) collective-permute-start(bf16[16,128,256]{2,1,0:T(8,128)(2,1)S(1)} %fusion.4), channel_id=1, source_target_pairs={{0,16},{16,0},{1,17},{17,1},{2,18},{18,2},{3,19},{19,3},{4,20},{20... | collective-permute-start | bytes 3145736 | tf_op jit(solution)/shard_map/ppermute | solution.py:39
  153.3 11.6 %collective-permute-start.4 = (bf16[8,128,256]{2,1,0:T(8,128)(2,1)S(1)}, bf16[8,128,256]{2,1,0:T(8,128)(2,1)S(1)}, u32[]{:S(2)}, u32[]{:S(2)}) collective-permute-start(bf16[8,128,256]{2,1,0:T(8,128)(2,1)S(1)} %slice.135), channel_id=1, source_target_pairs={{0,32},{16,496},{32,0},{48,80},{64,96},{80,48},{96,64},{112,144},{... | collective-permute-start | bytes 1572872 | tf_op jit(solution)/shard_map/ppermute | solution.py:48
  197.8 33.3 %copy-start.1 = (bf16[768,256]{1,0:T(8,128)(2,1)S(1)}, bf16[768,256]{1,0:T(8,128)(2,1)}, u32[]{:S(2)}) copy-start(bf16[768,256]{1,0:T(8,128)(2,1)} %param.35) | copy-start | bytes 1179652
  221.4 9.9 %collective-permute-start.6 = (bf16[8,40,384]{2,1,0:T(8,128)(2,1)S(1)}, bf16[8,40,384]{2,1,0:T(8,128)(2,1)S(1)}, u32[]{:S(2)}, u32[]{:S(2)}) collective-permute-start(bf16[8,40,384]{2,1,0:T(8,128)(2,1)S(1)} %all_to_all.49), channel_id=1, source_target_pairs={{0,32},{16,496},{32,0},{48,80},{64,96},{80,48},{96,64},{112,144},{... | collective-permute-start | bytes 737288 | tf_op jit(solution)/shard_map/ppermute | solution.py:48
  224.4 13.1 %collective-permute-start.5 = (bf16[8,40,384]{2,1,0:T(8,128)(2,1)S(1)}, bf16[8,40,384]{2,1,0:T(8,128)(2,1)S(1)}, u32[]{:S(2)}, u32[]{:S(2)}) collective-permute-start(bf16[8,40,384]{2,1,0:T(8,128)(2,1)S(1)} %all_to_all.49), channel_id=1, source_target_pairs={{0,16},{16,0},{1,17},{17,1},{2,18},{18,2},{3,19},{19,3},{4,20},{20... | collective-permute-start | bytes 737288 | tf_op jit(solution)/shard_map/ppermute | solution.py:39
  231.3 7.0 %collective-permute-start.7 = (bf16[8,40,384]{2,1,0:T(8,128)(2,1)S(1)}, bf16[8,40,384]{2,1,0:T(8,128)(2,1)S(1)}, u32[]{:S(2)}, u32[]{:S(2)}) collective-permute-start(bf16[8,40,384]{2,1,0:T(8,128)(2,1)S(1)} %collective-permute-done.6), channel_id=1, source_target_pairs={{0,16},{16,0},{1,17},{17,1},{2,18},{18,2},{3,19},{19,3},{4,20},{20... | collective-permute-start | bytes 737288 | tf_op jit(solution)/shard_map/ppermute | solution.py:39
  239.3 11.8 %all-to-all-start.8 = ((bf16[16,40,256]{2,1,0:T(8,128)(2,1)}), bf16[16,40,256]{2,1,0:T(8,128)(2,1)S(1)}, u32[]{:S(2)}, u32[]{:S(2)}) async-start(bf16[16,40,256]{2,1,0:T(8,128)(2,1)} %bitcast.21), calls=%async_computation.8 | async-start | bytes 655360 | tf_op jit(solution)/shard_map/all_to_all | solution.py:35
  (6 other events, 34.4 us)

commit v10 on v9

--- a/solution.py
+++ b/solution.py
@@ -174,14 +174,14 @@
     same = spread(dense, RING, 16).reshape(16, own_rows, inner_dev)
     same = lax.optimization_barrier(same)
     other = swap(same, "c")
-    rows = jnp.concatenate(
-        [jnp.where(core == 0, same, other), jnp.where(core == 0, other, same)], axis=1
-    )
+    rows = jnp.concatenate([same, other], axis=1)
     out_terms = dot(rows.reshape(16 * token_rows, inner_dev), out_weight).astype(BF16)
-    out_own = jnp.sum(
+    out_sum = jnp.sum(
         lax.all_to_all(out_terms.reshape(16, token_rows, token_cols), TENSOR, 0, 0).astype(F32),
         axis=0,
     )
+    turned = jnp.concatenate([out_sum[own_rows:], out_sum[:own_rows]], axis=0)
+    out_own = jnp.where(core == 0, out_sum, turned)
     residual = (tokens.astype(F32) + out_own).astype(BF16)
 
     sums, second = reduce_wide_rows(residual, post_gain, gate_weight, up_weight)

time: 253 us -> 252 us (level)
  no operation moved by 1% of the time
where the time goes in v10:
time: 252 us; the launch traced here: 251 us
  blocking collectives  119 us (47%)
  starting transfers between devices  70.9 us (28%)
  waiting for transfers between devices  46.8 us (19%)
  other arithmetic  5.82 us (2%)
  local copies, waits for them, and re-layouts  4.2 us (2%)
  matrix products  3.42 us (1%)
    all_to_all x2, blocking collectives, spread(): lax.all_to_all(jnp.broadcast_to(block[None], (count,) + block.shape), axe...  41.9 us
    all_to_all x1, blocking collectives, reduce_wide_rows(): sums = jnp.sum(lax.all_to_all(total, PAIRS, 0, 0).astype(F32), axis=0)  32.7 us
    ppermute x5, starting transfers between devices, swap(): return lax.ppermute(block, axis, [(0, 1), (1, 0)])  32.1 us
    all_to_all x1, blocking collectives, reduce_rows(): sums = jnp.sum(lax.all_to_all(total, PAIRS, 0, 0).astype(F32), axis=0)  31.9 us
    all_to_all x3, waiting for transfers between devices, exchange(): lax.all_to_all(blocks, RING + ('c',) + TENSOR, 0, 0, axis_index_groups=pl...  21.5 us
    ppermute x3, starting transfers between devices, swap_pairs(): return lax.ppermute(block, RING + ('c',), moves)  19.1 us
    all_to_all x3, starting transfers between devices, exchange(): lax.all_to_all(blocks, RING + ('c',) + TENSOR, 0, 0, axis_index_groups=pl...  15 us
    all_to_all x1, blocking collectives, on_device(): lax.all_to_all(out_terms.reshape(16, token_rows, token_cols), TENSOR, 0, 0)  12 us
  transfers between devices with their start and end apart: 12, of which 10 were waited for; matrix products, arithmetic and copies ran while one was open for 1% of the time, Pallas kernels for 0%

profile of v10, /device:TPU:1, one launch (start us, length us, event | category | flops | bytes accessed | tf_op | source)
XLA Modules:
  0.0 251.0 jit_solution(15626090521135534647)
XLA Ops:
  2.2 7.8 %all-to-all-start = ((bf16[16,40,256]{2,1,0:T(8,128)(2,1)}), bf16[16,40,256]{2,1,0:T(8,128)(2,1)S(1)}, u32[]{:S(2)}, u32[]{:S(2)}) async-start(bf16[16,40,256]{2,1,0:T(8,128)(2,1)} %broadcast_in_dim.45), calls=%async_computation | async-start | bytes 655360 | tf_op jit(solution)/shard_map/all_to_all | solution.py:35
  10.1 7.0 %all-to-all-done = bf16[16,40,256]{2,1,0:T(8,128)(2,1)S(1)} async-done(((bf16[16,40,256]{2,1,0:T(8,128)(2,1)}), bf16[16,40,256]{2,1,0:T(8,128)(2,1)S(1)}, u32[]{:S(2)}, u32[]{:S(2)}) %all-to-all-start) | async-done | bytes 327712 | tf_op jit(solution)/shard_map/all_to_all | solution.py:35
  17.9 4.9 %collective-permute-start = (bf16[16,24,1024]{2,1,0:T(8,128)(2,1)S(1)}, bf16[16,24,1024]{2,1,0:T(8,128)(2,1)S(1)}, u32[]{:S(2)}, u32[]{:S(2)}) collective-permute-start(bf16[16,24,1024]{2,1,0:T(8,128)(2,1)S(1)} %broadcast_select_fusion), channel_id=1, source_target_pairs={{0,16},{16,0},{1,17},{17,1},{2,18},{18,2},{3,19},{19,3},{4,20},{20... | collective-permute-start | bytes 2359304 | tf_op jit(solution)/shard_map/ppermute | solution.py:39
  25.3 11.1 %collective-permute-start.1 = (bf16[8,24,1024]{2,1,0:T(8,128)(2,1)S(1)}, bf16[8,24,1024]{2,1,0:T(8,128)(2,1)S(1)}, u32[]{:S(2)}, u32[]{:S(2)}) collective-permute-start(bf16[8,24,1024]{2,1,0:T(8,128)(2,1)S(1)} %slice.126), channel_id=1, source_target_pairs={{0,32},{16,496},{32,0},{48,80},{64,96},{80,48},{96,64},{112,144},{... | collective-permute-start | bytes 1179656 | tf_op jit(solution)/shard_map/ppermute | solution.py:48
  36.5 5.2 %collective-permute-done.1 = bf16[8,24,1024]{2,1,0:T(8,128)(2,1)S(1)} collective-permute-done((bf16[8,24,1024]{2,1,0:T(8,128)(2,1)S(1)}, bf16[8,24,1024]{2,1,0:T(8,128)(2,1)S(1)}, u32[]{:S(2)}, u32[]{:S(2)}) %collective-permute-start.1) | collective-permute-done | bytes 393248 | tf_op jit(solution)/shard_map/ppermute | solution.py:48
  41.8 31.9 %all_to_all.45 = bf16[8,24,1024]{2,1,0:T(8,128)(2,1)S(1)} all-to-all(bf16[8,24,1024]{2,1,0:T(8,128)(2,1)S(1)} %add_convert_fusion.3), channel_id=1, replica_groups=mesh['zh'=4,'zm'=2,'zp'=2,'c'=2,'y'=4,'xm'=2,'xp'=2] {'zh','zm'}, dimensions={0} | all-to-all | bytes 786432 | tf_op jit(solution)/shard_map/all_to_all | solution.py:92
  75.1 4.7 %all-to-all-start.2 = ((bf16[16,24,512]{2,1,0:T(8,128)(2,1)}), bf16[16,24,512]{2,1,0:T(8,128)(2,1)S(1)}, u32[]{:S(2)}, u32[]{:S(2)}) async-start(bf16[16,24,512]{2,1,0:T(8,128)(2,1)} %broadcast_in_dim.89), calls=%async_computation.2 | async-start | bytes 786432 | tf_op jit(solution)/shard_map/all_to_all | solution.py:22
  79.8 8.4 %all-to-all-done.2 = bf16[16,24,512]{2,1,0:T(8,128)(2,1)S(1)} async-done(((bf16[16,24,512]{2,1,0:T(8,128)(2,1)}), bf16[16,24,512]{2,1,0:T(8,128)(2,1)S(1)}, u32[]{:S(2)}, u32[]{:S(2)}) %all-to-all-start.2) | async-done | bytes 393248 | tf_op jit(solution)/shard_map/all_to_all | solution.py:22
  90.2 18.5 %all_to_all.46 = bf16[16,16,640]{2,1,0:T(8,128)(2,1)S(1)} all-to-all(bf16[16,16,640]{2,1,0:T(8,128)(2,1)S(1)} %broadcast_in_dim.91), channel_id=1, replica_groups=mesh['zh'=4,'zm'=2,'zp'=2,'c'=2,'y'=4,'xm'=2,'xp'=2] {'zh','zm','zp'}, dimensions={0} | all-to-all | bytes 655360 | tf_op jit(solution)/shard_map/all_to_all | solution.py:22
  109.0 10.2 %collective-permute-start.2 = (bf16[16,20,512]{2,1,0:T(8,128)(2,1)S(1)}, bf16[16,20,512]{2,1,0:T(8,128)(2,1)S(1)}, u32[]{:S(2)}, u32[]{:S(2)}) collective-permute-start(bf16[16,20,512]{2,1,0:T(8,128)(2,1)S(1)} %reshape.135), channel_id=1, source_target_pairs={{0,16},{16,0},{1,17},{17,1},{2,18},{18,2},{3,19},{19,3},{4,20},{20... | collective-permute-start | bytes 983048 | tf_op jit(solution)/shard_map/ppermute | solution.py:39
  121.0 12.0 %all_to_all.47 = bf16[16,40,256]{2,1,0:T(8,128)(2,1)S(1)} all-to-all(bf16[16,40,256]{2,1,0:T(8,128)(2,1)S(1)} %bitcast.54), channel_id=1, replica_groups=mesh['zh'=4,'zm'=2,'zp'=2,'c'=2,'y'=4,'xm'=2,'xp'=2] {'y','xm','xp'}, dimensions={0} | all-to-all | bytes 655360 | tf_op jit(solution)/shard_map/all_to_all | solution.py:180
  133.8 3.7 %all-to-all-start.5 = ((bf16[16,40,256]{2,1,0:T(8,128)(2,1)}), bf16[16,40,256]{2,1,0:T(8,128)(2,1)S(1)}, u32[]{:S(2)}, u32[]{:S(2)}) async-start(bf16[16,40,256]{2,1,0:T(8,128)(2,1)} %broadcast_in_dim.92), calls=%async_computation.5 | async-start | bytes 655360 | tf_op jit(solution)/shard_map/all_to_all | solution.py:35
  137.6 6.9 %all-to-all-done.5 = bf16[16,40,256]{2,1,0:T(8,128)(2,1)S(1)} async-done(((bf16[16,40,256]{2,1,0:T(8,128)(2,1)}), bf16[16,40,256]{2,1,0:T(8,128)(2,1)S(1)}, u32[]{:S(2)}, u32[]{:S(2)}) %all-to-all-start.5) | async-done | bytes 327712 | tf_op jit(solution)/shard_map/all_to_all | solution.py:35
  145.4 4.5 %collective-permute-start.3 = (bf16[16,128,256]{2,1,0:T(8,128)(2,1)S(1)}, bf16[16,128,256]{2,1,0:T(8,128)(2,1)S(1)}, u32[]{:S(2)}, u32[]{:S(2)}) collective-permute-start(bf16[16,128,256]{2,1,0:T(8,128)(2,1)S(1)} %fusion.4), channel_id=1, source_target_pairs={{0,16},{16,0},{1,17},{17,1},{2,18},{18,2},{3,19},{19,3},{4,20},{20... | collective-permute-start | bytes 3145736 | tf_op jit(solution)/shard_map/ppermute | solution.py:39
  150.3 1.8 collective-permute-done.3
  152.5 5.0 %collective-permute-start.4 = (bf16[8,128,256]{2,1,0:T(8,128)(2,1)S(1)}, bf16[8,128,256]{2,1,0:T(8,128)(2,1)S(1)}, u32[]{:S(2)}, u32[]{:S(2)}) collective-permute-start(bf16[8,128,256]{2,1,0:T(8,128)(2,1)S(1)} %slice.145), channel_id=1, source_target_pairs={{0,32},{16,496},{32,0},{48,80},{64,96},{80,48},{96,64},{112,144},{... | collective-permute-start | bytes 1572872 | tf_op jit(solution)/shard_map/ppermute | solution.py:48
  157.5 6.6 %collective-permute-done.4 = bf16[8,128,256]{2,1,0:T(8,128)(2,1)S(1)} collective-permute-done((bf16[8,128,256]{2,1,0:T(8,128)(2,1)S(1)}, bf16[8,128,256]{2,1,0:T(8,128)(2,1)S(1)}, u32[]{:S(2)}, u32[]{:S(2)}) %collective-permute-start.4) | collective-permute-done | bytes 524320 | tf_op jit(solution)/shard_map/ppermute | solution.py:48
  164.2 32.7 %all_to_all.48 = bf16[8,128,256]{2,1,0:T(8,128)(2,1)S(1)} all-to-all(bf16[8,128,256]{2,1,0:T(8,128)(2,1)S(1)} %add_convert_fusion.2), channel_id=1, replica_groups=mesh['zh'=4,'zm'=2,'zp'=2,'c'=2,'y'=4,'xm'=2,'xp'=2] {'zh','zm'}, dimensions={0} | all-to-all | bytes 1048576 | tf_op jit(solution)/shard_map/all_to_all | solution.py:118
  197.2 23.4 %all_to_all.49 = bf16[8,40,384]{2,1,0:T(8,128)(2,1)S(1)} all-to-all(bf16[8,40,384]{2,1,0:T(8,128)(2,1)S(1)} %broadcast_in_dim.93), channel_id=1, replica_groups=mesh['zh'=4,'zm'=2,'zp'=2,'c'=2,'y'=4,'xm'=2,'xp'=2] {'zh','zm'}, dimensions={0} | all-to-all | bytes 491520 | tf_op jit(solution)/shard_map/all_to_all | solution.py:22
  220.6 2.9 %collective-permute-start.6 = (bf16[8,40,384]{2,1,0:T(8,128)(2,1)S(1)}, bf16[8,40,384]{2,1,0:T(8,128)(2,1)S(1)}, u32[]{:S(2)}, u32[]{:S(2)}) collective-permute-start(bf16[8,40,384]{2,1,0:T(8,128)(2,1)S(1)} %all_to_all.49), channel_id=1, source_target_pairs={{0,32},{16,496},{32,0},{48,80},{64,96},{80,48},{96,64},{112,144},{... | collective-permute-start | bytes 737288 | tf_op jit(solution)/shard_map/ppermute | solution.py:48
  223.5 6.7 %collective-permute-start.5 = (bf16[8,40,384]{2,1,0:T(8,128)(2,1)S(1)}, bf16[8,40,384]{2,1,0:T(8,128)(2,1)S(1)}, u32[]{:S(2)}, u32[]{:S(2)}) collective-permute-start(bf16[8,40,384]{2,1,0:T(8,128)(2,1)S(1)} %all_to_all.49), channel_id=1, source_target_pairs={{0,16},{16,0},{1,17},{17,1},{2,18},{18,2},{3,19},{19,3},{4,20},{20... | collective-permute-start | bytes 737288 | tf_op jit(solution)/shard_map/ppermute | solution.py:39
  230.5 5.9 %collective-permute-start.7 = (bf16[8,40,384]{2,1,0:T(8,128)(2,1)S(1)}, bf16[8,40,384]{2,1,0:T(8,128)(2,1)S(1)}, u32[]{:S(2)}, u32[]{:S(2)}) collective-permute-start(bf16[8,40,384]{2,1,0:T(8,128)(2,1)S(1)} %collective-permute-done.6), channel_id=1, source_target_pairs={{0,16},{16,0},{1,17},{17,1},{2,18},{18,2},{3,19},{19,3},{4,20},{20... | collective-permute-start | bytes 737288 | tf_op jit(solution)/shard_map/ppermute | solution.py:39
  238.5 3.5 %all-to-all-start.8 = ((bf16[16,40,256]{2,1,0:T(8,128)(2,1)}), bf16[16,40,256]{2,1,0:T(8,128)(2,1)S(1)}, u32[]{:S(2)}, u32[]{:S(2)}) async-start(bf16[16,40,256]{2,1,0:T(8,128)(2,1)} %bitcast.21), calls=%async_computation.8 | async-start | bytes 655360 | tf_op jit(solution)/shard_map/all_to_all | solution.py:35
  242.7 7.6 %all-to-all-done.8 = bf16[16,40,256]{2,1,0:T(8,128)(2,1)S(1)} async-done(((bf16[16,40,256]{2,1,0:T(8,128)(2,1)}), bf16[16,40,256]{2,1,0:T(8,128)(2,1)S(1)}, u32[]{:S(2)}, u32[]{:S(2)}) %all-to-all-start.8) | async-done | bytes 327712 | tf_op jit(solution)/shard_map/all_to_all | solution.py:35
  (109 shorter events, 16.9 us)
Async XLA Ops:
  0.6 73.3 %copy-start = (bf16[512,544]{0,1:T(8,128)(2,1)S(1)}, bf16[512,544]{0,1:T(8,128)(2,1)}, u32[]{:S(2)}) copy-start(bf16[512,544]{0,1:T(8,128)(2,1)} %param.25) | copy-start | bytes 1671172
  2.2 14.9 %all-to-all-start = ((bf16[16,40,256]{2,1,0:T(8,128)(2,1)}), bf16[16,40,256]{2,1,0:T(8,128)(2,1)S(1)}, u32[]{:S(2)}, u32[]{:S(2)}) async-start(bf16[16,40,256]{2,1,0:T(8,128)(2,1)} %broadcast_in_dim.45), calls=%async_computation | async-start | bytes 655360 | tf_op jit(solution)/shard_map/all_to_all | solution.py:35
  17.9 6.8 %collective-permute-start = (bf16[16,24,1024]{2,1,0:T(8,128)(2,1)S(1)}, bf16[16,24,1024]{2,1,0:T(8,128)(2,1)S(1)}, u32[]{:S(2)}, u32[]{:S(2)}) collective-permute-start(bf16[16,24,1024]{2,1,0:T(8,128)(2,1)S(1)} %broadcast_select_fusion), channel_id=1, source_target_pairs={{0,16},{16,0},{1,17},{17,1},{2,18},{18,2},{3,19},{19,3},{4,20},{20... | collective-permute-start | bytes 2359304 | tf_op jit(solution)/shard_map/ppermute | solution.py:39
  25.3 48.6 %copy-start.6 = (bf16[3,20,512]{2,1,0:T(8,128)(2,1)S(1)}, bf16[3,20,512]{2,1,0:T(8,128)(2,1)}, u32[]{:S(2)}) copy-start(bf16[3,20,512]{2,1,0:T(8,128)(2,1)} %param.22) | copy-start | bytes 184324
  25.3 48.5 %copy-start.13 = (f32[4,512]{1,0:T(4,128)S(1)}, f32[4,512]{1,0:T(4,128)}, u32[]{:S(2)}) copy-start(f32[4,512]{1,0:T(4,128)} %param.23) | copy-start | bytes 24580
  25.3 16.3 %collective-permute-start.1 = (bf16[8,24,1024]{2,1,0:T(8,128)(2,1)S(1)}, bf16[8,24,1024]{2,1,0:T(8,128)(2,1)S(1)}, u32[]{:S(2)}, u32[]{:S(2)}) collective-permute-start(bf16[8,24,1024]{2,1,0:T(8,128)(2,1)S(1)} %slice.126), channel_id=1, source_target_pairs={{0,32},{16,496},{32,0},{48,80},{64,96},{80,48},{96,64},{112,144},{... | collective-permute-start | bytes 1179656 | tf_op jit(solution)/shard_map/ppermute | solution.py:48
  41.7 32.2 %copy-start.12 = (f32[512]{0:T(512)S(1)}, f32[512]{0:T(512)}, u32[]{:S(2)}) copy-start(f32[512]{0:T(512)} %param.24) | copy-start | bytes 6148
  74.2 14.4 %copy-start.3 = (bf16[512,512]{1,0:T(8,128)(2,1)S(1)}, bf16[512,512]{1,0:T(8,128)(2,1)}, u32[]{:S(2)}) copy-start(bf16[512,512]{1,0:T(8,128)(2,1)} %param.26) | copy-start | bytes 1572868
  74.2 14.4 %copy-start.14 = (f32[512]{0:T(512)S(1)}, f32[512]{0:T(512)}, u32[]{:S(2)}) copy-start(f32[512]{0:T(512)} %param.27) | copy-start | bytes 6148
  75.1 13.8 %copy-start.2 = (f32[20,16,512]{2,1,0:T(8,128)S(1)}, f32[20,16,512]{2,1,0:T(8,128)}, u32[]{:S(2)}) copy-start(f32[20,16,512]{2,1,0:T(8,128)} %param.29) | copy-start | bytes 1966084
  75.1 13.1 %all-to-all-start.2 = ((bf16[16,24,512]{2,1,0:T(8,128)(2,1)}), bf16[16,24,512]{2,1,0:T(8,128)(2,1)S(1)}, u32[]{:S(2)}, u32[]{:S(2)}) async-start(bf16[16,24,512]{2,1,0:T(8,128)(2,1)} %broadcast_in_dim.89), calls=%async_computation.2 | async-start | bytes 786432 | tf_op jit(solution)/shard_map/all_to_all | solution.py:22
  108.7 11.9 %copy-start.7 = (bf16[512,256]{1,0:T(8,128)(2,1)S(1)}, bf16[512,256]{1,0:T(8,128)(2,1)}, u32[]{:S(2)}) copy-start(bf16[512,256]{1,0:T(8,128)(2,1)} %param.31) | copy-start | bytes 786436
  109.0 11.5 %collective-permute-start.2 = (bf16[16,20,512]{2,1,0:T(8,128)(2,1)S(1)}, bf16[16,20,512]{2,1,0:T(8,128)(2,1)S(1)}, u32[]{:S(2)}, u32[]{:S(2)}) collective-permute-start(bf16[16,20,512]{2,1,0:T(8,128)(2,1)S(1)} %reshape.135), channel_id=1, source_target_pairs={{0,16},{16,0},{1,17},{17,1},{2,18},{18,2},{3,19},{19,3},{4,20},{20... | collective-permute-start | bytes 983048 | tf_op jit(solution)/shard_map/ppermute | solution.py:39
  120.6 12.4 %copy-start.10 = (bf16[40,256]{1,0:T(8,128)(2,1)S(1)}, bf16[40,256]{1,0:T(8,128)(2,1)}, u32[]{:S(2)}) copy-start(bf16[40,256]{1,0:T(8,128)(2,1)} %param.18) | copy-start | bytes 61444
  121.0 16.5 %copy-start.4 = (bf16[256,768]{1,0:T(8,128)(2,1)S(1)}, bf16[256,768]{1,0:T(8,128)(2,1)}, u32[]{:S(2)}) copy-start(bf16[256,768]{1,0:T(8,128)(2,1)} %param.34) | copy-start | bytes 1179652
  121.0 16.5 %copy-start.5 = (bf16[256,768]{1,0:T(8,128)(2,1)S(1)}, bf16[256,768]{1,0:T(8,128)(2,1)}, u32[]{:S(2)}) copy-start(bf16[256,768]{1,0:T(8,128)(2,1)} %param.33) | copy-start | bytes 1179652
  133.8 10.7 %all-to-all-start.5 = ((bf16[16,40,256]{2,1,0:T(8,128)(2,1)}), bf16[16,40,256]{2,1,0:T(8,128)(2,1)S(1)}, u32[]{:S(2)}, u32[]{:S(2)}) async-start(bf16[16,40,256]{2,1,0:T(8,128)(2,1)} %broadcast_in_dim.92), calls=%async_computation.5 | async-start | bytes 655360 | tf_op jit(solution)/shard_map/all_to_all | solution.py:35
  145.4 6.7 %collective-permute-start.3 = (bf16[16,128,256]{2,1,0:T(8,128)(2,1)S(1)}, bf16[16,128,256]{2,1,0:T(8,128)(2,1)S(1)}, u32[]{:S(2)}, u32[]{:S(2)}) collective-permute-start(bf16[16,128,256]{2,1,0:T(8,128)(2,1)S(1)} %fusion.4), channel_id=1, source_target_pairs={{0,16},{16,0},{1,17},{17,1},{2,18},{18,2},{3,19},{19,3},{4,20},{20... | collective-permute-start | bytes 3145736 | tf_op jit(solution)/shard_map/ppermute | solution.py:39
  152.5 11.6 %collective-permute-start.4 = (bf16[8,128,256]{2,1,0:T(8,128)(2,1)S(1)}, bf16[8,128,256]{2,1,0:T(8,128)(2,1)S(1)}, u32[]{:S(2)}, u32[]{:S(2)}) collective-permute-start(bf16[8,128,256]{2,1,0:T(8,128)(2,1)S(1)} %slice.145), channel_id=1, source_target_pairs={{0,32},{16,496},{32,0},{48,80},{64,96},{80,48},{96,64},{112,144},{... | collective-permute-start | bytes 1572872 | tf_op jit(solution)/shard_map/ppermute | solution.py:48
  197.0 33.3 %copy-start.1 = (bf16[768,256]{1,0:T(8,128)(2,1)S(1)}, bf16[768,256]{1,0:T(8,128)(2,1)}, u32[]{:S(2)}) copy-start(bf16[768,256]{1,0:T(8,128)(2,1)} %param.35) | copy-start | bytes 1179652
  220.6 9.9 %collective-permute-start.6 = (bf16[8,40,384]{2,1,0:T(8,128)(2,1)S(1)}, bf16[8,40,384]{2,1,0:T(8,128)(2,1)S(1)}, u32[]{:S(2)}, u32[]{:S(2)}) collective-permute-start(bf16[8,40,384]{2,1,0:T(8,128)(2,1)S(1)} %all_to_all.49), channel_id=1, source_target_pairs={{0,32},{16,496},{32,0},{48,80},{64,96},{80,48},{96,64},{112,144},{... | collective-permute-start | bytes 737288 | tf_op jit(solution)/shard_map/ppermute | solution.py:48
  223.5 13.1 %collective-permute-start.5 = (bf16[8,40,384]{2,1,0:T(8,128)(2,1)S(1)}, bf16[8,40,384]{2,1,0:T(8,128)(2,1)S(1)}, u32[]{:S(2)}, u32[]{:S(2)}) collective-permute-start(bf16[8,40,384]{2,1,0:T(8,128)(2,1)S(1)} %all_to_all.49), channel_id=1, source_target_pairs={{0,16},{16,0},{1,17},{17,1},{2,18},{18,2},{3,19},{19,3},{4,20},{20... | collective-permute-start | bytes 737288 | tf_op jit(solution)/shard_map/ppermute | solution.py:39
  230.5 7.0 %collective-permute-start.7 = (bf16[8,40,384]{2,1,0:T(8,128)(2,1)S(1)}, bf16[8,40,384]{2,1,0:T(8,128)(2,1)S(1)}, u32[]{:S(2)}, u32[]{:S(2)}) collective-permute-start(bf16[8,40,384]{2,1,0:T(8,128)(2,1)S(1)} %collective-permute-done.6), channel_id=1, source_target_pairs={{0,16},{16,0},{1,17},{17,1},{2,18},{18,2},{3,19},{19,3},{4,20},{20... | collective-permute-start | bytes 737288 | tf_op jit(solution)/shard_map/ppermute | solution.py:39
  238.5 11.8 %all-to-all-start.8 = ((bf16[16,40,256]{2,1,0:T(8,128)(2,1)}), bf16[16,40,256]{2,1,0:T(8,128)(2,1)S(1)}, u32[]{:S(2)}, u32[]{:S(2)}) async-start(bf16[16,40,256]{2,1,0:T(8,128)(2,1)} %bitcast.21), calls=%async_computation.8 | async-start | bytes 655360 | tf_op jit(solution)/shard_map/all_to_all | solution.py:35
  (6 other events, 44.2 us)
